TPU v7x, 32 devices: a whole 2x2x4 slice. The times are simulated.
32 devices in a mesh: dp: 8 (over y, x, core), seq: 4 (over z).
Axes of the slice: x: 2, y: 2, z: 4, core: 2. Of those that a mesh axis runs over, the one named last changes fastest.
Arguments:
- hidden_in: bfloat16 [8192, 1536], P(('dp', 'seq')), may hold values from -6 to 6
- segment_ids: int32 [8192], P(('dp', 'seq')), may hold values from 0 to 4, as said below
- position_ids: int32 [8192], P(('dp', 'seq')), may hold values from 0 to 767, as said below
- out_grad: bfloat16 [8192, 1536], P(('dp', 'seq')), may hold values from -6 to 6
- attn_norm: bfloat16 [1536], P('dp'), may hold values from 0.5 to 1.5
- w_query: bfloat16 [1536, 1536], P('dp'), may hold values from -0.15625 to 0.15625
- w_key: bfloat16 [1536, 256], P('dp'), may hold values from -0.15625 to 0.15625
- w_value: bfloat16 [1536, 256], P('dp'), may hold values from -0.15625 to 0.15625
- b_query: bfloat16 [1536], P('dp'), may hold values from -3 to 3
- b_key: bfloat16 [256], P('dp'), may hold values from -3 to 3
- b_value: bfloat16 [256], P('dp'), may hold values from -3 to 3
- w_out: bfloat16 [1536, 1536], P(None, 'dp'), may hold values from -1.25 to 1.25
- mlp_norm: bfloat16 [1536], P('dp'), may hold values from 0.5 to 1.5
- w_gate: bfloat16 [1536, 8960], P('dp', 'seq'), may hold values from -0.15625 to 0.15625
- w_up: bfloat16 [1536, 8960], P('dp', 'seq'), may hold values from -0.15625 to 0.15625
- w_down: bfloat16 [1536, 8960], P('dp', 'seq'), may hold values from -0.25 to 0.25
Outputs:
- block_out: bfloat16 [8192, 1536], P(('dp', 'seq'))
- input_grad: float32 [8192, 1536], P(('dp', 'seq'))
- attn_norm_grad: float32 [1536], P('dp')
- w_query_grad: float32 [1536, 1536], P('dp')
- w_key_grad: float32 [1536, 256], P('dp')
- w_value_grad: float32 [1536, 256], P('dp')
- b_query_grad: float32 [1536], P('dp')
- b_key_grad: float32 [256], P('dp')
- b_value_grad: float32 [256], P('dp')
- w_out_grad: float32 [1536, 1536], P(None, 'dp')
- mlp_norm_grad: float32 [1536], P('dp')
- w_gate_grad: float32 [1536, 8960], P('dp', 'seq')
- w_up_grad: float32 [1536, 8960], P('dp', 'seq')
- w_down_grad: float32 [1536, 8960], P('dp', 'seq')
Inputs may be any that keep to these rules, and one draw needn't show every extreme that they name: `segment_ids`: within each row of 1024 tokens the ids start at 0 and never fall; one segment runs from a token among the row's first 256 to one among its last 256. `position_ids`: A position is 0 at the first token of its segment; from each token to the next inside the segment it rises by 1 or 2 until it reaches the maximum, and stays there. Every row reaches the maximum.
All inputs are finite; a program needn't handle non-finite values.
Results may differ from a plain program's by a relative error of at most 0.025.
Values may be sent and summed in bfloat16 or wider, within the bound.
A program may use at most 256 MiB of HBM per device.

v0:
```python
import jax
import jax.numpy as jnp
from jax import lax
from jax.sharding import PartitionSpec as P

HEADS = 12
KV_HEADS = 2
HD = 128


EPS = 1e-06
ROPE_BASE = 1000000.0
NEG_FILL = -1e30


def rope_tables(positions, head_dim):
    half_dim = head_dim // 2
    inv_freq = ROPE_BASE ** (-(jnp.arange(half_dim).astype(jnp.float32) * 2.0 / head_dim))
    angles = positions.astype(jnp.float32)[:, None] * inv_freq[None, :]
    cosine_tab = jnp.cos(angles)
    sine_tab = jnp.sin(angles)
    return (
        jnp.concatenate([cosine_tab, cosine_tab], axis=-1),
        jnp.concatenate([sine_tab, sine_tab], axis=-1),
    )


def rotate(values, cosine_tab, sine_tab):
    half_dim = values.shape[-1] // 2
    turned = jnp.concatenate([-values[..., half_dim:], values[..., :half_dim]], axis=-1)
    return values * cosine_tab[:, None, :] + turned * sine_tab[:, None, :]


def rotate_back(grads, cosine_tab, sine_tab):
    half_dim = grads.shape[-1] // 2
    scaled = grads * sine_tab[:, None, :]
    return grads * cosine_tab[:, None, :] + jnp.concatenate(
        [scaled[..., half_dim:], -scaled[..., :half_dim]], axis=-1
    )


def norm_factor(values):
    return lax.rsqrt(jnp.mean(values * values, axis=-1, keepdims=True) + EPS)


def norm_back(grad_in, values, factor, gain):
    scaled = grad_in * gain
    return factor * scaled - values * factor**3 * jnp.mean(scaled * values, axis=-1, keepdims=True)


def contract_rows(left, right):
    return lax.dot_general(
        left, right, (((0,), (0,)), ((), ())), preferred_element_type=jnp.float32
    )


def contract_cols(left, right):
    return lax.dot_general(
        left, right, (((1,), (1,)), ((), ())), preferred_element_type=jnp.float32
    )


def masked_scores(query_block, keys_all, seg_block, seg_all, start, scale):
    scores = (
        jnp.einsum("qhd,kd->hqk", query_block, keys_all, preferred_element_type=jnp.float32) * scale
    )
    query_index = start + jnp.arange(query_block.shape[0], dtype=jnp.int32)
    key_index = jnp.arange(keys_all.shape[0], dtype=jnp.int32)
    keep_mask = (seg_block[:, None] == seg_all[None, :]) & (
        query_index[:, None] >= key_index[None, :]
    )
    return jnp.where(keep_mask[None], scores, NEG_FILL)


def body(
    hidden_in,
    segment_ids,
    position_ids,
    out_grad,
    attn_norm,
    w_query,
    w_key,
    w_value,
    b_query,
    b_key,
    b_value,
    w_out,
    mlp_norm,
    w_gate,
    w_up,
    w_down,
):
    lane_count = lax.axis_size("seq")
    local_tok = hidden_in.shape[0]
    row_len = local_tok * lane_count
    heads_lane = HEADS // lane_count
    kv_group = lane_count // KV_HEADS
    query_width = heads_lane * HD
    scale = HD ** (-0.5)
    gathered = (
        lax.all_gather(w_query, "dp", axis=0, tiled=True),
        lax.all_gather(w_key, "dp", axis=0, tiled=True),
        lax.all_gather(w_value, "dp", axis=0, tiled=True),
        lax.all_gather(w_out, "dp", axis=1, tiled=True),
        lax.all_gather(b_query, "dp", axis=0, tiled=True),
        lax.all_gather(b_key, "dp", axis=0, tiled=True),
        lax.all_gather(b_value, "dp", axis=0, tiled=True),
        lax.all_gather(attn_norm, "dp", axis=0, tiled=True),
        lax.all_gather(mlp_norm, "dp", axis=0, tiled=True),
    )
    (
        query_full,
        key_full,
        value_full,
        out_full,
        query_bias,
        key_bias,
        value_bias,
        attn_gain,
        mlp_gain,
    ) = gathered
    attn_gain = attn_gain.astype(jnp.float32)
    mlp_gain = mlp_gain.astype(jnp.float32)
    input_f32 = hidden_in.astype(jnp.float32)
    factor_one = norm_factor(input_f32)
    normed = (input_f32 * factor_one * attn_gain).astype(jnp.bfloat16)
    query_pre = jnp.dot(normed, query_full, preferred_element_type=jnp.float32) + query_bias.astype(
        jnp.float32
    )
    key_pre = jnp.dot(normed, key_full, preferred_element_type=jnp.float32) + key_bias.astype(
        jnp.float32
    )
    value_pre = jnp.dot(normed, value_full, preferred_element_type=jnp.float32) + value_bias.astype(
        jnp.float32
    )
    cosine_tab, sine_tab = rope_tables(position_ids, HD)
    query_rot = rotate(query_pre.reshape(local_tok, HEADS, HD), cosine_tab, sine_tab).astype(
        jnp.bfloat16
    )
    key_rot = rotate(key_pre.reshape(local_tok, KV_HEADS, HD), cosine_tab, sine_tab).astype(
        jnp.bfloat16
    )
    value_low = value_pre.reshape(local_tok, KV_HEADS, HD).astype(jnp.bfloat16)
    key_lanes = jnp.repeat(key_rot, kv_group, axis=1)
    value_lanes = jnp.repeat(value_low, kv_group, axis=1)
    outgoing = jnp.concatenate(
        [query_rot.reshape(local_tok, lane_count, query_width), key_lanes, value_lanes], axis=-1
    )
    seg_copies = jnp.broadcast_to(
        segment_ids.astype(jnp.bfloat16)[:, None], (local_tok, lane_count)
    )
    incoming, seg_incoming = (
        lax.all_to_all(outgoing, "seq", split_axis=1, concat_axis=0, tiled=True),
        lax.all_to_all(seg_copies, "seq", split_axis=1, concat_axis=0, tiled=True),
    )
    head_query = incoming[:, 0, :query_width].reshape(row_len, heads_lane, HD)
    head_key = incoming[:, 0, query_width : query_width + HD]
    head_value = incoming[:, 0, query_width + HD :]
    seg_all = seg_incoming[:, 0]
    block_rows = min(512, row_len)
    block_count = row_len // block_rows
    starts = jnp.arange(block_count, dtype=jnp.int32) * block_rows
    query_blocks = head_query.reshape(block_count, block_rows, heads_lane, HD)
    seg_blocks = seg_all.reshape(block_count, block_rows)

    def forward_block(items):
        query_block, seg_block, start = items
        scores = masked_scores(query_block, head_key, seg_block, seg_all, start, scale)
        peak = jnp.max(scores, axis=-1, keepdims=True)
        exp_scores = jnp.exp(scores - peak)
        totals = jnp.sum(exp_scores, axis=-1, keepdims=True)
        attn_prob = (exp_scores / totals).astype(jnp.bfloat16)
        out_block = jnp.einsum(
            "hqk,kd->qhd", attn_prob, head_value, preferred_element_type=jnp.float32
        ).astype(jnp.bfloat16)
        return (out_block, (peak + jnp.log(totals))[..., 0])

    out_blocks, log_sums = lax.map(forward_block, (query_blocks, seg_blocks, starts))
    attended_heads = out_blocks.reshape(row_len, 1, query_width)
    attended = lax.all_to_all(
        attended_heads, "seq", split_axis=0, concat_axis=1, tiled=True
    ).reshape(local_tok, HEADS * HD)
    resid = input_f32 + jnp.dot(attended, out_full, preferred_element_type=jnp.float32)
    factor_two = norm_factor(resid)
    mlp_local = (resid * factor_two * mlp_gain).astype(jnp.bfloat16)
    mlp_in = lax.all_gather(mlp_local, "seq", axis=0, tiled=True)
    gate_full, up_full, down_full = (
        lax.all_gather(w_gate, "dp", axis=0, tiled=True),
        lax.all_gather(w_up, "dp", axis=0, tiled=True),
        lax.all_gather(w_down, "dp", axis=0, tiled=True),
    )
    gate_act = jnp.dot(mlp_in, gate_full, preferred_element_type=jnp.float32)
    up_act = jnp.dot(mlp_in, up_full, preferred_element_type=jnp.float32)
    gate_sig = jax.nn.sigmoid(gate_act)
    silu_act = gate_act * gate_sig
    hidden = (silu_act * up_act).astype(jnp.bfloat16)
    mlp_part = contract_cols(hidden, down_full)
    mlp_out = lax.psum_scatter(mlp_part, "seq", scatter_dimension=0, tiled=True)
    block_out = (resid + mlp_out).astype(jnp.bfloat16)
    grad_rows = lax.all_gather(out_grad, "seq", axis=0, tiled=True)
    gate_back, up_back, down_back = (
        lax.all_gather(w_gate, "dp", axis=0, tiled=True),
        lax.all_gather(w_up, "dp", axis=0, tiled=True),
        lax.all_gather(w_down, "dp", axis=0, tiled=True),
    )
    grad_hidden = jnp.dot(grad_rows, down_back, preferred_element_type=jnp.float32)
    grad_gate = (grad_hidden * up_act * gate_sig * (1.0 + gate_act * (1.0 - gate_sig))).astype(
        jnp.bfloat16
    )
    grad_up = (grad_hidden * silu_act).astype(jnp.bfloat16)
    mlp_in_part = contract_cols(grad_gate, gate_back) + contract_cols(grad_up, up_back)
    grad_mlp_in = lax.psum_scatter(mlp_in_part, "seq", scatter_dimension=0, tiled=True)
    mlp_grads = lax.psum_scatter(
        jnp.concatenate(
            [
                contract_rows(mlp_in, grad_gate),
                contract_rows(mlp_in, grad_up),
                contract_rows(grad_rows, hidden),
            ],
            axis=1,
        ),
        "dp",
        scatter_dimension=0,
        tiled=True,
    )
    hidden_width = hidden.shape[1]
    gate_grad = mlp_grads[:, :hidden_width]
    up_grad = mlp_grads[:, hidden_width : 2 * hidden_width]
    down_grad = mlp_grads[:, 2 * hidden_width :]
    mlp_gain_part = jnp.sum(grad_mlp_in * resid * factor_two, axis=0)
    grad_resid = out_grad.astype(jnp.float32) + norm_back(grad_mlp_in, resid, factor_two, mlp_gain)
    grad_resid_low = grad_resid.astype(jnp.bfloat16)
    out_grad_part = contract_rows(attended, grad_resid_low)
    grad_attended = contract_cols(grad_resid_low, out_full).astype(jnp.bfloat16)
    grad_heads = lax.all_to_all(
        grad_attended.reshape(local_tok, lane_count, query_width),
        "seq",
        split_axis=1,
        concat_axis=0,
        tiled=True,
    )
    grad_blocks = grad_heads.reshape(block_count, block_rows, heads_lane, HD)

    def backward_block(carry, items):
        key_acc, value_acc = carry
        query_block, grad_block, seg_block, start, log_block = items
        scores = masked_scores(query_block, head_key, seg_block, seg_all, start, scale)
        attn_prob = jnp.exp(scores - log_block[..., None])
        prob_low = attn_prob.astype(jnp.bfloat16)
        grad_prob = jnp.einsum(
            "qhd,kd->hqk", grad_block, head_value, preferred_element_type=jnp.float32
        )
        inner = jnp.sum(attn_prob * grad_prob, axis=-1, keepdims=True)
        grad_scores = (attn_prob * (grad_prob - inner)).astype(jnp.bfloat16)
        grad_query = (
            jnp.einsum("hqk,kd->qhd", grad_scores, head_key, preferred_element_type=jnp.float32)
            * scale
        ).astype(jnp.bfloat16)
        key_acc = (
            key_acc
            + jnp.einsum(
                "hqk,qhd->kd", grad_scores, query_block, preferred_element_type=jnp.float32
            )
            * scale
        )
        value_acc = value_acc + jnp.einsum(
            "hqk,qhd->kd", prob_low, grad_block, preferred_element_type=jnp.float32
        )
        return ((key_acc, value_acc), grad_query)

    zero_lane = jnp.zeros((row_len, HD), jnp.float32)
    (key_acc, value_acc), grad_query_blocks = lax.scan(
        backward_block,
        (zero_lane, zero_lane),
        (query_blocks, grad_blocks, seg_blocks, starts, log_sums),
    )
    returning = jnp.concatenate(
        [
            grad_query_blocks.reshape(row_len, query_width),
            key_acc.astype(jnp.bfloat16),
            value_acc.astype(jnp.bfloat16),
        ],
        axis=-1,
    )
    arriving = lax.all_to_all(
        returning.reshape(row_len, 1, query_width + 2 * HD),
        "seq",
        split_axis=0,
        concat_axis=1,
        tiled=True,
    )
    grad_query_rot = arriving[:, :, :query_width].reshape(local_tok, HEADS, HD).astype(jnp.float32)
    grad_key_sum = (
        arriving[:, :, query_width : query_width + HD]
        .astype(jnp.float32)
        .reshape(local_tok, KV_HEADS, kv_group, HD)
        .sum(axis=2)
    )
    grad_value_sum = (
        arriving[:, :, query_width + HD :]
        .astype(jnp.float32)
        .reshape(local_tok, KV_HEADS, kv_group, HD)
        .sum(axis=2)
    )
    grad_query_pre = (
        rotate_back(grad_query_rot, cosine_tab, sine_tab)
        .reshape(local_tok, HEADS * HD)
        .astype(jnp.bfloat16)
    )
    grad_key_pre = (
        rotate_back(grad_key_sum, cosine_tab, sine_tab)
        .reshape(local_tok, KV_HEADS * HD)
        .astype(jnp.bfloat16)
    )
    grad_value_pre = grad_value_sum.reshape(local_tok, KV_HEADS * HD).astype(jnp.bfloat16)
    grad_normed = (
        contract_cols(grad_query_pre, query_full)
        + contract_cols(grad_key_pre, key_full)
        + contract_cols(grad_value_pre, value_full)
    )
    attn_gain_part = jnp.sum(grad_normed * input_f32 * factor_one, axis=0)
    input_grad = grad_resid + norm_back(grad_normed, input_f32, factor_one, attn_gain)
    query_grad = contract_rows(normed, grad_query_pre)
    key_grad = contract_rows(normed, grad_key_pre)
    value_grad = contract_rows(normed, grad_value_pre)
    query_bias_grad = jnp.sum(grad_query_pre.astype(jnp.float32), axis=0)
    key_bias_grad = jnp.sum(grad_key_pre.astype(jnp.float32), axis=0)
    value_bias_grad = jnp.sum(grad_value_pre.astype(jnp.float32), axis=0)
    local_terms = (
        query_grad,
        key_grad,
        value_grad,
        out_grad_part,
        query_bias_grad,
        key_bias_grad,
        value_bias_grad,
        attn_gain_part,
        mlp_gain_part,
    )
    partials = lax.psum(
        (
            local_terms[0],
            local_terms[1],
            local_terms[2],
            local_terms[3],
            local_terms[4],
            local_terms[5],
            local_terms[6],
            local_terms[7],
            local_terms[8],
        ),
        "seq",
    )
    return (
        block_out,
        input_grad,
        lax.psum_scatter(partials[7], "dp", scatter_dimension=0, tiled=True),
        lax.psum_scatter(partials[0], "dp", scatter_dimension=0, tiled=True),
        lax.psum_scatter(partials[1], "dp", scatter_dimension=0, tiled=True),
        lax.psum_scatter(partials[2], "dp", scatter_dimension=0, tiled=True),
        lax.psum_scatter(partials[4], "dp", scatter_dimension=0, tiled=True),
        lax.psum_scatter(partials[5], "dp", scatter_dimension=0, tiled=True),
        lax.psum_scatter(partials[6], "dp", scatter_dimension=0, tiled=True),
        lax.psum_scatter(partials[3], "dp", scatter_dimension=1, tiled=True),
        lax.psum_scatter(partials[8], "dp", scatter_dimension=0, tiled=True),
        gate_grad,
        up_grad,
        down_grad,
    )


def solution(mesh):
    return jax.shard_map(
        body,
        mesh=mesh,
        in_specs=(
            P(("dp", "seq"), None),
            P(("dp", "seq")),
            P(("dp", "seq")),
            P(("dp", "seq"), None),
            P("dp"),
            P("dp", None),
            P("dp", None),
            P("dp", None),
            P("dp"),
            P("dp"),
            P("dp"),
            P(None, "dp"),
            P("dp"),
            P("dp", "seq"),
            P("dp", "seq"),
            P("dp", "seq"),
        ),
        out_specs=(
            P(("dp", "seq"), None),
            P(("dp", "seq"), None),
            P("dp"),
            P("dp", None),
            P("dp", None),
            P("dp", None),
            P("dp"),
            P("dp"),
            P("dp"),
            P(None, "dp"),
            P("dp"),
            P("dp", "seq"),
            P("dp", "seq"),
            P("dp", "seq"),
        ),
        check_vma=False,
    )
```

profile of v0, /device:TPU:0, one launch (start us, length us, event | category | flops | bytes accessed | tf_op | source)
XLA Modules:
  0.0 1422.4 jit_solution(18184777021741992296)
XLA Ops:
  11.2 6.3 all-to-all-start
  23.7 24.2 %all-reduce.13 = (bf16[256]{0:T(256)(128)(2,1)S(1)}, bf16[1536]{0:T(1024)(128)(2,1)S(1)}, bf16[256]{0:T(256)(128)(2,1)S(1)}, bf16[1536]{0:T(1024)(128)(2,1)S(1)}, bf16[1536]{0:T(1024)(128)(2,1)S(1)}) all-reduce(bf16[256]{0:T(256)(128)(2,1)S(1)} %dynamic-update-slice.3, ...), channel_id=1, replica_groups=mesh['dp'=8,'seq'=4] {'dp'}, use_global_device_ids=true, to_apply=%add.3 | all-reduce | flops 5120 | bytes 20480
  47.9 9.6 all_gather.48
  58.4 13.4 all_gather.50
  74.0 4.9 convolution_add_fusion.3
  83.7 5.0 all-to-all-start.1
  88.8 31.8 %all-to-all-done.1 = bf16[256,4,640]{0,2,1:T(8,128)(2,1)S(1)} async-done(((bf16[256,4,640]{0,2,1:T(8,128)(2,1)}), bf16[256,4,640]{0,2,1:T(8,128)(2,1)S(1)}, u32[]{:S(2)}, u32[]{:S(2)}) %all-to-all-start.1) | async-done | bytes 1310752 | tf_op jit(solution)/shard_map/all_to_all | solution.py:153
  124.9 15.2 %while.27 = (s32[]{:T(128)}, bf16[2,512,3,128]{3,1,2,0:T(8,128)(2,1)S(1)}, f32[2,3,512]{2,1,0:T(4,128)S(1)}, bf16[2,512]{1,0:T(2,128)(2,1)S(1)}, bf16[1024,1]{0,...) while((s32[]{:T(128)}, ...), condition=%wide.region_4.5_spmd, body=%wide.region_1.4_spmd.sunk | while | flops 826997760 | bytes 22355096 | solution.py:178
  142.9 3.2 reshape.358
  146.1 6.4 reduce.15
  153.5 4.2 all-to-all-start.2
  158.2 19.5 %all-to-all-done.2 = bf16[4,2,49152]{2,1,0:T(2,128)(2,1)} async-done(((bf16[4,2,49152]{2,1,0:T(2,128)(2,1)}), bf16[4,2,49152]{2,1,0:T(2,128)(2,1)}, u32[]{:S(2)}, u32[]{:S(2)}) %all-to-all-start.2) | async-done | bytes 786464 | tf_op jit(solution)/shard_map/all_to_all | solution.py:180
  183.4 4.1 multiply_reduce_fusion.2
  190.8 60.0 %all-gather.12.cloned.1.call-done = bf16[1024,1536]{1,0:T(8,128)(2,1)} async-done(((bf16[256,1536]{1,0:T(8,128)(2,1)}), bf16[1024,1536]{1,0:T(8,128)(2,1)}) %all-gather.12.cloned.1.call-update) | async-done | bytes 3145744 | tf_op jit(solution)/shard_map/all_gather | solution.py:186
  250.8 13.2 fusion.91
  264.0 36.1 %all-gather.14.cloned.1.call-done = bf16[1536,2240]{1,0:T(8,128)(2,1)} async-done(((bf16[192,2240]{1,0:T(8,128)(2,1)}), bf16[1536,2240]{1,0:T(8,128)(2,1)}) %all-gather.14.cloned.1.call-update) | async-done | bytes 6881296 | tf_op jit(solution)/shard_map/all_gather | solution.py:188
  300.1 13.2 fusion.90
  313.3 51.7 %all-gather.20.cloned.1.call-done = bf16[1024,1536]{1,0:T(8,128)(2,1)} async-done(((bf16[256,1536]{1,0:T(8,128)(2,1)}), bf16[1024,1536]{1,0:T(8,128)(2,1)}) %all-gather.20.cloned.1.call-update) | async-done | bytes 3145744 | tf_op jit(solution)/shard_map/all_gather | solution.py:200
  365.0 49.4 %all-gather.18.cloned.1.call-done = bf16[1536,2240]{1,0:T(8,128)(2,1)} async-done(((bf16[192,2240]{1,0:T(8,128)(2,1)}), bf16[1536,2240]{1,0:T(8,128)(2,1)}) %all-gather.18.cloned.1.call-update) | async-done | bytes 6881296 | tf_op jit(solution)/shard_map/all_gather | solution.py:190
  414.4 20.2 %multiply_convert_fusion = (bf16[1024,2240]{0,1:T(8,128)(2,1)}, bf16[1024,2240]{0,1:T(8,128)(2,1)}, bf16[1024,2240]{0,1:T(8,128)(2,1)}) fusion(f32[1024,2240]{0,1:T(8,128)} %fusion.90, f32[1024,2240]{0,1:T(8,128)} %fusion.91, bf16[1024,1536]{1,0:T(8,128)(2,1)} %all-gather.20.cloned.1.call-done, bf16[1536,2240]{1,0:T(8,128)(2,1)} %all-gather.18.cloned.1.call-done), kind=kOutput, calls=%fused_computation.68 | convolution fusion | flops 7080837120 | bytes 42139648 | tf_op jit(solution)/shard_map/dot_general | solution.py:206
  434.6 11.4 fusion.93
  446.0 12.2 convolution_add_fusion
  458.3 12.9 fusion.92
  471.2 97.9 %reduce-scatter.12.cloned.1.call-done = f32[256,1536]{1,0:T(8,128)} async-done(((f32[1024,1536]{1,0:T(8,128)}), f32[256,1536]{1,0:T(8,128)}) %reduce-scatter.12.cloned.1.call-update) | async-done | bytes 1572880 | tf_op jit(solution)/shard_map/reduce_scatter | solution.py:212
  571.5 111.2 %reduce-scatter.10.cloned.1.call-done = f32[256,1536]{1,0:T(8,128)} async-done(((f32[1024,1536]{1,0:T(8,128)}), f32[256,1536]{1,0:T(8,128)}) %reduce-scatter.10.cloned.1.call-update) | async-done | bytes 1572880 | tf_op jit(solution)/shard_map/reduce_scatter | solution.py:198
  682.8 3.7 subtract_add_fusion
  686.5 4.3 convolution_convert_fusion
  691.9 4.2 all-to-all-start.3
  696.2 20.7 %all-to-all-done.3 = bf16[256,4,384]{0,2,1:T(8,128)(2,1)} async-done(((bf16[256,4,384]{0,2,1:T(8,128)(2,1)}), bf16[256,4,384]{0,2,1:T(8,128)(2,1)}, u32[]{:S(2)}, u32[]{:S(2)}) %all-to-all-start.3) | async-done | bytes 786464 | tf_op jit(solution)/shard_map/all_to_all | solution.py:235
  719.6 3.1 reshape.316
  726.8 26.4 %while.28 = (s32[]{:T(128)}, f32[1024,128]{1,0:T(8,128)S(1)}, f32[1024,128]{1,0:T(8,128)}, bf16[2,512,3,128]{3,1,2,0:T(8,128)(2,1)}, bf16[2,512]{1,0:T(2,128)(2,...) while((s32[]{:T(128)}, f32[1024,128]{1,0:T(8,128)S(1)}, ...), condition=%wide.region_11.12_spmd.clone, body=%wide.region_9.11_spmd.clone.sunk | while | flops 2040527872 | bytes 67824976 | solution.py:272
  764.9 34.8 %all_to_all.82 = bf16[4,2,81920]{2,1,0:T(2,128)(2,1)S(1)} all-to-all(bf16[4,2,81920]{2,1,0:T(2,128)(2,1)} %reshape.376), channel_id=1, replica_groups=mesh['dp'=8,'seq'=4] {'seq'}, dimensions={0} | all-to-all | bytes 2621440 | tf_op jit(solution)/shard_map/all_to_all | solution.py:285
  814.2 5.0 fusion.70
  821.4 5.2 fusion.80
  826.9 13.3 fusion.96
  840.3 12.4 fusion.95
  852.7 9.9 convolution_bitcast_fusion.1
  862.6 28.6 %pad_maximum_fusion = f32[1536,6720]{0,1:T(8,128)} fusion(f32[1536,2240]{0,1:T(8,128)} %convolution_bitcast_fusion.1, f32[1536,2240]{0,1:T(8,128)} %fusion.96, f32[1536,2240]{0,1:T(8,128)} %fusion.95), kind=kLoop, calls=%fused_computation.66 | loop fusion | flops 20643840 | bytes 82575360 | tf_op jit(solution)/shard_map/concatenate | solution.py:214
  891.3 42.4 %copy.130 = f32[1536,6720]{1,0:T(8,128)} copy(f32[1536,6720]{0,1:T(8,128)} %pad_maximum_fusion) | data formatting | bytes 82575360
  937.3 33.0 %reduce-scatter.20.cloned.1.call-done = f32[1536,192]{0,1:T(8,128)} async-done(((f32[1536,1536]{0,1:T(8,128)}), f32[1536,192]{0,1:T(8,128)}) %reduce-scatter.20.cloned.1.call-update) | async-done | bytes 1179664 | tf_op jit(solution)/shard_map/reduce_scatter | solution.py:364
  970.3 80.0 %reduce-scatter.14.cloned.1.call-done = f32[192,1536]{1,0:T(8,128)} async-done(((f32[1536,1536]{1,0:T(8,128)}), f32[192,1536]{1,0:T(8,128)}) %reduce-scatter.14.cloned.1.call-update) | async-done | bytes 1179664 | tf_op jit(solution)/shard_map/reduce_scatter | solution.py:358
  1050.4 3.8 fusion.94
  1057.3 23.1 %all-reduce.10 = (f32[1536]{0:T(1024)S(1)}, f32[1536]{0:T(1024)S(1)}, f32[256]{0:T(256)S(1)}, f32[256]{0:T(256)S(1)}, f32[1536]{0:T(1024)S(1)}) all-reduce(f32[1536]{0:T(1024)S(1)} %get-tuple-element.326, f32[1536]{0:T(1024)S(1)} %reduce_sum.131, f32[256]{0:T(256)S(1)} %bitcast.319, ...), channel_id=4, replica_groups=mesh['dp'=8,'seq'=4] {'dp'}, use_global_device_ids=true, to_apply=%region_17.18.clone | all-reduce | flops 5120 | bytes 40960
  1080.7 12.2 all-reduce.11
  1093.0 3.3 fusion.64
  1096.3 201.3 %reduce-scatter.22.cloned.1.call-done = f32[192,6720]{1,0:T(8,128)} async-done(((f32[1536,6720]{1,0:T(8,128)}), f32[192,6720]{1,0:T(8,128)}) %reduce-scatter.22.cloned.1.call-update) | async-done | bytes 5160976
  1297.6 5.5 fusion.86
  1303.1 106.6 %all-reduce.16.cloned.1.call-done = (f32[192,1536]{1,0:T(8,128)}, f32[192,256]{1,0:T(8,128)}, f32[192,256]{1,0:T(8,128)}, f32[1536,192]{0,1:T(8,128)}) async-done(((f32[192,1536]{1,0:T(8,128)}, f32[192,256]{1,0:T(8,128)}, f32[192,256]{1,0:T(8,128)}, f32[1536,192]{0,1:T(8,128)}), (f32[192,1536]{1,0:T(8,128)}, f32[192,256]{1,0:T(8,128)}, f32[192,256]{1,0:T(8,128)}, ...) | async-done | bytes 2752528 | tf_op jit(solution)/shard_map/psum | solution.py:340
  (288 shorter events, 125.6 us)
Async XLA Ops:
  7.2 14.4 %copy-start = (bf16[256,1536]{1,0:T(8,128)(2,1)S(1)}, bf16[256,1536]{1,0:T(8,128)(2,1)}, u32[]{:S(2)}) copy-start(bf16[256,1536]{1,0:T(8,128)(2,1)} %param.20) | copy-start | bytes 2359300
  7.2 15.2 %copy-start.40 = (bf16[32]{0:T(256)(128)(2,1)S(1)}, bf16[32]{0:T(256)(128)(2,1)}, u32[]{:S(2)}) copy-start(bf16[32]{0:T(256)(128)(2,1)} %param.30) | copy-start | bytes 196
  7.2 15.5 %copy-start.41 = (bf16[32]{0:T(256)(128)(2,1)S(1)}, bf16[32]{0:T(256)(128)(2,1)}, u32[]{:S(2)}) copy-start(bf16[32]{0:T(256)(128)(2,1)} %param.29) | copy-start | bytes 196
  7.2 15.7 %copy-start.42 = (bf16[192]{0:T(256)(128)(2,1)S(1)}, bf16[192]{0:T(256)(128)(2,1)}, u32[]{:S(2)}) copy-start(bf16[192]{0:T(256)(128)(2,1)} %param.28) | copy-start | bytes 1156
  7.2 16.0 %copy-start.43 = (bf16[192]{0:T(256)(128)(2,1)S(1)}, bf16[192]{0:T(256)(128)(2,1)}, u32[]{:S(2)}) copy-start(bf16[192]{0:T(256)(128)(2,1)} %param.24) | copy-start | bytes 1156
  7.2 16.2 %copy-start.44 = (bf16[192]{0:T(256)(128)(2,1)S(1)}, bf16[192]{0:T(256)(128)(2,1)}, u32[]{:S(2)}) copy-start(bf16[192]{0:T(256)(128)(2,1)} %param.32) | copy-start | bytes 1156
  7.2 40.7 %copy-start.32 = (bf16[192,256]{1,0:T(8,128)(2,1)S(1)}, bf16[192,256]{1,0:T(8,128)(2,1)}, u32[]{:S(2)}) copy-start(bf16[192,256]{1,0:T(8,128)(2,1)} %param.26) | copy-start | bytes 294916
  7.3 66.7 %all-gather.8.cloned.1.call-start = ((), (), s32[]{:S(2)}) async-start(), calls=%async_computation.12 | async-start | bytes 5308416 | tf_op jit(solution)/shard_map/all_gather | solution.py:101
  8.0 175.4 %all-gather.10.cloned.1.call-start = ((), (), s32[]{:S(2)}) async-start(), calls=%async_computation.13 | async-start | bytes 5308416 | tf_op jit(solution)/shard_map/all_gather | solution.py:104
  11.2 72.5 %all-to-all-start = ((bf16[4,2,128]{2,1,0:T(2,128)(2,1)}), bf16[4,2,128]{2,1,0:T(2,128)(2,1)S(1)}, u32[]{:S(2)}, u32[]{:S(2)}) async-start(bf16[4,2,128]{2,1,0:T(2,128)(2,1)} %reshape.372), calls=%async_computation | async-start | bytes 4096 | tf_op jit(solution)/shard_map/all_to_all | solution.py:154
  17.5 40.9 %copy-start.33 = (bf16[192,256]{1,0:T(8,128)(2,1)S(1)}, bf16[192,256]{1,0:T(8,128)(2,1)}, u32[]{:S(2)}) copy-start(bf16[192,256]{1,0:T(8,128)(2,1)} %param.27) | copy-start | bytes 294916
  17.5 173.3 %all-gather.16.cloned.1.call-start = ((), (), s32[]{:S(2)}) async-start(), calls=%async_computation.16 | async-start | bytes 7962624 | tf_op jit(solution)/shard_map/all_gather | solution.py:189
  22.4 51.6 %copy-start.34 = (f32[256]{0:T(256)}, f32[256]{0:T(256)S(1)}, u32[]{:S(2)}) copy-start(f32[256]{0:T(256)S(1)} %get-tuple-element.416) | copy-start | bytes 3076
  47.9 26.1 %copy-start.28 = (f32[1536]{0:T(1024)}, f32[1536]{0:T(1024)S(1)}, u32[]{:S(2)}) copy-start(f32[1536]{0:T(1024)S(1)} %convert_element_type.152) | copy-start | bytes 18436
  57.5 14.4 %copy-start.18 = (bf16[1536,256]{1,0:T(8,128)(2,1)}, bf16[1536,256]{1,0:T(8,128)(2,1)S(1)}, u32[]{:S(2)}) copy-start(bf16[1536,256]{1,0:T(8,128)(2,1)S(1)} %all_gather.48) | copy-start | bytes 2359300
  71.9 9.2 copy-start.11
  71.9 9.3 copy-start.13
  83.7 36.9 %all-to-all-start.1 = ((bf16[256,4,640]{0,2,1:T(8,128)(2,1)}), bf16[256,4,640]{0,2,1:T(8,128)(2,1)S(1)}, u32[]{:S(2)}, u32[]{:S(2)}) async-start(bf16[256,4,640]{0,2,1:T(8,128)(2,1)} %pad_maximum_fusion.2), calls=%async_computation.1 | async-start | bytes 2621440 | tf_op jit(solution)/shard_map/all_to_all | solution.py:153
  141.0 11.5 copy-start.7
  153.5 24.1 %all-to-all-start.2 = ((bf16[4,2,49152]{2,1,0:T(2,128)(2,1)}), bf16[4,2,49152]{2,1,0:T(2,128)(2,1)}, u32[]{:S(2)}, u32[]{:S(2)}) async-start(bf16[4,2,49152]{2,1,0:T(2,128)(2,1)} %reshape.374), calls=%async_computation.2 | async-start | bytes 1572864 | tf_op jit(solution)/shard_map/all_to_all | solution.py:180
  157.7 93.0 %all-gather.12.cloned.1.call-start = ((), (), s32[]{:S(2)}) async-start(), calls=%async_computation.14 | async-start | bytes 3932160 | tf_op jit(solution)/shard_map/all_gather | solution.py:186
  187.5 381.6 %copy-start.5 = (f32[256,1536]{1,0:T(8,128)}, f32[256,1536]{1,0:T(8,128)S(1)}, u32[]{:S(2)}) copy-start(f32[256,1536]{1,0:T(8,128)S(1)} %get-tuple-element.422) | copy-start | bytes 4718596
  188.8 111.3 %all-gather.14.cloned.1.call-start = ((), (), s32[]{:S(2)}) async-start(), calls=%async_computation.15 | async-start | bytes 7962624 | tf_op jit(solution)/shard_map/all_gather | solution.py:188
  189.4 175.6 %all-gather.20.cloned.1.call-start = ((), (), s32[]{:S(2)}) async-start(), calls=%async_computation.19 | async-start | bytes 3932160 | tf_op jit(solution)/shard_map/all_gather | solution.py:200
  190.0 224.5 %all-gather.18.cloned.1.call-start = ((), (), s32[]{:S(2)}) async-start(), calls=%async_computation.17 | async-start | bytes 7962624 | tf_op jit(solution)/shard_map/all_gather | solution.py:190
  190.7 378.4 %reduce-scatter.12.cloned.1.call-start = ((), (), s32[]{:S(2)}) async-start(), calls=%async_computation.20 | async-start | bytes 7864320 | tf_op jit(solution)/shard_map/reduce_scatter | solution.py:212
  434.6 11.4 copy-start.45
  458.2 224.5 %reduce-scatter.10.cloned.1.call-start = ((), (), s32[]{:S(2)}) async-start(), calls=%async_computation.18 | async-start | bytes 7864320 | tf_op jit(solution)/shard_map/reduce_scatter | solution.py:198
  471.2 211.6 %copy-start.22 = (bf16[256,1536]{1,0:T(8,128)(2,1)S(1)}, bf16[256,1536]{1,0:T(8,128)(2,1)}, u32[]{:S(2)}) copy-start(bf16[256,1536]{1,0:T(8,128)(2,1)} %param.23) | copy-start | bytes 2359300
  686.5 127.7 %copy-start.3 = (f32[256,1536]{1,0:T(8,128)}, f32[256,1536]{1,0:T(8,128)S(1)}, u32[]{:S(2)}) copy-start(f32[256,1536]{1,0:T(8,128)S(1)} %get-tuple-element.403) | copy-start | bytes 4718596
  691.9 25.0 %all-to-all-start.3 = ((bf16[256,4,384]{0,2,1:T(8,128)(2,1)}), bf16[256,4,384]{0,2,1:T(8,128)(2,1)}, u32[]{:S(2)}, u32[]{:S(2)}) async-start(bf16[256,4,384]{0,2,1:T(8,128)(2,1)} %bitcast.28), calls=%async_computation.5 | async-start | bytes 1572864 | tf_op jit(solution)/shard_map/all_to_all | solution.py:235
  696.2 241.1 %reduce-scatter.18.cloned.1.call-start = ((), (), s32[]{:S(2)}) async-start(), calls=%async_computation.23 | async-start | bytes 1769472 | tf_op jit(solution)/shard_map/reduce_scatter | solution.py:360
  717.0 9.8 copy-start.8
  802.2 6.5 copy-start.1
  802.2 6.5 copy-start.29
  802.2 6.5 copy-start.35
  810.5 126.8 %reduce-scatter.16.cloned.1.call-start = ((), (), s32[]{:S(2)}) async-start(), calls=%async_computation.22 | async-start | bytes 1769472 | tf_op jit(solution)/shard_map/reduce_scatter | solution.py:359
  814.1 156.2 %reduce-scatter.20.cloned.1.call-start = ((), (), s32[]{:S(2)}) async-start(), calls=%async_computation.24 | async-start | bytes 10616832 | tf_op jit(solution)/shard_map/reduce_scatter | solution.py:364
  819.2 231.1 %reduce-scatter.14.cloned.1.call-start = ((), (), s32[]{:S(2)}) async-start(), calls=%async_computation.21 | async-start | bytes 10616832 | tf_op jit(solution)/shard_map/reduce_scatter | solution.py:358
  826.7 470.9 %reduce-scatter.22.cloned.1.call-start = ((), (), s32[]{:S(2)}) async-start(), calls=%async_computation.25 | async-start | bytes 46891008
  826.9 13.4 copy-start.38
  826.9 25.8 %slice-start = ((s8[4587520]{0:T(1024)(128)(4,1)}), s8[4194304]{0:T(1024)(128)(4,1)S(1)}, s32[]{:S(2)}) async-start(s8[4587520]{0:T(1024)(128)(4,1)} %bitcast.321), calls=%async_computation.27 | async-start | bytes 8388608
  840.3 12.4 copy-start.39
  840.3 12.5 slice-start.1
  933.7 476.0 %all-reduce.16.cloned.1.call-start = ((), (), s32[]{:S(2)}) async-start(), calls=%async_computation.26 | async-start | bytes 5505024 | tf_op jit(solution)/shard_map/psum | solution.py:340
  1055.4 37.6 %copy-start.4 = (f32[256,1536]{1,0:T(8,128)S(1)}, f32[256,1536]{1,0:T(8,128)}, u32[]{:S(2)}) copy-start(f32[256,1536]{1,0:T(8,128)} %copy-done.3) | copy-start | bytes 4718596
  1055.4 37.6 %copy-start.37 = (f32[256]{0:T(256)S(1)}, f32[256]{0:T(256)}, u32[]{:S(2)}) copy-start(f32[256]{0:T(256)} %get-tuple-element.415) | copy-start | bytes 3076
  1409.7 4.8 copy-start.25
  (24 other events, 44.6 us)
Sparse Core Ops, SparseCore 0:
  10.0 41.8 all-gather.7
  53.7 41.4 all-gather.9
  97.1 48.8 all-gather.15
  188.9 61.8 all-gather.11
  252.5 47.4 all-gather.13
  301.5 63.4 all-gather.19
  366.9 47.4 all-gather.17
  458.4 110.7 reduce-scatter.11
  571.4 111.2 reduce-scatter.9
  810.6 37.4 reduce-scatter.17
  852.0 38.4 reduce-scatter.15
  893.9 76.4 reduce-scatter.19
  973.8 76.4 reduce-scatter.13
  1053.8 243.7 reduce-scatter.21
  1300.3 109.3 all-reduce.15
where the time goes:
time: 1430 us; the launch traced here: 1420 us
  waiting for transfers between devices  903 us (63%)
  matrix products  177 us (12%)
  blocking collectives  117 us (8%)
  local copies, waits for them, and re-layouts  113 us (8%)
  other arithmetic  72.3 us (5%)
  starting transfers between devices  20.9 us (1%)
  between operations  17.7 us (1%)
    unnamed x16, waiting for transfers between devices  205 us
    reduce_scatter x1, waiting for transfers between devices, body(): mlp_out = lax.psum_scatter(mlp_part, 'seq', scatter_dimension=0, tiled=True)  111 us
    psum x1, waiting for transfers between devices, body(): lax.psum((local_terms[0], local_terms[1], local_terms[2], local_terms[3],...  107 us
    reduce_scatter x1, waiting for transfers between devices, body(): lax.psum_scatter(mlp_in_part, 'seq', scatter_dimension=0, tiled=True)  97.9 us
    reduce_scatter x1, waiting for transfers between devices, body(): lax.psum_scatter(partials[0], 'dp', scatter_dimension=0, tiled=True)  80 us
    unnamed x120, local copies, waits for them, and re-layouts  74.9 us
    all_gather x1, waiting for transfers between devices, body(): mlp_in = lax.all_gather(mlp_local, 'seq', axis=0, tiled=True)  60 us
    all_gather x1, waiting for transfers between devices, body(): grad_rows = lax.all_gather(out_grad, 'seq', axis=0, tiled=True)  51.7 us
  transfers between devices with their start and end apart: 19, of which 13 were waited for; matrix products, arithmetic and copies ran while one was open for 17% of the time, Pallas kernels for 0%

commit v1 on v0

--- a/solution.py
+++ b/solution.py
@@ -1,6 +1,8 @@
 import jax
 import jax.numpy as jnp
 from jax import lax
+from jax.experimental import pallas as pl
+from jax.experimental.pallas import tpu as pltpu
 from jax.sharding import PartitionSpec as P
 
 HEADS = 12
@@ -70,6 +72,350 @@
         query_index[:, None] >= key_index[None, :]
     )
     return jnp.where(keep_mask[None], scores, NEG_FILL)
+
+
+MESH_ID = pl.DeviceIdType.MESH
+LANES = 4
+BF16 = jnp.bfloat16
+F32 = jnp.float32
+
+
+def nn(left, right):
+    return jnp.dot(left, right, preferred_element_type=F32)
+
+
+def nt(left, right):
+    return lax.dot_general(left, right, (((1,), (1,)), ((), ())), preferred_element_type=F32)
+
+
+def rows_of(index, size):
+    return pl.ds(pl.multiple_of(index * size, size), size)
+
+
+def digit(codes, lane):
+    return lax.rem(lax.shift_right_logical(jnp.int32(codes), 2 * lane), 4)
+
+
+def order_of(step, lane):
+    tables = ((0, 1, 2, 3), (1, 0, 2, 3), (2, 3, 1, 0), (3, 2, 1, 0))
+    codes = [sum(tables[k][i] * 4**k for k in range(LANES)) for i in range(LANES)]
+    out = digit(codes[0], lane)
+    for i in range(1, LANES):
+        out = jnp.where(step == i, digit(codes[i], lane), out)
+    return out
+
+
+def ff_kernel(
+    x_hbm, og_hbm, wg_hbm, wu_hbm, wd_hbm,
+    mo_ref, gm_ref, gw_hbm,
+    xb, og, wg, wu, wd, hid, gg, gu, pb, rb, rf,
+    load_sem, ag_send, ag_recv, rb_send, rb_recv, rf_send, rf_recv, out_sem,
+):
+    lane = lax.axis_index("seq")
+    tok, width = x_hbm.shape
+    units = wg_hbm.shape[1]
+    tile = 512
+    full_tiles = units // tile
+    tail = units - full_tiles * tile
+    wtile = 384
+    has_left, has_right = lane > 0, lane < LANES - 1
+    is_end = jnp.logical_or(lane == 0, lane == LANES - 1)
+    is_mid = jnp.logical_not(is_end)
+    left, right = jnp.maximum(lane - 1, 0), jnp.minimum(lane + 1, LANES - 1)
+
+    loads = [
+        pltpu.make_async_copy(src, dst, load_sem.at[k])
+        for k, (src, dst) in enumerate(
+            ((wg_hbm, wg), (wu_hbm, wu), (wd_hbm, wd), (og_hbm, og))
+        )
+    ]
+    own = pltpu.make_async_copy(x_hbm, xb.at[rows_of(lane, tok)], load_sem.at[4])
+    own.start()
+    for copy in loads:
+        copy.start()
+
+    barrier = pltpu.get_barrier_semaphore()
+
+    @pl.when(has_left)
+    def _():
+        pl.semaphore_signal(barrier, 1, device_id={"seq": left}, device_id_type=MESH_ID)
+
+    @pl.when(has_right)
+    def _():
+        pl.semaphore_signal(barrier, 1, device_id={"seq": right}, device_id_type=MESH_ID)
+
+    @pl.when(is_end)
+    def _():
+        pl.semaphore_wait(barrier, 1)
+
+    @pl.when(is_mid)
+    def _():
+        pl.semaphore_wait(barrier, 2)
+
+    own.wait()
+
+    def gather_copy(block, way):
+        part = xb.at[rows_of(block, tok)]
+        return pltpu.make_async_remote_copy(
+            part, part, ag_send.at[way, block], ag_recv.at[block],
+            device_id={"seq": right if way == 0 else left}, device_id_type=MESH_ID,
+        )
+
+    @pl.when(has_right)
+    def _():
+        gather_copy(lane, 0).start()
+
+    @pl.when(has_left)
+    def _():
+        gather_copy(lane, 1).start()
+
+    def arrivals(step):
+        @pl.when(lane - step >= 0)
+        def _():
+            block = jnp.maximum(lane - step, 0)
+            gather_copy(block, 0).wait_recv()
+
+            @pl.when(has_right)
+            def _():
+                gather_copy(block, 0).start()
+
+        @pl.when(lane + step < LANES)
+        def _():
+            block = jnp.minimum(lane + step, LANES - 1)
+            gather_copy(block, 1).wait_recv()
+
+            @pl.when(has_left)
+            def _():
+                gather_copy(block, 1).start()
+
+    def sum_send(part, landing, send, recv, block):
+        goes_left = block < lane
+        target = jnp.where(goes_left, left, right)
+        slot = jnp.where(jnp.logical_and(goes_left, target == block), LANES, block)
+        return pltpu.make_async_remote_copy(
+            part.at[rows_of(block, tok), pl.ds(0, width)], landing.at[rows_of(slot, tok)],
+            send.at[block], recv.at[slot],
+            device_id={"seq": target}, device_id_type=MESH_ID,
+        )
+
+    def sum_arrived(part, landing, send, recv, slot):
+        pltpu.make_async_remote_copy(
+            landing.at[rows_of(slot, tok)], landing.at[rows_of(slot, tok)],
+            send.at[0], recv.at[slot], device_id={"seq": left}, device_id_type=MESH_ID,
+        ).wait_recv()
+
+    def sum_pass(part, landing, send, recv, block):
+        @pl.when(is_mid)
+        def _():
+            sum_arrived(part, landing, send, recv, block)
+
+            def add(i, carry):
+                mine = pl.ds(pl.multiple_of(block * tok + i * 32, 32), 32)
+                total = part[mine, :width].astype(F32) + landing[mine, :].astype(F32)
+                part[mine, :width] = total.astype(BF16)
+                return carry
+
+            lax.fori_loop(0, tok // 32, add, 0)
+            sum_send(part, landing, send, recv, block).start()
+
+    def sum_last(part, landing, send, recv, out):
+        def begin(i, carry):
+            here = pl.ds(pl.multiple_of(i * 32, 32), 32)
+            mine = pl.ds(pl.multiple_of(lane * tok + i * 32, 32), 32)
+            out[here, :] = part[mine, :width].astype(F32)
+            return carry
+
+        lax.fori_loop(0, tok // 32, begin, 0)
+
+        def take(slot):
+            sum_arrived(part, landing, send, recv, slot)
+
+            def add(i, carry):
+                here = pl.ds(pl.multiple_of(i * 32, 32), 32)
+                there = pl.ds(pl.multiple_of(slot * tok + i * 32, 32), 32)
+                out[here, :] = out[here, :] + landing[there, :].astype(F32)
+                return carry
+
+            lax.fori_loop(0, tok // 32, add, 0)
+
+        @pl.when(has_left)
+        def _():
+            take(lane)
+
+        @pl.when(has_right)
+        def _():
+            take(jnp.int32(LANES))
+
+    back = (pb, rb, rb_send, rb_recv)
+    ahead = (wg, rf, rf_send, rf_recv)
+    for copy in loads:
+        copy.wait()
+
+    def block_step(step, carry):
+        block = order_of(step, lane)
+        mine = rows_of(block, tok)
+
+        def act(cols):
+            gate = nn(xb[mine, :], wg[:, cols])
+            up = nn(xb[mine, :], wu[:, cols])
+            grad = nn(og[mine, :], wd[:, cols])
+            sig = jax.nn.sigmoid(gate)
+            silu = gate * sig
+            hid[mine, cols] = (silu * up).astype(BF16)
+            gg[mine, cols] = (grad * up * sig * (1.0 + gate * (1.0 - sig))).astype(BF16)
+            gu[mine, cols] = (grad * silu).astype(BF16)
+
+        def act_tile(t, c):
+            act(pl.ds(pl.multiple_of(t * tile, tile), tile))
+            return c
+
+        lax.fori_loop(0, full_tiles, act_tile, 0)
+        if tail:
+            act(pl.ds(full_tiles * tile, tail))
+
+        @pl.when(step < LANES - 1)
+        def _():
+            arrivals(step + 1)
+
+        def back_tile(t, c):
+            cols = pl.ds(pl.multiple_of(t * tile, tile), tile)
+            pb[mine, cols] = (nt(gg[mine, :], wg[cols, :]) + nt(gu[mine, :], wu[cols, :])).astype(BF16)
+            return c
+
+        lax.fori_loop(0, width // tile, back_tile, 0)
+
+        @pl.when(jnp.logical_and(is_end, step > 0))
+        def _():
+            sum_send(*back, block).start()
+
+        return carry
+
+    lax.fori_loop(0, LANES, block_step, 0)
+
+    def down_step(step, carry):
+        block = order_of(LANES - 1 - step, lane)
+        mine = rows_of(block, tok)
+
+        def down_tile(t, c):
+            cols = pl.ds(pl.multiple_of(t * tile, tile), tile)
+            wg[mine, cols] = nt(hid[mine, :], wd[cols, :]).astype(BF16)
+            return c
+
+        lax.fori_loop(0, width // tile, down_tile, 0)
+
+        @pl.when(jnp.logical_and(is_end, step < LANES - 1))
+        def _():
+            sum_send(*ahead, block).start()
+
+        return carry
+
+    lax.fori_loop(0, 2, down_step, 0)
+    mid_near, mid_far, mid_back = 3 - lane, 6 - 3 * lane, 3 * lane - 3
+    sum_pass(*back, mid_near)
+    lax.fori_loop(2, LANES, down_step, 0)
+
+    def grad_tile(k, carry):
+        part = pl.ds(pl.multiple_of(k * wtile, wtile), wtile)
+        turned = (pl.ds(2 * wtile, wtile), pl.ds(0, LANES * tok))
+        turned_og = (pl.ds(3 * wtile, wtile), pl.ds(0, LANES * tok))
+        wu[turned] = xb[:, part].T
+        wu[turned_og] = og[:, part].T
+        copies = []
+        for which, (lhs, rhs) in enumerate(((turned, gg), (turned, gu), (turned_og, hid))):
+            slot = which % 2
+            stage = pl.ds(slot * wtile, wtile)
+            if which >= 2:
+                copies[which - 2].wait()
+
+            def tile_of(cols):
+                wu[stage, cols] = nn(wu[lhs], rhs[:, cols]).astype(BF16)
+
+            def step(t, c):
+                tile_of(pl.ds(pl.multiple_of(t * tile, tile), tile))
+                return c
+
+            lax.fori_loop(0, full_tiles, step, 0)
+            if tail:
+                tile_of(pl.ds(full_tiles * tile, tail))
+            copy = pltpu.make_async_copy(wu.at[stage], gw_hbm.at[which, part], out_sem.at[which])
+            copy.start()
+            copies.append(copy)
+        copies[1].wait()
+        copies[2].wait()
+        return carry
+
+    wtiles = width // wtile
+    lax.fori_loop(0, 1, grad_tile, 0)
+    sum_pass(*back, mid_far)
+    lax.fori_loop(1, wtiles - 1, grad_tile, 0)
+    sum_pass(*back, mid_back)
+    lax.fori_loop(wtiles - 1, wtiles, grad_tile, 0)
+    sum_pass(*ahead, mid_far)
+    sum_last(*back, gm_ref)
+    sum_pass(*ahead, mid_back)
+    sum_pass(*ahead, mid_near)
+    sum_last(*ahead, mo_ref)
+
+    for block in range(LANES):
+        @pl.when(jnp.logical_and(has_right, block <= lane))
+        def _(block=block):
+            gather_copy(block, 0).wait_send()
+
+        @pl.when(jnp.logical_and(has_left, block >= lane))
+        def _(block=block):
+            gather_copy(block, 1).wait_send()
+
+        @pl.when(block != lane)
+        def _(block=block):
+            sum_send(*back, block).wait_send()
+            sum_send(*ahead, block).wait_send()
+
+
+def feed_forward(mlp_local, grad_rows, gate_full, up_full, down_full):
+    tok, width = mlp_local.shape
+    units = gate_full.shape[1]
+    row = tok * LANES
+    anywhere = pl.BlockSpec(memory_space=pl.ANY)
+    vmem = pl.BlockSpec(memory_space=pltpu.VMEM)
+    dma = pltpu.SemaphoreType.DMA
+    return pl.pallas_call(
+        ff_kernel,
+        out_shape=(
+            jax.ShapeDtypeStruct((tok, width), F32),
+            jax.ShapeDtypeStruct((tok, width), F32),
+            jax.ShapeDtypeStruct((3, width, units), BF16),
+        ),
+        in_specs=[anywhere] * 5,
+        out_specs=(vmem, vmem, anywhere),
+        scratch_shapes=[
+            pltpu.VMEM((row, width), BF16),
+            pltpu.VMEM((row, width), BF16),
+            pltpu.VMEM((width, units), BF16),
+            pltpu.VMEM((width, units), BF16),
+            pltpu.VMEM((width, units), BF16),
+            pltpu.VMEM((row, units), BF16),
+            pltpu.VMEM((row, units), BF16),
+            pltpu.VMEM((row, units), BF16),
+            pltpu.VMEM((row, width), BF16),
+            pltpu.VMEM((row + tok, width), BF16),
+            pltpu.VMEM((row + tok, width), BF16),
+            dma((5,)),
+            dma((2, LANES)),
+            dma((LANES,)),
+            dma((LANES,)),
+            dma((LANES + 1,)),
+            dma((LANES,)),
+            dma((LANES + 1,)),
+            dma((3,)),
+        ],
+        compiler_params=pltpu.CompilerParams(
+            collective_id=3, has_side_effects=True, vmem_limit_bytes=60 * 2**20
+        ),
+        cost_estimate=pl.CostEstimate(
+            flops=18 * row * width * units, bytes_accessed=12 * width * units, transcendentals=row * units
+        ),
+        name="feed_forward",
+    )(mlp_local, grad_rows, gate_full, up_full, down_full)
 
 
 def body(
@@ -183,50 +529,20 @@
     resid = input_f32 + jnp.dot(attended, out_full, preferred_element_type=jnp.float32)
     factor_two = norm_factor(resid)
     mlp_local = (resid * factor_two * mlp_gain).astype(jnp.bfloat16)
-    mlp_in = lax.all_gather(mlp_local, "seq", axis=0, tiled=True)
+    grad_rows = lax.all_gather(out_grad, "seq", axis=0, tiled=True)
     gate_full, up_full, down_full = (
         lax.all_gather(w_gate, "dp", axis=0, tiled=True),
         lax.all_gather(w_up, "dp", axis=0, tiled=True),
         lax.all_gather(w_down, "dp", axis=0, tiled=True),
     )
-    gate_act = jnp.dot(mlp_in, gate_full, preferred_element_type=jnp.float32)
-    up_act = jnp.dot(mlp_in, up_full, preferred_element_type=jnp.float32)
-    gate_sig = jax.nn.sigmoid(gate_act)
-    silu_act = gate_act * gate_sig
-    hidden = (silu_act * up_act).astype(jnp.bfloat16)
-    mlp_part = contract_cols(hidden, down_full)
-    mlp_out = lax.psum_scatter(mlp_part, "seq", scatter_dimension=0, tiled=True)
+    mlp_out, grad_mlp_in, mlp_grads = feed_forward(
+        mlp_local, grad_rows, gate_full, up_full, down_full
+    )
     block_out = (resid + mlp_out).astype(jnp.bfloat16)
-    grad_rows = lax.all_gather(out_grad, "seq", axis=0, tiled=True)
-    gate_back, up_back, down_back = (
-        lax.all_gather(w_gate, "dp", axis=0, tiled=True),
-        lax.all_gather(w_up, "dp", axis=0, tiled=True),
-        lax.all_gather(w_down, "dp", axis=0, tiled=True),
-    )
-    grad_hidden = jnp.dot(grad_rows, down_back, preferred_element_type=jnp.float32)
-    grad_gate = (grad_hidden * up_act * gate_sig * (1.0 + gate_act * (1.0 - gate_sig))).astype(
-        jnp.bfloat16
-    )
-    grad_up = (grad_hidden * silu_act).astype(jnp.bfloat16)
-    mlp_in_part = contract_cols(grad_gate, gate_back) + contract_cols(grad_up, up_back)
-    grad_mlp_in = lax.psum_scatter(mlp_in_part, "seq", scatter_dimension=0, tiled=True)
-    mlp_grads = lax.psum_scatter(
-        jnp.concatenate(
-            [
-                contract_rows(mlp_in, grad_gate),
-                contract_rows(mlp_in, grad_up),
-                contract_rows(grad_rows, hidden),
-            ],
-            axis=1,
-        ),
-        "dp",
-        scatter_dimension=0,
-        tiled=True,
-    )
-    hidden_width = hidden.shape[1]
-    gate_grad = mlp_grads[:, :hidden_width]
-    up_grad = mlp_grads[:, hidden_width : 2 * hidden_width]
-    down_grad = mlp_grads[:, 2 * hidden_width :]
+    gate_grad, up_grad, down_grad = (
+        lax.psum_scatter(mlp_grads[k], "dp", scatter_dimension=0, tiled=True).astype(jnp.float32)
+        for k in range(3)
+    )
     mlp_gain_part = jnp.sum(grad_mlp_in * resid * factor_two, axis=0)
     grad_resid = out_grad.astype(jnp.float32) + norm_back(grad_mlp_in, resid, factor_two, mlp_gain)
     grad_resid_low = grad_resid.astype(jnp.bfloat16)

time: 1430 us -> 1170 us (0.82)
  waiting for transfers between devices: 903 us -> 675 us
  Pallas kernels: 0 us -> 157 us
  matrix products: 177 us -> 66.9 us
  local copies, waits for them, and re-layouts: 113 us -> 64.6 us
  other arithmetic: 72.3 us -> 45.1 us
    unnamed x16 -> x14, waiting for transfers between devices: 205 us -> 4.98 us
    pallas_call x0 -> x1, Pallas kernels: none -> 157 us  [feed_forward(): pl.pallas_call(ff_kernel, out_shape=(jax.ShapeDtypeStruct((tok, width), F...]
    all_gather x1 -> x0, waiting for transfers between devices: 60 us -> none  [body(): mlp_in = lax.all_gather(mlp_local, 'seq', axis=0, tiled=True)]
    reduce_scatter x2 -> x3, waiting for transfers between devices: 209 us -> 153 us  [body(): lax.psum_scatter(mlp_grads[k], 'dp', scatter_dimension=0, tiled=True)]
    all_gather x1, waiting for transfers between devices: 51.7 us -> 0.01 us  [body(): grad_rows = lax.all_gather(out_grad, 'seq', axis=0, tiled=True)]
    all_gather x1, waiting for transfers between devices: 0.02 us -> 50.6 us  [body(): lax.all_gather(w_up, 'dp', axis=0, tiled=True)]
    unnamed x120 -> x127, local copies, waits for them, and re-layouts: 74.9 us -> 24.9 us
    reduce_scatter x1, waiting for transfers between devices: 33 us -> 80 us  [body(): lax.psum_scatter(partials[3], 'dp', scatter_dimension=1, tiled=True)]
  transfers between devices with their start and end apart: 19 -> 18, of which waited for: 13 -> 14; matrix products, arithmetic and copies ran while one was open for 17% -> 9% of each run, Pallas kernels for 0% -> 0%
where the time goes in v1:
time: 1170 us
  waiting for transfers between devices  675 us (58%)
  Pallas kernels  157 us (13%)
  blocking collectives  114 us (10%)
  matrix products  66.9 us (6%)
  local copies, waits for them, and re-layouts  64.6 us (6%)
  other arithmetic  45.1 us (4%)
  starting transfers between devices  25.9 us (2%)
  between operations  17.7 us (2%)
    pallas_call x1, Pallas kernels, feed_forward(): pl.pallas_call(ff_kernel, out_shape=(jax.ShapeDtypeStruct((tok, width), F...  157 us
    reduce_scatter x3, waiting for transfers between devices, body(): lax.psum_scatter(mlp_grads[k], 'dp', scatter_dimension=0, tiled=True)  153 us
    psum x1, waiting for transfers between devices, body(): lax.psum((local_terms[0], local_terms[1], local_terms[2], local_terms[3],...  110 us
    reduce_scatter x1, waiting for transfers between devices, body(): lax.psum_scatter(partials[3], 'dp', scatter_dimension=1, tiled=True)  80 us
    reduce_scatter x1, waiting for transfers between devices, body(): lax.psum_scatter(partials[0], 'dp', scatter_dimension=0, tiled=True)  79.9 us
    all_to_all x1, waiting for transfers between devices, body(): lax.all_to_all(outgoing, 'seq', split_axis=1, concat_axis=0, tiled=True)  51.3 us
    all_gather x1, waiting for transfers between devices, body(): lax.all_gather(w_down, 'dp', axis=0, tiled=True)  50.6 us
    all_gather x1, waiting for transfers between devices, body(): lax.all_gather(w_up, 'dp', axis=0, tiled=True)  50.6 us
  transfers between devices with their start and end apart: 18, of which 14 were waited for; matrix products, arithmetic and copies ran while one was open for 9% of the time, Pallas kernels for 0%

profile of v1, /device:TPU:0, one launch (start us, length us, event | category | flops | bytes accessed | tf_op | source)
XLA Modules:
  0.0 1166.5 jit_solution(11785357088342823033)
XLA Ops:
  12.5 6.3 all-to-all-start
  22.6 24.3 %all-reduce.13 = (bf16[256]{0:T(256)(128)(2,1)S(1)}, bf16[1536]{0:T(1024)(128)(2,1)S(1)}, bf16[256]{0:T(256)(128)(2,1)S(1)}, bf16[1536]{0:T(1024)(128)(2,1)S(1)}, bf16[1536]{0:T(1024)(128)(2,1)S(1)}) all-reduce(bf16[256]{0:T(256)(128)(2,1)S(1)} %dynamic-update-slice.3, ...), channel_id=1, replica_groups=mesh['dp'=8,'seq'=4] {'dp'}, use_global_device_ids=true, to_apply=%add.3 | all-reduce | flops 5120 | bytes 20480
  47.7 9.5 all_gather.42
  58.1 13.4 %all_gather.44 = bf16[1536,256]{1,0:T(8,128)(2,1)S(1)} all-gather(bf16[192,256]{1,0:T(8,128)(2,1)S(1)} %copy-done.40), channel_id=1, replica_groups=mesh['dp'=8,'seq'=4] {'dp'}, dimensions={0}, use_global_device_ids=true | all-gather | bytes 884736 | tf_op jit(solution)/shard_map/all_gather | solution.py:449
  73.0 4.9 convolution_add_fusion.2
  83.0 4.6 all-to-all-start.1
  87.7 51.3 %all-to-all-done.1 = bf16[256,4,640]{0,2,1:T(8,128)(2,1)S(1)} async-done(((bf16[256,4,640]{0,2,1:T(8,128)(2,1)}), bf16[256,4,640]{0,2,1:T(8,128)(2,1)S(1)}, u32[]{:S(2)}, u32[]{:S(2)}) %all-to-all-start.1) | async-done | bytes 1310752 | tf_op jit(solution)/shard_map/all_to_all | solution.py:499
  143.2 15.2 %while.27 = (s32[]{:T(128)}, bf16[2,512,3,128]{3,1,2,0:T(8,128)(2,1)S(1)}, f32[2,3,512]{2,1,0:T(4,128)S(1)}, bf16[2,512]{1,0:T(2,128)(2,1)S(1)}, bf16[1024,1]{0,...) while((s32[]{:T(128)}, ...), condition=%wide.region_4.5_spmd, body=%wide.region_1.4_spmd.sunk | while | flops 826997760 | bytes 22355088 | solution.py:524
  161.2 3.2 reshape.358
  164.4 6.4 reduce.15
  171.8 6.6 all-to-all-start.2
  178.4 16.3 %all-to-all-done.2 = bf16[4,2,49152]{2,1,0:T(2,128)(2,1)} async-done(((bf16[4,2,49152]{2,1,0:T(2,128)(2,1)}), bf16[4,2,49152]{2,1,0:T(2,128)(2,1)}, u32[]{:S(2)}, u32[]{:S(2)}) %all-to-all-start.2) | async-done | bytes 786464 | tf_op jit(solution)/shard_map/all_to_all | solution.py:526
  194.7 2.5 reshape.373
  200.5 4.1 multiply_reduce_fusion.2
  205.9 13.4 %all-gather.13.cloned.1.call-done.wg_hbm = bf16[1536,2240]{1,0:T(8,128)(2,1)} async-done(((bf16[192,2240]{1,0:T(8,128)(2,1)}), bf16[1536,2240]{1,0:T(8,128)(2,1)}) %all-gather.13.cloned.1.call-update) | async-done | bytes 6881296 | tf_op jit(solution)/shard_map/all_gather | solution.py:534
  219.3 50.6 %all-gather.15.cloned.1.call-done.wu_hbm = bf16[1536,2240]{1,0:T(8,128)(2,1)} async-done(((bf16[192,2240]{1,0:T(8,128)(2,1)}), bf16[1536,2240]{1,0:T(8,128)(2,1)}) %all-gather.15.cloned.1.call-update) | async-done | bytes 6881296 | tf_op jit(solution)/shard_map/all_gather | solution.py:535
  269.9 50.6 %all-gather.17.cloned.1.call-done.wd_hbm = bf16[1536,2240]{1,0:T(8,128)(2,1)} async-done(((bf16[192,2240]{1,0:T(8,128)(2,1)}), bf16[1536,2240]{1,0:T(8,128)(2,1)}) %all-gather.17.cloned.1.call-update) | async-done | bytes 6881296 | tf_op jit(solution)/shard_map/all_gather | solution.py:536
  320.5 157.0 %feed_forward.1 = (f32[256,1536]{1,0:T(8,128)}, f32[256,1536]{1,0:T(8,128)}, bf16[3,1536,2240]{2,1,0:T(8,128)(2,1)}) custom-call(bf16[256,1536]{1,0:T(8,128)(2,1)} %multiply_convert_fusion.x_hbm, bf16[1024,1536]{1,0:T(8,128)(2,1)} %all-gather.11.cloned.1.call-done.og_hbm, bf16[1536,2240]{1,0:T(8,128)(2,1)} %all-gather.13.cloned.1.call-done.wg_hbm, ...), custom_call_target="tpu_custom_call" | custom-call | flops 63417876480 | bytes 41287680 | tf_op jit(solution)/shard_map/feed_forward/pallas_call | solution.py:381
  477.5 2.5 multiply_reduce_fusion
  480.1 3.3 subtract_add_fusion
  486.0 7.5 all-to-all-start.3
  493.7 15.9 %all-to-all-done.3 = bf16[256,4,384]{0,2,1:T(8,128)(2,1)S(1)} async-done(((bf16[256,4,384]{0,2,1:T(8,128)(2,1)}), bf16[256,4,384]{0,2,1:T(8,128)(2,1)S(1)}, u32[]{:S(2)}, u32[]{:S(2)}) %all-to-all-start.3) | async-done | bytes 786464 | tf_op jit(solution)/shard_map/all_to_all | solution.py:551
  512.4 36.2 %while.28 = (s32[]{:T(128)}, f32[1024,128]{1,0:T(8,128)}, f32[1024,128]{1,0:T(8,128)}, bf16[2,512,3,128]{3,1,2,0:T(8,128)(2,1)}, bf16[2,512]{1,0:T(2,128)(2,1)S(...) while((s32[]{:T(128)}, f32[1024,128]{1,0:T(8,128)}, ...), condition=%wide.region_9.10_spmd.clone, body=%wide.region_7.9_spmd.clone.sunk | while | flops 2040527872 | bytes 97184688 | solution.py:588
  515.4 2.6 fusion.140
  521.7 2.9 fusion.142
  524.6 5.7 fusion.143
  533.4 2.6 fusion.140
  539.7 3.0 fusion.142
  542.7 5.9 fusion.143
  555.4 31.9 %all_to_all.82 = bf16[4,2,81920]{2,1,0:T(2,128)(2,1)} all-to-all(bf16[4,2,81920]{2,1,0:T(2,128)(2,1)S(1)} %reshape.374), channel_id=1, replica_groups=mesh['dp'=8,'seq'=4] {'seq'}, dimensions={0} | all-to-all | bytes 2621440 | tf_op jit(solution)/shard_map/all_to_all | solution.py:601
  587.3 2.8 reshape.375
  598.7 5.1 fusion.69
  606.0 5.1 fusion.79
  611.1 14.2 %slice_bitcast_fusion = (bf16[1536,2240]{1,0:T(8,128)(2,1)}, bf16[1536,2240]{1,0:T(8,128)(2,1)}, bf16[1536,2240]{1,0:T(8,128)(2,1)}) fusion(bf16[3,1536,2240]{2,1,0:T(8,128)(2,1)} %get-tuple-element.136), kind=kLoop, calls=%fused_computation.66 | loop fusion | bytes 41287680 | tf_op jit(solution)/shard_map/squeeze | solution.py:543
  626.8 6.3 reduce-scatter.16.cloned.1.call-done
  633.1 42.4 %reduce-scatter.18.cloned.1.call-done = f32[192,256]{1,0:T(8,128)} async-done(((f32[1536,256]{1,0:T(8,128)}), f32[192,256]{1,0:T(8,128)}) %reduce-scatter.18.cloned.1.call-update) | async-done | bytes 196624 | tf_op jit(solution)/shard_map/reduce_scatter | solution.py:676
  675.4 80.0 %reduce-scatter.20.cloned.1.call-done = f32[1536,192]{0,1:T(8,128)} async-done(((f32[1536,1536]{0,1:T(8,128)}), f32[1536,192]{0,1:T(8,128)}) %reduce-scatter.20.cloned.1.call-update) | async-done | bytes 1179664 | tf_op jit(solution)/shard_map/reduce_scatter | solution.py:680
  755.5 79.9 %reduce-scatter.14.cloned.1.call-done = f32[192,1536]{1,0:T(8,128)} async-done(((f32[1536,1536]{1,0:T(8,128)}), f32[192,1536]{1,0:T(8,128)}) %reduce-scatter.14.cloned.1.call-update) | async-done | bytes 1179664 | tf_op jit(solution)/shard_map/reduce_scatter | solution.py:674
  838.8 3.8 fusion.88
  845.6 23.3 %all-reduce.10 = (f32[1536]{0:T(1024)S(1)}, f32[1536]{0:T(1024)S(1)}, f32[256]{0:T(256)S(1)}, f32[256]{0:T(256)S(1)}, f32[1536]{0:T(1024)S(1)}) all-reduce(f32[1536]{0:T(1024)S(1)} %get-tuple-element.262, f32[1536]{0:T(1024)S(1)} %reduce_sum.131, f32[256]{0:T(256)S(1)} %bitcast.305, ...), channel_id=2, replica_groups=mesh['dp'=8,'seq'=4] {'dp'}, use_global_device_ids=true, to_apply=%region_15.16.clone | all-reduce | flops 5120 | bytes 40960
  869.3 12.2 %all-reduce.11 = (f32[192]{0:T(256)}, f32[192]{0:T(256)}, f32[32]{0:T(128)}, f32[32]{0:T(128)}, f32[192]{0:T(256)}) all-reduce(f32[192]{0:T(256)S(1)} %dynamic-slice.6, f32[192]{0:T(256)S(1)} %dynamic-slice.8, f32[32]{0:T(128)S(1)} %dynamic-slice.10, f32[32]{0:T(128)S(1)} %dynamic-slice.12, ...), channel_id=1, replica_groups=mesh['dp'=8,'seq'=4] {'seq'}, use_global_device_ids=true, to_apply=%region_14.15 | all-reduce | flops 640 | bytes 5120 | tf_op jit(solution)/shard_map/psum | solution.py:656
  881.5 3.0 fusion.63
  884.5 19.9 %reduce-scatter.8.cloned.1.call-done = bf16[192,2240]{1,0:T(8,128)(2,1)} async-done(((bf16[1536,2240]{1,0:T(8,128)(2,1)}), bf16[192,2240]{1,0:T(8,128)(2,1)}) %reduce-scatter.8.cloned.1.call-update) | async-done | bytes 860176 | tf_op jit(solution)/shard_map/reduce_scatter | solution.py:543
  906.9 66.8 %reduce-scatter.10.cloned.1.call-done = bf16[192,2240]{1,0:T(8,128)(2,1)} async-done(((bf16[1536,2240]{1,0:T(8,128)(2,1)}), bf16[192,2240]{1,0:T(8,128)(2,1)}) %reduce-scatter.10.cloned.1.call-update) | async-done | bytes 860176 | tf_op jit(solution)/shard_map/reduce_scatter | solution.py:543
  973.7 2.5 convert_element_type.186
  976.2 66.5 %reduce-scatter.12.cloned.1.call-done = bf16[192,2240]{1,0:T(8,128)(2,1)} async-done(((bf16[1536,2240]{1,0:T(8,128)(2,1)}), bf16[192,2240]{1,0:T(8,128)(2,1)}) %reduce-scatter.12.cloned.1.call-update) | async-done | bytes 860176 | tf_op jit(solution)/shard_map/reduce_scatter | solution.py:543
  1042.8 2.5 convert_element_type.187
  1045.3 109.6 %all-reduce.16.cloned.1.call-done = (f32[192,1536]{1,0:T(8,128)}, f32[192,256]{1,0:T(8,128)}, f32[192,256]{1,0:T(8,128)}, f32[1536,192]{0,1:T(8,128)}) async-done(((f32[192,1536]{1,0:T(8,128)}, f32[192,256]{1,0:T(8,128)}, f32[192,256]{1,0:T(8,128)}, f32[1536,192]{0,1:T(8,128)}), (f32[192,1536]{1,0:T(8,128)}, f32[192,256]{1,0:T(8,128)}, f32[192,256]{1,0:T(8,128)}, ...) | async-done | bytes 2752528 | tf_op jit(solution)/shard_map/psum | solution.py:656
  (298 shorter events, 93.7 us)
Async XLA Ops:
  7.2 65.8 %all-gather.7.cloned.1.call-start = ((), (), s32[]{:S(2)}) async-start(), calls=%async_computation.12 | async-start | bytes 5308416 | tf_op jit(solution)/shard_map/all_gather | solution.py:447
  7.9 192.6 %all-gather.9.cloned.1.call-start = ((), (), s32[]{:S(2)}) async-start(), calls=%async_computation.13 | async-start | bytes 5308416 | tf_op jit(solution)/shard_map/all_gather | solution.py:450
  8.7 10.7 copy-start.45
  8.7 12.6 %copy-start.48 = (bf16[192]{0:T(256)(128)(2,1)S(1)}, bf16[192]{0:T(256)(128)(2,1)}, u32[]{:S(2)}) copy-start(bf16[192]{0:T(256)(128)(2,1)} %param.24) | copy-start | bytes 1156
  8.7 12.9 %copy-start.49 = (bf16[192]{0:T(256)(128)(2,1)S(1)}, bf16[192]{0:T(256)(128)(2,1)}, u32[]{:S(2)}) copy-start(bf16[192]{0:T(256)(128)(2,1)} %param.28) | copy-start | bytes 1156
  8.7 13.1 %copy-start.50 = (bf16[192]{0:T(256)(128)(2,1)S(1)}, bf16[192]{0:T(256)(128)(2,1)}, u32[]{:S(2)}) copy-start(bf16[192]{0:T(256)(128)(2,1)} %param.32) | copy-start | bytes 1156
  8.7 13.4 %copy-start.51 = (bf16[32]{0:T(256)(128)(2,1)S(1)}, bf16[32]{0:T(256)(128)(2,1)}, u32[]{:S(2)}) copy-start(bf16[32]{0:T(256)(128)(2,1)} %param.29) | copy-start | bytes 196
  8.7 13.6 %copy-start.52 = (bf16[32]{0:T(256)(128)(2,1)S(1)}, bf16[32]{0:T(256)(128)(2,1)}, u32[]{:S(2)}) copy-start(bf16[32]{0:T(256)(128)(2,1)} %param.30) | copy-start | bytes 196
  8.7 197.2 %all-gather.11.cloned.1.call-start = ((), (), s32[]{:S(2)}) async-start(), calls=%async_computation.14 | async-start | bytes 3932160 | tf_op jit(solution)/shard_map/all_gather | solution.py:532
  9.5 37.4 %copy-start.5 = (bf16[256,1536]{1,0:T(8,128)(2,1)S(1)}, bf16[256,1536]{1,0:T(8,128)(2,1)}, u32[]{:S(2)}) copy-start(bf16[256,1536]{1,0:T(8,128)(2,1)} %param.20) | copy-start | bytes 2359300
  9.5 38.2 %copy-start.46 = (s32[256]{0:T(256)S(1)}, s32[256]{0:T(256)}, u32[]{:S(2)}) copy-start(s32[256]{0:T(256)} %param.22) | copy-start | bytes 3076
  9.5 38.2 %copy-start.39 = (bf16[192,256]{1,0:T(8,128)(2,1)S(1)}, bf16[192,256]{1,0:T(8,128)(2,1)}, u32[]{:S(2)}) copy-start(bf16[192,256]{1,0:T(8,128)(2,1)} %param.26) | copy-start | bytes 294916
  9.5 209.8 %all-gather.13.cloned.1.call-start = ((), (), s32[]{:S(2)}) async-start(), calls=%async_computation.15 | async-start | bytes 7962624 | tf_op jit(solution)/shard_map/all_gather | solution.py:534
  10.1 259.8 %all-gather.15.cloned.1.call-start = ((), (), s32[]{:S(2)}) async-start(), calls=%async_computation.16 | async-start | bytes 7962624 | tf_op jit(solution)/shard_map/all_gather | solution.py:535
  12.5 70.5 %all-to-all-start = ((bf16[4,2,128]{2,1,0:T(2,128)(2,1)}), bf16[4,2,128]{2,1,0:T(2,128)(2,1)S(1)}, u32[]{:S(2)}, u32[]{:S(2)}) async-start(bf16[4,2,128]{2,1,0:T(2,128)(2,1)} %reshape.370), calls=%async_computation | async-start | bytes 4096 | tf_op jit(solution)/shard_map/all_to_all | solution.py:500
  18.8 301.7 %all-gather.17.cloned.1.call-start = ((), (), s32[]{:S(2)}) async-start(), calls=%async_computation.17 | async-start | bytes 7962624 | tf_op jit(solution)/shard_map/all_gather | solution.py:536
  46.8 26.1 %copy-start.35 = (f32[1536]{0:T(1024)}, f32[1536]{0:T(1024)S(1)}, u32[]{:S(2)}) copy-start(f32[1536]{0:T(1024)S(1)} %convert_element_type.152) | copy-start | bytes 18436
  47.7 25.3 %copy-start.41 = (f32[256]{0:T(256)}, f32[256]{0:T(256)S(1)}, u32[]{:S(2)}) copy-start(f32[256]{0:T(256)S(1)} %get-tuple-element.349) | copy-start | bytes 3076
  57.2 14.3 %copy-start.27 = (bf16[1536,256]{1,0:T(8,128)(2,1)}, bf16[1536,256]{1,0:T(8,128)(2,1)S(1)}, u32[]{:S(2)}) copy-start(bf16[1536,256]{1,0:T(8,128)(2,1)S(1)} %all_gather.42) | copy-start | bytes 2359300
  71.5 8.8 copy-start.22
  71.6 9.0 copy-start.24
  83.0 56.0 %all-to-all-start.1 = ((bf16[256,4,640]{0,2,1:T(8,128)(2,1)}), bf16[256,4,640]{0,2,1:T(8,128)(2,1)S(1)}, u32[]{:S(2)}, u32[]{:S(2)}) async-start(bf16[256,4,640]{0,2,1:T(8,128)(2,1)} %pad_maximum_fusion.1), calls=%async_computation.1 | async-start | bytes 2621440 | tf_op jit(solution)/shard_map/all_to_all | solution.py:499
  159.2 5.1 copy-start.15
  171.8 22.9 %all-to-all-start.2 = ((bf16[4,2,49152]{2,1,0:T(2,128)(2,1)}), bf16[4,2,49152]{2,1,0:T(2,128)(2,1)}, u32[]{:S(2)}, u32[]{:S(2)}) async-start(bf16[4,2,49152]{2,1,0:T(2,128)(2,1)} %reshape.372), calls=%async_computation.2 | async-start | bytes 1572864 | tf_op jit(solution)/shard_map/all_to_all | solution.py:526
  204.6 272.9 %copy-start.12 = (f32[256,1536]{1,0:T(8,128)}, f32[256,1536]{1,0:T(8,128)S(1)}, u32[]{:S(2)}) copy-start(f32[256,1536]{1,0:T(8,128)S(1)} %get-tuple-element.355) | copy-start | bytes 4718596
  477.5 5.9 slice-start
  486.0 23.6 %all-to-all-start.3 = ((bf16[256,4,384]{0,2,1:T(8,128)(2,1)}), bf16[256,4,384]{0,2,1:T(8,128)(2,1)S(1)}, u32[]{:S(2)}, u32[]{:S(2)}) async-start(bf16[256,4,384]{0,2,1:T(8,128)(2,1)} %bitcast.28), calls=%async_computation.3 | async-start | bytes 1572864 | tf_op jit(solution)/shard_map/all_to_all | solution.py:551
  493.5 139.6 %reduce-scatter.16.cloned.1.call-start = ((), (), s32[]{:S(2)}) async-start(), calls=%async_computation.22 | async-start | bytes 1769472 | tf_op jit(solution)/shard_map/reduce_scatter | solution.py:675
  514.4 3.7 copy-start.1
  524.6 5.8 copy-start.4
  524.6 5.8 copy-start.14
  524.6 5.8 copy-start.17
  532.3 3.7 copy-start.1
  542.7 5.9 copy-start.4
  542.7 5.9 copy-start.14
  542.7 5.9 copy-start.17
  596.4 79.1 %reduce-scatter.18.cloned.1.call-start = ((), (), s32[]{:S(2)}) async-start(), calls=%async_computation.23 | async-start | bytes 1769472 | tf_op jit(solution)/shard_map/reduce_scatter | solution.py:676
  598.4 157.0 %reduce-scatter.20.cloned.1.call-start = ((), (), s32[]{:S(2)}) async-start(), calls=%async_computation.24 | async-start | bytes 10616832 | tf_op jit(solution)/shard_map/reduce_scatter | solution.py:680
  603.8 231.5 %reduce-scatter.14.cloned.1.call-start = ((), (), s32[]{:S(2)}) async-start(), calls=%async_computation.21 | async-start | bytes 10616832 | tf_op jit(solution)/shard_map/reduce_scatter | solution.py:674
  611.1 293.4 %reduce-scatter.8.cloned.1.call-start = ((), (), s32[]{:S(2)}) async-start(), calls=%async_computation.18 | async-start | bytes 7962624 | tf_op jit(solution)/shard_map/reduce_scatter | solution.py:543
  625.4 348.4 %reduce-scatter.10.cloned.1.call-start = ((), (), s32[]{:S(2)}) async-start(), calls=%async_computation.19 | async-start | bytes 7962624 | tf_op jit(solution)/shard_map/reduce_scatter | solution.py:543
  626.0 416.8 %reduce-scatter.12.cloned.1.call-start = ((), (), s32[]{:S(2)}) async-start(), calls=%async_computation.20 | async-start | bytes 7962624 | tf_op jit(solution)/shard_map/reduce_scatter | solution.py:543
  626.7 528.2 %all-reduce.16.cloned.1.call-start = ((), (), s32[]{:S(2)}) async-start(), calls=%async_computation.25 | async-start | bytes 5505024 | tf_op jit(solution)/shard_map/psum | solution.py:656
  838.7 3.9 copy-start.28
  838.7 3.9 copy-start.33
  843.8 37.8 %copy-start.11 = (f32[256,1536]{1,0:T(8,128)S(1)}, f32[256,1536]{1,0:T(8,128)}, u32[]{:S(2)}) copy-start(f32[256,1536]{1,0:T(8,128)} %copy-done.9) | copy-start | bytes 4718596
  843.8 37.8 %copy-start.44 = (f32[256]{0:T(256)S(1)}, f32[256]{0:T(256)}, u32[]{:S(2)}) copy-start(f32[256]{0:T(256)} %get-tuple-element.348) | copy-start | bytes 3076
  1154.9 3.8 copy-start.34
  (33 other events, 73.0 us)
Sparse Core Ops, SparseCore 0:
  9.9 41.8 all-gather.6
  53.6 41.4 all-gather.8
  96.7 73.8 all-gather.10
  172.4 46.8 all-gather.12
  221.0 48.8 all-gather.14
  271.7 48.8 all-gather.16
  596.5 36.5 reduce-scatter.15
  636.9 38.4 reduce-scatter.17
  678.9 76.4 reduce-scatter.19
  758.8 76.4 reduce-scatter.13
  838.9 65.5 reduce-scatter.7
  908.2 65.4 reduce-scatter.9
  977.3 65.4 reduce-scatter.11
  1045.4 109.4 all-reduce.15

commit v2 on v1

v2 whole, which is shorter than its diff:
```python
import functools

import jax
import jax.numpy as jnp
import numpy as np
from jax import lax
from jax.experimental import pallas as pl
from jax.experimental.pallas import tpu as pltpu
from jax.sharding import PartitionSpec as P

HEADS = 12
KV_HEADS = 2
HD = 128
EPS = 1e-06
ROPE_BASE = 1000000.0
NEG_FILL = -1e30
MESH_ID = pl.DeviceIdType.MESH
LANES = 4
BF16 = jnp.bfloat16
F32 = jnp.float32


def nn(left, right):
    return jnp.dot(left, right, preferred_element_type=F32)


def nt(left, right):
    return lax.dot_general(left, right, (((1,), (1,)), ((), ())), preferred_element_type=F32)


def rows_of(index, size):
    return pl.ds(pl.multiple_of(index * size, size), size)


def digit(codes, lane):
    return lax.rem(lax.shift_right_logical(jnp.int32(codes), 2 * lane), 4)


def order_of(step, lane):
    tables = ((0, 1, 2, 3), (1, 0, 2, 3), (2, 3, 1, 0), (3, 2, 1, 0))
    codes = [sum(tables[k][i] * 4**k for k in range(LANES)) for i in range(LANES)]
    out = digit(codes[0], lane)
    for i in range(1, LANES):
        out = jnp.where(step == i, digit(codes[i], lane), out)
    return out


def flipped(chip, mask):
    out = chip
    for bit in range(8):
        if mask >> bit & 1:
            out = out + (1 - 2 * lax.rem(chip // 2**bit, 2)) * 2**bit
    return out


def meet_all(chips):
    dp, lane = lax.axis_index("dp"), lax.axis_index("seq")
    chip, core = dp // 2, lax.rem(dp, 2)
    barrier = pltpu.get_barrier_semaphore()
    for mask in range(1, chips):
        pl.semaphore_signal(
            barrier, 1, device_id={"dp": 2 * flipped(chip, mask) + core}, device_id_type=MESH_ID
        )
    pl.semaphore_signal(barrier, 1, device_id={"dp": 2 * chip + 1 - core}, device_id_type=MESH_ID)
    for step in range(1, LANES):
        pl.semaphore_signal(
            barrier, 1, device_id={"seq": lax.rem(lane + step, LANES)}, device_id_type=MESH_ID
        )
    pl.semaphore_wait(barrier, chips + LANES - 1)


class Gather:
    def __init__(self, chips, shard, full, send, fwd, recv, half_send, half_recv, halves=True):
        self.dp = lax.axis_index("dp")
        self.chip, self.core = self.dp // 2, lax.rem(self.dp, 2)
        self.chips, self.shard, self.full = chips, shard, full
        self.send, self.fwd, self.recv = send, fwd, recv
        self.half_send, self.half_recv = half_send, half_recv
        self.rows = shard.shape[0]
        self.square = chips == 4 and halves
        self.masks = (1, 2) if self.square else tuple(range(1, chips))

    def device(self, mask, other=False):
        return 2 * flipped(self.chip, mask) + (1 - self.core if other else self.core)

    def to(self, src, dst, send, recv, target):
        return pltpu.make_async_remote_copy(
            src, dst, send, recv, device_id={"dp": target}, device_id_type=MESH_ID
        )

    def own_copy(self, mask):
        return self.to(
            self.shard, self.full.at[rows_of(self.dp, self.rows)], self.send.at[mask],
            self.recv.at[self.dp], self.device(mask) if mask else self.device(0, True),
        )

    def hand_on(self, source):
        part = self.full.at[rows_of(source, self.rows)]
        return self.to(part, part, self.fwd.at[source // 2], self.recv.at[source], self.device(0, True))

    def half_copy(self, source, half, target):
        size = self.rows // 2
        part = self.full.at[rows_of(2 * source + half, size)]
        return self.to(part, part, self.half_send.at[half], self.half_recv.at[half], target)

    def begin(self):
        for mask in self.masks + (0,):
            self.own_copy(mask).start()

    def relay(self):
        for mask in self.masks:
            source = self.device(mask)
            self.hand_on(source).wait_recv()
            if self.square:
                self.half_copy(source, mask - 1, self.device(3 - mask)).start()
            self.hand_on(source).start()

    def relay_across(self):
        if self.square:
            source = self.device(3)
            for half in range(2):
                self.half_copy(source, half, self.device(1)).wait_recv()
            self.hand_on(source).start()

    def end(self):
        for mask in range(self.chips):
            self.hand_on(self.device(mask, True)).wait_recv()
        for mask in self.masks + (0,):
            self.own_copy(mask).wait_send()
        for mask in range(1, self.chips):
            self.hand_on(self.device(mask)).wait_send()
        if self.square:
            for half in range(2):
                self.half_copy(self.device(half + 1), half, self.device(2 - half)).wait_send()


def spread(out, shards, devices, first, size, count):
    width = out.shape[1]
    column = lax.broadcasted_iota(jnp.int32, (HD, width), 1)
    value = lax.broadcasted_iota(jnp.int32, (HD, width), 0)
    owner = lax.broadcasted_iota(jnp.int32, (devices, width), 1) // size
    mine = owner == lax.broadcasted_iota(jnp.int32, (devices, width), 0)
    for n in range(count):
        total = jnp.zeros((devices, width), F32)
        for part in range(2 if size > HD else 1):
            place = (lax.rem(column, size) == value + part * HD).astype(F32).astype(BF16)
            row = 2 * (first + n) + part
            rows = jnp.concatenate([shards[k * 16 : k * 16 + 16, :][row : row + 1] for k in range(devices)], axis=0)
            total = total + nn(rows, place)
        out[first + n : first + n + 1, :] = jnp.sum(jnp.where(mine, total, 0.0), axis=0, keepdims=True)


def front_kernel(
    chips,
    x_hbm, ids_hbm, freq_ref, og_hbm, vec_hbm, wq_hbm, wk_hbm, wv_hbm, wo_hbm, wg_hbm, wu_hbm, wd_hbm,
    resid_ref, mlp_ref, vecs_ref, qkv_ref, att_ref, lse_ref, cos_ref, sin_ref, segc_ref, segr_ref,
    nrm_hbm, ogf, vecf, wqkvf, wof, wgf, wuf, wdf,
    xb, ids, nrm, wqkv, wo, vecb, ab, own_vec, own_qkv, own_wo, own_gate, own_up, own_down, own_og,
    load_sem, dp_send, dp_fwd, dp_recv, half_send, half_recv, x_send, x_recv, i_send, i_recv, o_send, o_recv, a_send, a_recv,
):
    dp, lane = lax.axis_index("dp"), lax.axis_index("seq")
    chip, core = dp // 2, lax.rem(dp, 2)
    sibling = 2 * chip + 1 - core
    tok, width = x_hbm.shape
    heads = qkv_ref.shape[1] // HD - 2
    has_left, has_right = lane > 0, lane < LANES - 1
    left, right = jnp.maximum(lane - 1, 0), jnp.minimum(lane + 1, LANES - 1)
    here = rows_of(lane, tok)

    first_loads = [
        pltpu.make_async_copy(x_hbm, xb.at[here], load_sem.at[0]),
        pltpu.make_async_copy(ids_hbm, ids.at[lane], load_sem.at[1]),
        pltpu.make_async_copy(og_hbm, own_og, load_sem.at[2]),
    ]
    shards = (vec_hbm, own_qkv, wo_hbm, wg_hbm, wu_hbm, wd_hbm)
    fulls = (vecf, wqkvf, wof, wgf, wuf, wdf)
    own_parts = (own_vec, own_qkv, own_wo, own_gate, own_up, own_down)
    own_loads = [
        pltpu.make_async_copy(s, v, load_sem.at[3 + k])
        for k, (s, v) in enumerate(zip(shards, own_parts))
        if k != 1
    ]
    kv_at = pl.multiple_of(lane * KV_HEADS // LANES * HD, HD)
    qkv_loads = [
        pltpu.make_async_copy(
            wq_hbm.at[:, pl.ds(pl.multiple_of(lane * heads * HD, HD), heads * HD)],
            own_qkv.at[:, pl.ds(0, heads * HD)], load_sem.at[4],
        ),
        pltpu.make_async_copy(
            wk_hbm.at[:, pl.ds(kv_at, HD)], own_qkv.at[:, pl.ds(heads * HD, HD)], load_sem.at[13]
        ),
        pltpu.make_async_copy(
            wv_hbm.at[:, pl.ds(kv_at, HD)], own_qkv.at[:, pl.ds((heads + 1) * HD, HD)], load_sem.at[14]
        ),
    ]
    own_copies = [
        pltpu.make_async_copy(v, f.at[rows_of(dp, v.shape[0])], load_sem.at[3 + k])
        for k, (v, f) in enumerate(zip(own_parts, fulls))
    ]
    og_copy = pltpu.make_async_copy(own_og, ogf.at[here], load_sem.at[2])
    for copy in qkv_loads + first_loads + own_loads:
        copy.start()
    lse_ref[...] = jnp.zeros_like(lse_ref)
    meet_all(chips)

    gathers = [
        Gather(
            chips, shard, full, dp_send.at[k], dp_fwd.at[k], dp_recv.at[k], half_send.at[k], half_recv.at[k], k > 0
        )
        for k, (shard, full) in enumerate(zip(shards, fulls))
    ]

    def line_copy(buf, send, recv, block, way):
        part = buf(block)
        return pltpu.make_async_remote_copy(
            part, part, send.at[way, block], recv.at[block],
            device_id={"seq": right if way == 0 else left}, device_id_type=MESH_ID,
        )

    x_line = (lambda b: xb.at[rows_of(b, tok)], x_send, x_recv)
    i_line = (lambda b: ids.at[b], i_send, i_recv)
    o_line = (lambda b: ogf.at[rows_of(b, tok)], o_send, o_recv)

    def line_begin(*lines):
        @pl.when(has_right)
        def _():
            for line in lines:
                line_copy(*line, lane, 0).start()

        @pl.when(has_left)
        def _():
            for line in lines:
                line_copy(*line, lane, 1).start()

    def line_step(step, *lines):
        @pl.when(lane - step >= 0)
        def _():
            block = jnp.maximum(lane - step, 0)
            for line in lines:
                line_copy(*line, block, 0).wait_recv()

            @pl.when(has_right)
            def _():
                for line in lines:
                    line_copy(*line, block, 0).start()

        @pl.when(lane + step < LANES)
        def _():
            block = jnp.minimum(lane + step, LANES - 1)
            for line in lines:
                line_copy(*line, block, 1).wait_recv()

            @pl.when(has_left)
            def _():
                for line in lines:
                    line_copy(*line, block, 1).start()

    def line_end(*lines):
        for block in range(LANES):
            @pl.when(jnp.logical_and(has_right, block <= lane))
            def _(block=block):
                for line in lines:
                    line_copy(*line, block, 0).wait_send()

            @pl.when(jnp.logical_and(has_left, block >= lane))
            def _(block=block):
                for line in lines:
                    line_copy(*line, block, 1).wait_send()

    with jax.named_scope("first_sends"):
        gathers[0].begin()
        for copy in qkv_loads:
            copy.wait()
        gathers[1].begin()
    first_loads[0].wait()
    first_loads[1].wait()
    line_begin(i_line, x_line)
    for load in own_loads:
        load.wait()
    for copy in own_copies:
        copy.start()
    first_loads[2].wait()
    og_copy.start()
    with jax.named_scope("first_relay"):
        gathers[0].relay()
        gathers[1].relay()
    gathers[2].begin()
    gathers[3].begin()
    with jax.named_scope("first_end"):
        gathers[1].relay_across()
        for copy in own_copies + [og_copy]:
            copy.wait()
        gathers[0].end()
        gathers[1].end()
    vec_load = pltpu.make_async_copy(vecf, vecb, load_sem.at[9])
    wqkv_load = pltpu.make_async_copy(wqkvf, wqkv, load_sem.at[10])
    vec_load.start()
    wqkv_load.start()
    vec_load.wait()
    devices = 2 * chips
    spread(vecs_ref, vecb, devices, 0, width // devices, 3)
    spread(vecs_ref, vecb, devices, 3, KV_HEADS * HD // devices, 2)
    wqkv_load.wait()
    bias = jnp.concatenate(
        [
            vecs_ref[2:3, pl.ds(pl.multiple_of(lane * heads * HD, HD), heads * HD)],
            vecs_ref[3:4, pl.ds(pl.multiple_of(lane * KV_HEADS // LANES * HD, HD), HD)],
            vecs_ref[4:5, pl.ds(pl.multiple_of(lane * KV_HEADS // LANES * HD, HD), HD)],
        ],
        axis=1,
    )
    lane_sign = jnp.where(lax.broadcasted_iota(jnp.int32, (1, HD), 1) < HD // 2, -1.0, 1.0)

    def block_step(step, carry):
        block = order_of(step, lane)
        mine = rows_of(block, tok)
        id_rows = ids[block].astype(F32)
        segr_ref[:, mine] = jnp.broadcast_to(id_rows[1:2, :], (8, tok))
        segc_ref[mine, :] = jnp.broadcast_to(id_rows[1:2, :], (HD, tok)).T
        angles = jnp.broadcast_to(id_rows[0:1, :], (HD, tok)).T * freq_ref[0:1, :]
        cos_ref[mine, :] = jnp.cos(angles)
        sin_ref[mine, :] = jnp.sin(angles) * lane_sign

        def norm(i, c):
            some = pl.ds(pl.multiple_of(block * tok + i * 32, 32), 32)
            x = xb[some, :].astype(F32)
            factor = lax.rsqrt(jnp.mean(x * x, axis=-1, keepdims=True) + EPS)
            nrm[some, :] = (x * factor * vecs_ref[0:1, :]).astype(BF16)
            return c

        lax.fori_loop(0, tok // 32, norm, 0)

        @pl.when(step < LANES - 1)
        def _():
            with jax.named_scope("row_arrival"):
                @pl.when(step == LANES - 2)
                def _():
                    line_begin(o_line)

                line_step(step + 1, i_line, x_line)

        @pl.when(step == 1)
        def _():
            with jax.named_scope("w_out_relay"):
                gathers[2].relay()
            gathers[4].begin()

        pre = nn(nrm[mine, :], wqkv[...]) + bias
        cosine, sine = cos_ref[mine, :], sin_ref[mine, :]
        for h in range(heads + 1):
            cols = slice(h * HD, (h + 1) * HD)
            part = pre[:, cols]
            qkv_ref[mine, cols] = (part * cosine + pltpu.roll(part, HD // 2, 1) * sine).astype(BF16)
        cols = slice((heads + 1) * HD, (heads + 2) * HD)
        qkv_ref[mine, cols] = pre[:, cols].astype(BF16)
        return carry

    lax.fori_loop(0, LANES, block_step, 0)
    nrm_copy = pltpu.make_async_copy(nrm, nrm_hbm, load_sem.at[11])
    nrm_copy.start()
    with jax.named_scope("w_out_across"):
        gathers[2].relay_across()
    with jax.named_scope("gate_relay"):
        gathers[3].relay()
    gathers[5].begin()

    def att_send(i):
        cols = pl.ds(pl.multiple_of(lane * heads * HD, HD), heads * HD)
        return pltpu.make_async_remote_copy(
            ab.at[pl.ds(i * tok, tok)], att_ref.at[:, cols], a_send.at[i], a_recv.at[lane],
            device_id={"seq": i}, device_id_type=MESH_ID,
        )

    sub = 128
    for i in (3, 0, 2, 1):
        keys = (i + 1) * tok

        def att_step(t, carry, i=i, keys=keys):
            h = t // (tok // sub)
            start = i * tok + lax.rem(t, tok // sub) * sub
            some = pl.ds(pl.multiple_of(start, sub), sub)
            cols = pl.ds(pl.multiple_of(h * HD, HD), HD)
            scores = nt(qkv_ref[some, cols], qkv_ref[0:keys, heads * HD : (heads + 1) * HD]) * HD**-0.5
            same = segc_ref[some, 0:1] == segr_ref[0:1, 0:keys]
            behind = (
                lax.broadcasted_iota(jnp.int32, (sub, keys), 0) + start
                >= lax.broadcasted_iota(jnp.int32, (sub, keys), 1)
            )
            scores = jnp.where(jnp.logical_and(same, behind), scores, NEG_FILL)
            peak = jnp.max(scores, axis=-1, keepdims=True)
            exps = jnp.exp(scores - peak)
            totals = jnp.sum(exps, axis=-1, keepdims=True)
            prob = (exps * (1.0 / totals)).astype(BF16)
            ab[some, cols] = nn(prob, qkv_ref[0:keys, (heads + 1) * HD :]).astype(BF16)
            at_head = lax.broadcasted_iota(jnp.int32, (sub, HD), 1) == h
            lse_ref[some, :] = jnp.where(at_head, peak + jnp.log(totals), lse_ref[some, :])
            return carry

        with jax.named_scope("attention"):
            lax.fori_loop(0, heads * (tok // sub), att_step, 0)

        @pl.when(lane != i)
        def _(i=i):
            att_send(i).start()

    with jax.named_scope("cotangent_1"):
        line_step(1, o_line)
    own_cols = pl.ds(pl.multiple_of(lane * heads * HD, HD), heads * HD)
    att_ref[:, own_cols] = ab[here, :]
    with jax.named_scope("gate_across"):
        gathers[3].relay_across()
    with jax.named_scope("w_out_end"):
        gathers[2].end()
    wo_load = pltpu.make_async_copy(wof, wo, load_sem.at[12])
    wo_load.start()
    wo_load.wait()
    for i in range(LANES):
        @pl.when(lane != i)
        def _(i=i):
            pltpu.make_async_remote_copy(
                ab.at[pl.ds(0, tok)], att_ref.at[:, pl.ds(i * heads * HD, heads * HD)],
                a_send.at[0], a_recv.at[i], device_id={"seq": i}, device_id_type=MESH_ID,
            ).wait_recv()

    def out_tile(t, carry):
        cols = pl.ds(pl.multiple_of(t * 512, 512), 512)
        resid_ref[:, cols] = xb[here, cols].astype(F32) + nt(att_ref[...], wo[cols, :])
        return carry

    with jax.named_scope("out_project"):
        lax.fori_loop(0, width // 512, out_tile, 0)

    def mlp_norm(i, carry):
        some = pl.ds(pl.multiple_of(i * 32, 32), 32)
        x = resid_ref[some, :]
        factor = lax.rsqrt(jnp.mean(x * x, axis=-1, keepdims=True) + EPS)
        mlp_ref[some, :] = (x * factor * vecs_ref[1:2, :]).astype(BF16)
        return carry

    lax.fori_loop(0, tok // 32, mlp_norm, 0)
    with jax.named_scope("cotangent_2"):
        line_step(2, o_line)
    with jax.named_scope("up_down_relay"):
        gathers[4].relay()
        gathers[5].relay()
    with jax.named_scope("cotangent_3"):
        line_step(3, o_line)
    with jax.named_scope("weights_end"):
        gathers[4].relay_across()
        gathers[5].relay_across()
        for which in (3, 4, 5):
            gathers[which].end()
    nrm_copy.wait()
    line_end(i_line, x_line, o_line)
    for i in range(LANES):
        @pl.when(lane != i)
        def _(i=i):
            att_send(i).wait_send()


def front(chips, hidden_in, ids, freqs, out_grad, vec, w_query, w_key, w_value, wo, w_gate, w_up, w_down):
    tok, width = hidden_in.shape
    row = tok * LANES
    qkv_width = w_query.shape[1] // LANES + 2 * HD
    own_qkv = jax.ShapeDtypeStruct((w_query.shape[0], qkv_width), BF16)
    ff = w_gate.shape[1]
    anywhere = pl.BlockSpec(memory_space=pl.ANY)
    vmem = pl.BlockSpec(memory_space=pltpu.VMEM)
    dma = pltpu.SemaphoreType.DMA
    shape = jax.ShapeDtypeStruct
    vmem_outs = [
        shape((tok, width), F32),
        shape((tok, width), BF16),
        shape((16, width), F32),
        shape((row, qkv_width), BF16),
        shape((tok, width), BF16),
        shape((row, HD), F32),
        shape((row, HD), F32),
        shape((row, HD), F32),
        shape((row, HD), F32),
        shape((8, row), F32),
    ]
    hbm_outs = [
        shape((row, width), BF16),
        shape((row, width), BF16),
        shape((2 * chips * 16, HD), BF16),
        shape((width, qkv_width), BF16),
        shape((width, width), BF16),
        shape((width, ff), BF16),
        shape((width, ff), BF16),
        shape((width, ff), BF16),
    ]
    return pl.pallas_call(
        functools.partial(front_kernel, chips),
        out_shape=vmem_outs + hbm_outs,
        in_specs=[anywhere, anywhere, vmem] + [anywhere] * 9,
        out_specs=[vmem] * len(vmem_outs) + [anywhere] * len(hbm_outs),
        scratch_shapes=[
            pltpu.VMEM((row, width), BF16),
            pltpu.VMEM((LANES, 8, tok), jnp.int32),
            pltpu.VMEM((row, width), BF16),
            pltpu.VMEM((width, qkv_width), BF16),
            pltpu.VMEM((width, width), BF16),
            pltpu.VMEM((2 * chips * 16, HD), BF16),
            pltpu.VMEM((row, qkv_width - 2 * HD), BF16),
            *[pltpu.VMEM(part.shape, BF16) for part in (vec, own_qkv, wo, w_gate, w_up, w_down, out_grad)],
            dma((15,)),
            dma((6, chips)),
            dma((6, chips)),
            dma((6, 2 * chips)),
            dma((6, 2)),
            dma((6, 2)),
            dma((2, LANES)),
            dma((LANES,)),
            dma((2, LANES)),
            dma((LANES,)),
            dma((2, LANES)),
            dma((LANES,)),
            dma((LANES,)),
            dma((LANES,)),
        ],
        compiler_params=pltpu.CompilerParams(
            collective_id=1, has_side_effects=True, vmem_limit_bytes=56 * 2**20
        ),
        cost_estimate=pl.CostEstimate(
            flops=10 * row * width * qkv_width, bytes_accessed=12 * width * ff, transcendentals=row * width
        ),
        name="front",
    )(hidden_in, ids, freqs, out_grad, vec, w_query, w_key, w_value, wo, w_gate, w_up, w_down)


def ff_kernel(
    chips,
    x_hbm, og_hbm, wg_hbm, wu_hbm, wd_hbm, wq_hbm, wk_hbm, wv_hbm, resid_hbm, own_og_hbm, wo_hbm, vecs_ref,
    mo_ref, gm_ref, vec_ref, grl_hbm, ga_hbm, gw_hbm, fpair, fland, fmid, wqf, wkf, wvf,
    xb, og, wg, wu, wd, hid, gg, gu, pb, rb, rf,
    load_sem, ag_send, ag_recv, rb_send, rb_recv, rf_send, rf_recv, out_sem,
    dp_send, dp_fwd, dp_recv, half_send, half_recv, own_sem, fp_send, fp_recv, fk_sem, fs_send, fs_recv, fl_sem,
    p1_send, p1_recv, p2_send, p2_recv, a_send, a_recv, late_sem,
):
    lane, dp = lax.axis_index("seq"), lax.axis_index("dp")
    chip, core = dp // 2, lax.rem(dp, 2)
    tok, width = x_hbm.shape
    units = wg_hbm.shape[1]
    tile = 512
    full_tiles = units // tile
    tail = units - full_tiles * tile
    wtile = 384
    has_left, has_right = lane > 0, lane < LANES - 1
    is_end = jnp.logical_or(lane == 0, lane == LANES - 1)
    is_mid = jnp.logical_not(is_end)
    left, right = jnp.maximum(lane - 1, 0), jnp.minimum(lane + 1, LANES - 1)

    loads = [
        pltpu.make_async_copy(src, dst, load_sem.at[k])
        for k, (src, dst) in enumerate(
            ((wg_hbm, wg), (wu_hbm, wu), (wd_hbm, wd), (og_hbm, og))
        )
    ]
    own = pltpu.make_async_copy(x_hbm, xb.at[rows_of(lane, tok)], load_sem.at[4])
    own.start()
    for copy in loads:
        copy.start()

    attn_shards = ((wq_hbm, wqf), (wk_hbm, wkf), (wv_hbm, wvf))
    attn_loads, attn_own, begin = [], [], 0
    for k, (shard, full) in enumerate(attn_shards):
        kept = hid.at[pl.ds(0, shard.shape[0]), pl.ds(begin, shard.shape[1])]
        attn_loads.append(pltpu.make_async_copy(shard, kept, own_sem.at[k]))
        attn_own.append(pltpu.make_async_copy(kept, full.at[rows_of(dp, shard.shape[0])], own_sem.at[k]))
        begin += shard.shape[1]
    resid_load = pltpu.make_async_copy(resid_hbm, mo_ref, late_sem.at[0])
    resid_load.start()
    vec_ref[...] = jnp.zeros_like(vec_ref)
    for copy in attn_loads:
        copy.start()
    meet_all(chips)
    gathers = [
        Gather(
            chips, shard, full, dp_send.at[k], dp_fwd.at[k], dp_recv.at[k], half_send.at[k], half_recv.at[k]
        )
        for k, (shard, full) in enumerate(attn_shards)
    ]
    own.wait()

    def gather_copy(block, way):
        part = xb.at[rows_of(block, tok)]
        return pltpu.make_async_remote_copy(
            part, part, ag_send.at[way, block], ag_recv.at[block],
            device_id={"seq": right if way == 0 else left}, device_id_type=MESH_ID,
        )

    @pl.when(has_right)
    def _():
        gather_copy(lane, 0).start()

    @pl.when(has_left)
    def _():
        gather_copy(lane, 1).start()

    def arrivals(step):
        @pl.when(lane - step >= 0)
        def _():
            block = jnp.maximum(lane - step, 0)
            gather_copy(block, 0).wait_recv()

            @pl.when(has_right)
            def _():
                gather_copy(block, 0).start()

        @pl.when(lane + step < LANES)
        def _():
            block = jnp.minimum(lane + step, LANES - 1)
            gather_copy(block, 1).wait_recv()

            @pl.when(has_left)
            def _():
                gather_copy(block, 1).start()

    def sum_send(part, landing, send, recv, block):
        goes_left = block < lane
        target = jnp.where(goes_left, left, right)
        slot = jnp.where(jnp.logical_and(goes_left, target == block), LANES, block)
        return pltpu.make_async_remote_copy(
            part.at[rows_of(block, tok), pl.ds(0, width)], landing.at[rows_of(slot, tok)],
            send.at[block], recv.at[slot],
            device_id={"seq": target}, device_id_type=MESH_ID,
        )

    def sum_arrived(part, landing, send, recv, slot):
        pltpu.make_async_remote_copy(
            landing.at[rows_of(slot, tok)], landing.at[rows_of(slot, tok)],
            send.at[0], recv.at[slot], device_id={"seq": left}, device_id_type=MESH_ID,
        ).wait_recv()

    def sum_pass(part, landing, send, recv, block):
        @pl.when(is_mid)
        def _():
            sum_arrived(part, landing, send, recv, block)

            def add(i, carry):
                mine = pl.ds(pl.multiple_of(block * tok + i * 32, 32), 32)
                total = part[mine, :width].astype(F32) + landing[mine, :].astype(F32)
                part[mine, :width] = total.astype(BF16)
                return carry

            lax.fori_loop(0, tok // 32, add, 0)
            sum_send(part, landing, send, recv, block).start()

    def sum_last(part, landing, send, recv, out, onto=False):
        def begin(i, carry):
            here = pl.ds(pl.multiple_of(i * 32, 32), 32)
            mine = pl.ds(pl.multiple_of(lane * tok + i * 32, 32), 32)
            own_part = part[mine, :width].astype(F32)
            out[here, :] = out[here, :] + own_part if onto else own_part
            return carry

        lax.fori_loop(0, tok // 32, begin, 0)

        def take(slot):
            sum_arrived(part, landing, send, recv, slot)

            def add(i, carry):
                here = pl.ds(pl.multiple_of(i * 32, 32), 32)
                there = pl.ds(pl.multiple_of(slot * tok + i * 32, 32), 32)
                out[here, :] = out[here, :] + landing[there, :].astype(F32)
                return carry

            lax.fori_loop(0, tok // 32, add, 0)

        @pl.when(has_left)
        def _():
            take(lane)

        @pl.when(has_right)
        def _():
            take(jnp.int32(LANES))

    back = (pb, rb, rb_send, rb_recv)
    ahead = (og, rf, rf_send, rf_recv)
    for gather in gathers:
        gather.begin()
    for load, copy in zip(attn_loads, attn_own):
        load.wait()
        copy.start()
    with jax.named_scope("weights_load"):
        for copy in loads + attn_own:
            copy.wait()

    def block_step(step, carry):
        block = order_of(step, lane)
        mine = rows_of(block, tok)

        def act(cols):
            gate = nn(xb[mine, :], wg[:, cols])
            up = nn(xb[mine, :], wu[:, cols])
            grad = nn(og[mine, :], wd[:, cols])
            sig = jax.nn.sigmoid(gate)
            silu = gate * sig
            hid[mine, cols] = (silu * up).astype(BF16)
            gg[mine, cols] = (grad * up * sig * (1.0 + gate * (1.0 - sig))).astype(BF16)
            gu[mine, cols] = (grad * silu).astype(BF16)

        def act_tile(t, c):
            act(pl.ds(pl.multiple_of(t * tile, tile), tile))
            return c

        with jax.named_scope("activations"):
            lax.fori_loop(0, full_tiles, act_tile, 0)
            if tail:
                act(pl.ds(full_tiles * tile, tail))

        @pl.when(step < LANES - 1)
        def _():
            with jax.named_scope("row_arrival"):
                arrivals(step + 1)

        @pl.when(step == 1)
        def _():
            with jax.named_scope("attn_relay"):
                for gather in gathers:
                    gather.relay()

        @pl.when(step == 2)
        def _():
            with jax.named_scope("attn_across"):
                for gather in gathers:
                    gather.relay_across()

        def back_tile(t, c):
            cols = pl.ds(pl.multiple_of(t * tile, tile), tile)
            pb[mine, cols] = (nt(gg[mine, :], wg[cols, :]) + nt(gu[mine, :], wu[cols, :])).astype(BF16)
            return c

        with jax.named_scope("input_grad_part"):
            lax.fori_loop(0, width // tile, back_tile, 0)

        @pl.when(jnp.logical_and(is_end, step > 0))
        def _():
            sum_send(*back, block).start()

        return carry

    lax.fori_loop(0, LANES, block_step, 0)

    def down_step(step, carry):
        block = order_of(LANES - 1 - step, lane)
        mine = rows_of(block, tok)

        def down_tile(t, c):
            cols = pl.ds(pl.multiple_of(t * tile, tile), tile)
            og[mine, cols] = nt(hid[mine, :], wd[cols, :]).astype(BF16)
            return c

        with jax.named_scope("down_part"):
            lax.fori_loop(0, width // tile, down_tile, 0)

        @pl.when(jnp.logical_and(is_end, step < LANES - 1))
        def _():
            sum_send(*ahead, block).start()

        return carry

    wtiles = width // wtile
    part_rows = width // (2 * chips)
    tile_chips = wtile // (2 * part_rows)

    square = chips == 4
    half = part_rows // 2

    def tile_at(step):
        base, mask = chip // (chips // wtiles), wtiles - 1 - step
        return lax.rem(base + mask, 2) + 2 * lax.rem(base // 2 + mask // 2, 2)

    def held(which, c):
        return rows_of(which * chips + c, part_rows)

    def pair_send(which, c, r):
        theirs = pl.ds(pl.multiple_of(which * wtile + (2 * r + 1 - core) * part_rows, 16), part_rows)
        return pltpu.make_async_remote_copy(
            wu.at[theirs], fpair.at[which, c], fp_send.at[which, c], fp_recv.at[which, c],
            device_id={"dp": 2 * chip + 1 - core}, device_id_type=MESH_ID,
        )

    def pair_keep(which, c, r):
        mine = pl.ds(pl.multiple_of(which * wtile + (2 * r + core) * part_rows, 16), part_rows)
        return pltpu.make_async_copy(wu.at[mine], wg.at[held(which, c)], fk_sem.at[which, c])

    def to_chip(src, dst, send, recv, mask):
        return pltpu.make_async_remote_copy(
            src, dst, send, recv, device_id={"dp": 2 * flipped(chip, mask) + core}, device_id_type=MESH_ID
        )

    def chip_keep(which):
        return pltpu.make_async_copy(
            wg.at[held(which, chip)], fland.at[which, 0], fl_sem.at[which]
        )

    def chip_send(which, mask):
        return to_chip(
            wg.at[held(which, flipped(chip, mask))], fland.at[which, mask], fs_send.at[which, mask],
            fs_recv.at[which, mask], mask,
        )

    def part_of(which, mask, upper):
        return wg.at[pl.ds(pl.multiple_of((which * chips + flipped(chip, mask)) * part_rows + upper * half, 16), half)]

    def first_hop(which, mask, upper):
        if mask == 3:
            landing = fmid.at[which, upper]
        else:
            landing = fland.at[which, 1, pl.ds(upper * half, half)]
        k = 2 * (mask == 3) + upper
        return to_chip(part_of(which, mask, upper), landing, p1_send.at[which, k], p1_recv.at[which, k], 1 + upper)

    def second_hop(which, upper):
        mask = 2 - upper
        return to_chip(
            part_of(which, mask, upper), fland.at[which, 2, pl.ds(upper * half, half)],
            p2_send.at[which, upper], p2_recv.at[which, upper], mask,
        )

    def load_slot(which):
        return wu.at[pl.ds(3 * wtile + which * part_rows, part_rows)]

    def add_in(which, first, rows):
        def add(i, carry):
            mine = pl.ds(pl.multiple_of(first + i * 16, 16), 16)
            other = pl.ds(pl.multiple_of(3 * wtile + which * part_rows + i * 16, 16), 16)
            wg[mine, :] = (wg[mine, :].astype(F32) + wu[other, :].astype(F32)).astype(BF16)
            return carry

        lax.fori_loop(0, rows // 16, add, 0)

    def pass_halves(upper):
        arrived = []
        for which in range(2):
            first_hop(which, 3, upper).wait_recv()
            arrived.append(
                pltpu.make_async_copy(
                    fmid.at[which, upper], wu.at[pl.ds(3 * wtile + which * part_rows, half)], load_sem.at[which]
                )
            )
            arrived[which].start()
        for which in range(2):
            arrived[which].wait()
            c = flipped(chip, 2 - upper)
            add_in(which, (which * chips + c) * part_rows + upper * half, half)
            second_hop(which, upper).start()

    def add_pairs(step):
        k = tile_at(step)
        for r in range(tile_chips):
            c = k * tile_chips + r
            arrived = []
            for which in range(2):
                pair_keep(which, c, r).wait()
                pair_send(which, c, r).wait_recv()
                arrived.append(pltpu.make_async_copy(fpair.at[which, c], load_slot(which), load_sem.at[which]))
                arrived[which].start()
            for which in range(2):
                arrived[which].wait()
                add_in(which, (which * chips + c) * part_rows, part_rows)
                if not square:
                    continue
                if step == 0:
                    first_hop(which, 3, 0).start()
                    first_hop(which, 3, 1).start()
                elif step == 1:
                    first_hop(which, 2, 1).start()
                elif step == 2:
                    first_hop(which, 1, 0).start()
                else:
                    chip_keep(which).start()

    def product(stage_ref, stage, lhs, rhs):
        def tile_of(cols):
            stage_ref[stage, cols] = nn(wu[lhs], rhs[:, cols]).astype(BF16)

        def one(t, c):
            tile_of(pl.ds(pl.multiple_of(t * tile, tile), tile))
            return c

        lax.fori_loop(0, full_tiles, one, 0)
        if tail:
            tile_of(pl.ds(full_tiles * tile, tail))

    turned = (pl.ds(2 * wtile, wtile), pl.ds(0, LANES * tok))

    def grad_tile(step):
        k = tile_at(step)
        if step:
            for which in range(2):
                for r in range(tile_chips):
                    before = tile_at(step - 1) * tile_chips + r
                    pair_send(which, before, r).wait_send()
        wu[turned] = xb[:, rows_of(k, wtile)].T
        for which, rhs in enumerate((gg, gu)):
            product(wu, pl.ds(which * wtile, wtile), turned, rhs)
            for r in range(tile_chips):
                pair_send(which, k * tile_chips + r, r).start()
                pair_keep(which, k * tile_chips + r, r).start()

    def down_grad_out(step):
        stage = rows_of(lax.rem(step, 2), wtile)
        return pltpu.make_async_copy(
            gg.at[stage], gw_hbm.at[0, rows_of(step, wtile)], out_sem.at[lax.rem(step, 2)]
        )

    def down_grad_tile(step, carry):
        @pl.when(step > 1)
        def _():
            down_grad_out(step - 2).wait()

        wu[turned] = xb[:, rows_of(step, wtile)].T
        product(gg, rows_of(lax.rem(step, 2), wtile), turned, hid)
        down_grad_out(step).start()
        return carry

    mid_near, mid_far, mid_back = 3 - lane, 6 - 3 * lane, 3 * lane - 3
    sum_pass(*back, mid_near)
    grad_tile(0)
    lax.fori_loop(0, 1, down_step, 0)
    add_pairs(0)
    lax.fori_loop(1, LANES, down_step, 0)
    wo = wd.at[:, pl.ds(0, width)]
    wo_load = pltpu.make_async_copy(wo_hbm, wo, late_sem.at[1])
    wo_load.start()
    sum_pass(*back, mid_far)
    grad_tile(1)
    add_pairs(1)
    sum_pass(*ahead, mid_far)
    grad_tile(2)
    add_pairs(2)
    sum_pass(*back, mid_back)
    grad_tile(3)
    for block in range(LANES):
        @pl.when(jnp.logical_and(has_right, block <= lane))
        def _(block=block):
            gather_copy(block, 0).wait_send()

        @pl.when(jnp.logical_and(has_left, block >= lane))
        def _(block=block):
            gather_copy(block, 1).wait_send()

    again = pltpu.make_async_copy(og_hbm, xb, load_sem.at[3])
    again.start()
    add_pairs(3)
    sum_pass(*ahead, mid_near)
    sum_pass(*ahead, mid_back)
    if square:
        pass_halves(0)
        pass_halves(1)
    else:
        for which in range(2):
            chip_keep(which).start()
            for mask in range(1, chips):
                chip_send(which, mask).start()
    sum_last(*back, gm_ref)
    for block in range(LANES):
        @pl.when(block != lane)
        def _(block=block):
            sum_send(*back, block).wait_send()

    own_og, grl, gao = (pb.at[pl.ds(k * tok, tok)] for k in range(3))
    og_load = pltpu.make_async_copy(own_og_hbm, own_og, late_sem.at[2])
    og_load.start()
    og_load.wait()
    resid_load.wait()

    def resid_rows(i, carry):
        some = pl.ds(pl.multiple_of(i * 32, 32), 32)
        values = mo_ref[some, :]
        grad_in = gm_ref[some, :]
        factor = lax.rsqrt(jnp.mean(values * values, axis=-1, keepdims=True) + EPS)
        scaled = grad_in * vecs_ref[1:2, :]
        inner = jnp.mean(scaled * values, axis=-1, keepdims=True)
        grad = own_og[some, :].astype(F32) + (factor * scaled - values * (factor * factor * factor) * inner)
        gm_ref[some, :] = grad
        grl[some, :] = grad.astype(BF16)
        vec_ref[1:2, :] = vec_ref[1:2, :] + jnp.sum(grad_in * values * factor, axis=0, keepdims=True)
        return carry

    lax.fori_loop(0, tok // 32, resid_rows, 0)
    grl_out = pltpu.make_async_copy(grl, grl_hbm, late_sem.at[2])
    grl_out.start()
    wo_load.wait()
    hw = width // LANES

    def head_cols(which):
        return pl.ds(pl.multiple_of(which * hw, hw), hw)

    def a_copy(target):
        return pltpu.make_async_remote_copy(
            gao.at[:, head_cols(target)], ga_hbm.at[rows_of(lane, tok)], a_send.at[target], a_recv.at[lane],
            device_id={"seq": target}, device_id_type=MESH_ID,
        )

    for step in range(1, LANES + 1):
        target = lax.rem(lane + step, LANES)
        gao[:, head_cols(target)] = nn(grl[...], wo[:, head_cols(target)]).astype(BF16)
        if step < LANES:
            a_copy(target).start()
    ga_own = pltpu.make_async_copy(gao.at[:, head_cols(lane)], ga_hbm.at[rows_of(lane, tok)], late_sem.at[1])
    ga_own.start()
    again.wait()
    lax.fori_loop(0, wtiles, down_grad_tile, 0)
    sum_last(*ahead, mo_ref, True)
    grl_out.wait()
    ga_own.wait()
    for step in range(1, LANES):
        other = lax.rem(lane + step, LANES)
        a_copy(other).wait_send()
        pltpu.make_async_remote_copy(
            gao.at[:, head_cols(other)], ga_hbm.at[rows_of(other, tok)], a_send.at[0], a_recv.at[other],
            device_id={"seq": other}, device_id_type=MESH_ID,
        ).wait_recv()
    for gather in gathers:
        gather.end()
    down_grad_out(wtiles - 2).wait()
    down_grad_out(wtiles - 1).wait()
    for which in range(2):
        for r in range(tile_chips):
            last = tile_at(wtiles - 1) * tile_chips + r
            pair_send(which, last, r).wait_send()
        chip_keep(which).wait()
        if square:
            for mask, upper in ((3, 0), (3, 1), (2, 1), (1, 0)):
                first_hop(which, mask, upper).wait_send()
                if mask != 3:
                    first_hop(which, mask, upper).wait_recv()
            for upper in range(2):
                second_hop(which, upper).wait()
        else:
            for mask in range(1, chips):
                chip_send(which, mask).wait()

    for block in range(LANES):
        @pl.when(block != lane)
        def _(block=block):
            sum_send(*ahead, block).wait_send()


def feed_forward(
    chips, mlp_local, grad_rows, gate_full, up_full, down_full, w_query, w_key, w_value, resid, out_grad, wo_full, vecs
):
    tok, width = mlp_local.shape
    units = gate_full.shape[1]
    row = tok * LANES
    own = width // (2 * chips)
    anywhere = pl.BlockSpec(memory_space=pl.ANY)
    vmem = pl.BlockSpec(memory_space=pltpu.VMEM)
    dma = pltpu.SemaphoreType.DMA
    shape = jax.ShapeDtypeStruct
    return pl.pallas_call(
        functools.partial(ff_kernel, chips),
        out_shape=(
            shape((tok, width), F32),
            shape((tok, width), F32),
            shape((8, width), F32),
            shape((tok, width), BF16),
            shape((row, width // LANES), BF16),
            shape((1, width, units), BF16),
            shape((2, chips, own, units), BF16),
            shape((2, 3 if chips == 4 else chips, own, units), BF16),
            shape((2, 2, own // 2, units), BF16),
            shape((width, w_query.shape[1]), BF16),
            shape((width, w_key.shape[1]), BF16),
            shape((width, w_value.shape[1]), BF16),
        ),
        in_specs=[anywhere] * 11 + [vmem],
        out_specs=(vmem, vmem, vmem) + (anywhere,) * 9,
        scratch_shapes=[
            pltpu.VMEM((row, width), BF16),
            pltpu.VMEM((row, width), BF16),
            pltpu.VMEM((width, units), BF16),
            pltpu.VMEM((width, units), BF16),
            pltpu.VMEM((width, units), BF16),
            pltpu.VMEM((row, units), BF16),
            pltpu.VMEM((row, units), BF16),
            pltpu.VMEM((row, units), BF16),
            pltpu.VMEM((row, width), BF16),
            pltpu.VMEM((row + tok, width), BF16),
            pltpu.VMEM((row + tok, width), BF16),
            dma((5,)),
            dma((2, LANES)),
            dma((LANES,)),
            dma((LANES,)),
            dma((LANES + 1,)),
            dma((LANES,)),
            dma((LANES + 1,)),
            dma((2,)),
            dma((3, chips)),
            dma((3, chips)),
            dma((3, 2 * chips)),
            dma((3, 2)),
            dma((3, 2)),
            dma((3,)),
            *[dma((2, chips))] * 5,
            dma((2,)),
            dma((2, 4)),
            dma((2, 4)),
            dma((2, 2)),
            dma((2, 2)),
            dma((LANES,)),
            dma((LANES,)),
            dma((3,)),
        ],
        compiler_params=pltpu.CompilerParams(
            collective_id=3, has_side_effects=True, vmem_limit_bytes=60 * 2**20
        ),
        cost_estimate=pl.CostEstimate(
            flops=18 * row * width * units, bytes_accessed=12 * width * units, transcendentals=row * units
        ),
        name="feed_forward",
    )(
        mlp_local, grad_rows, gate_full, up_full, down_full, w_query, w_key, w_value, resid, out_grad, wo_full, vecs
    )


def chunked(rows, body, size=32):
    lax.fori_loop(0, rows // size, lambda i, c: (body(pl.multiple_of(i * size, size)), c)[1], 0)


def tn(left, right):
    return lax.dot_general(left, right, (((0,), (0,)), ((), ())), preferred_element_type=F32)


def back_kernel(
    chips, mats,
    gr_ref, mlp_vec_ref, x_ref, vecs_ref, qkv_ref, lse_ref, cos_ref, sin_ref, segc_ref, segr_ref,
    grl_hbm, ga_hbm, att_hbm, wq_hbm, wk_hbm, wv_hbm, nrm_hbm, gw_hbm,
    ig_ref, vec_ref, woz_ref, wqz_ref, fpair, fsum, fland,
    att, wfull, nrm, grl, ga, gk, gv, g, gl, lt,
    wop, wopair, woland, wores, zin, zsum,
    wqp, wqpair, wqland, slots, vz, vd, gn,
    load_sem, g_send, g_recv, h_send, h_recv,
    po_send, po_recv, so_send, so_recv, pq_send, pq_recv, sq_send, sq_recv,
    zr_send, zr_recv, zg_send, zg_recv, zq_send, zq_recv,
    fp_send, fp_recv, fs_send, fs_recv, slot_sem, v_send, v_recv, vs_send, vs_recv,
):
    dp, lane = lax.axis_index("dp"), lax.axis_index("seq")
    chip, core = dp // 2, lax.rem(dp, 2)
    sibling = 2 * chip + 1 - core
    tok, width = x_ref.shape
    row = tok * LANES
    part_rows = width // (2 * chips)
    heads = qkv_ref.shape[1] // HD - 2
    hw = heads * HD
    gwid = hw + 2 * HD
    here = rows_of(lane, tok)

    def lane_cols(which, size):
        return pl.ds(pl.multiple_of(which * size, size), size)

    loads = [
        pltpu.make_async_copy(src, dst, load_sem.at[k])
        for k, (src, dst) in enumerate(
            (
                (grl_hbm, grl),
                (att_hbm, att),
                (ga_hbm, ga),
                (nrm_hbm, nrm),
                (wq_hbm, wfull.at[:, pl.ds(0, LANES * hw)]),
                (wk_hbm, wfull.at[:, pl.ds(LANES * hw, KV_HEADS * HD)]),
                (wv_hbm, wfull.at[:, pl.ds(LANES * hw + KV_HEADS * HD, KV_HEADS * HD)]),
            )
        )
    ]
    for copy in loads:
        copy.start()
    vec_ref[...] = mlp_vec_ref[...]
    meet_all(chips)

    def to_dp(src, dst, send, recv, target):
        return pltpu.make_async_remote_copy(
            src, dst, send, recv, device_id={"dp": target}, device_id_type=MESH_ID
        )

    def to_lane(src, dst, send, recv, target):
        return pltpu.make_async_remote_copy(
            src, dst, send, recv, device_id={"seq": target}, device_id_type=MESH_ID
        )

    def ff_pair(k, c):
        return to_dp(
            gw_hbm.at[mats[k], rows_of(2 * c + 1 - core, part_rows)], fpair.at[k, c],
            fp_send.at[k, c], fp_recv.at[k, c], sibling,
        )

    def ff_send(k, mask):
        c = flipped(chip, mask)
        return to_dp(
            fsum.at[k, c], fland.at[k, chip], fs_send.at[k, c], fs_recv.at[k, chip], 2 * c + core
        )

    for k in range(len(mats)):
        for mask in range(chips):
            ff_pair(k, flipped(chip, mask)).start()

    def ff_loads(k, mask):
        c = flipped(chip, mask)
        return [
            pltpu.make_async_copy(
                gw_hbm.at[mats[k], rows_of(2 * c + core, part_rows)], slots.at[0], slot_sem.at[0]
            ),
            pltpu.make_async_copy(fpair.at[k, c], slots.at[1], slot_sem.at[1]),
        ]

    def ff_load(k, mask):
        ff_pair(k, flipped(chip, mask)).wait_recv()
        for copy in ff_loads(k, mask):
            copy.start()

    def ff_add(k, mask):
        for copy in ff_loads(k, mask):
            copy.wait()

        def add(start):
            some = pl.ds(start, 16)
            slots[0, some, :] = (slots[0, some, :].astype(F32) + slots[1, some, :].astype(F32)).astype(BF16)

        chunked(part_rows, add, 16)
        out = pltpu.make_async_copy(
            slots.at[0], fsum.at[k, flipped(chip, mask)] if mask else fland.at[k, chip], slot_sem.at[2]
        )
        out.start()
        out.wait()
        if mask:
            ff_send(k, mask).start()

    loads[0].wait()
    loads[1].wait()

    def out_grad_tile(i, carry):
        some = lane_cols(i, 384)
        for n in range(width // 512):
            cols = slice(n * 512, (n + 1) * 512)
            wop[some, cols] = tn(grl[:, some], att[:, cols]).astype(BF16)
        return carry

    lax.fori_loop(0, width // 384, out_grad_tile, 0)

    class Sum:
        def __init__(self, partial, pair, land, pair_send, pair_recv, send, recv):
            self.partial, self.pair, self.land = partial, pair, land
            self.pair_send, self.pair_recv, self.send, self.recv = pair_send, pair_recv, send, recv

        def pair_copy(self, c):
            return to_dp(
                self.partial.at[rows_of(2 * c + 1 - core, part_rows)], self.pair.at[rows_of(c, part_rows)],
                self.pair_send.at[c], self.pair_recv.at[c], sibling,
            )

        def send_copy(self, mask):
            c = flipped(chip, mask)
            return to_dp(
                self.partial.at[rows_of(2 * c + core, part_rows)], self.land.at[rows_of(chip, part_rows)],
                self.send.at[c], self.recv.at[chip], 2 * c + core,
            )

        def begin(self):
            for mask in range(chips):
                self.pair_copy(flipped(chip, mask)).start()

        def middle(self):
            for mask in list(range(1, chips)) + [0]:
                c = flipped(chip, mask)
                self.pair_copy(c).wait_recv()

                def add(start, c=c):
                    mine = pl.ds(pl.multiple_of((2 * c + core) * part_rows + start, 16), 16)
                    other = pl.ds(pl.multiple_of(c * part_rows + start, 16), 16)
                    self.partial[mine, :] = (
                        self.partial[mine, :].astype(F32) + self.pair[other, :].astype(F32)
                    ).astype(BF16)

                chunked(part_rows, add, 16)
                if mask:
                    self.send_copy(mask).start()

        def last(self, out):
            for mask in range(1, chips):
                c = flipped(chip, mask)
                to_dp(
                    self.land.at[rows_of(c, part_rows)], self.land.at[rows_of(c, part_rows)],
                    self.send.at[0], self.recv.at[c], sibling,
                ).wait_recv()

            def add(start):
                some = pl.ds(start, 16)
                total = self.partial[pl.ds(pl.multiple_of(dp * part_rows + start, 16), 16), :].astype(F32)
                for mask in range(1, chips):
                    c = flipped(chip, mask)
                    total = total + self.land[
                        pl.ds(pl.multiple_of(c * part_rows + start, 16), 16), :
                    ].astype(F32)
                out(some, total.astype(BF16))

            chunked(part_rows, add, 16)

        def end(self):
            for mask in range(chips):
                self.pair_copy(flipped(chip, mask)).wait_send()
                if mask:
                    self.send_copy(mask).wait_send()

    out_sum = Sum(wop, wopair, woland, po_send, po_recv, so_send, so_recv)
    qkv_sum = Sum(wqp, wqpair, wqland, pq_send, pq_recv, sq_send, sq_recv)
    out_sum.begin()

    def turn(i, carry):
        some = rows_of(i, tok)
        turned = lse_ref[some, :].T
        for h in range(heads):
            lt[h, :, some] = jnp.broadcast_to(turned[h : h + 1, :], (8, tok))
        return carry

    lax.fori_loop(0, LANES, turn, 0)
    gk[...] = jnp.zeros_like(gk)
    gv[...] = jnp.zeros_like(gv)
    out_sum.middle()
    ff_turns = [(k, mask) for k in range(len(mats)) for mask in list(range(chips - 1, 0, -1)) + [0]]
    loads[2].wait()

    def out_store(some, value):
        wores[some, :] = value

    quarter = width // LANES

    def zr_copy(target):
        return to_lane(
            wores.at[:, lane_cols(target, quarter)], zin.at[lane], zr_send.at[target], zr_recv.at[lane], target
        )

    def own_out():
        out_sum.last(out_store)
        for step in range(1, LANES):
            zr_copy(lax.rem(lane + step, LANES)).start()
        zin[lane] = wores[:, lane_cols(lane, quarter)]

    def gq_copy(target):
        return to_lane(
            g.at[rows_of(target, tok), pl.ds(0, hw)],
            gl.at[:, pl.ds(pl.multiple_of(lane * gwid, HD), hw)],
            g_send.at[target], g_recv.at[lane], target,
        )

    def gkv_copy(target):
        return to_lane(
            g.at[rows_of(target, tok), pl.ds(hw, 2 * HD)],
            gl.at[:, pl.ds(pl.multiple_of(lane * gwid + hw, HD), 2 * HD)],
            h_send.at[target], h_recv.at[lane], target,
        )

    sub = 128
    scale = HD**-0.5
    for i in (3, 0, 2, 1):
        keys = (i + 1) * tok

        def att_step(t, carry, i=i, keys=keys):
            h = t // (tok // sub)
            start = i * tok + lax.rem(t, tok // sub) * sub
            some = pl.ds(pl.multiple_of(start, sub), sub)
            cols = lane_cols(h, HD)
            key, value = qkv_ref[0:keys, hw : hw + HD], qkv_ref[0:keys, hw + HD :]
            query, grad = qkv_ref[some, cols], ga[some, cols]
            scores = nt(key, query) * scale
            same = segc_ref[0:keys, 0:1] == segr_ref[0:1, some]
            behind = (
                lax.broadcasted_iota(jnp.int32, (keys, sub), 1) + start
                >= lax.broadcasted_iota(jnp.int32, (keys, sub), 0)
            )
            scores = jnp.where(jnp.logical_and(same, behind), scores, NEG_FILL)
            prob = jnp.exp(scores - lt[h, 0:1, some])
            grad_prob = nt(value, grad)
            inner = jnp.sum(prob * grad_prob, axis=0, keepdims=True)
            grad_scores = (prob * (grad_prob - inner)).astype(BF16)
            gq = (tn(grad_scores, key) * scale).astype(BF16).astype(F32)
            gk[0:keys, :] = gk[0:keys, :] + nn(grad_scores, query)
            gv[0:keys, :] = gv[0:keys, :] + nn(prob.astype(BF16), grad)
            g[some, cols] = (
                gq * cos_ref[some, :] + pltpu.roll(gq * sin_ref[some, :], HD // 2, 1)
            ).astype(BF16)
            return carry

        lax.fori_loop(0, heads * (tok // sub), att_step, 0)

        @pl.when(lane != i)
        def _(i=i):
            gq_copy(jnp.int32(i)).start()

    def close(start):
        some = pl.ds(start, 32)
        grad = (gk[some, :] * scale).astype(BF16).astype(F32)
        g[some, hw : hw + HD] = (
            grad * cos_ref[some, :] + pltpu.roll(grad * sin_ref[some, :], HD // 2, 1)
        ).astype(BF16)
        g[some, hw + HD :] = gv[some, :].astype(BF16)

    chunked(row, close)

    for step in range(1, LANES):
        gkv_copy(lax.rem(lane + step, LANES)).start()
    gl[:, lane_cols(lane, gwid)] = g[here, :]
    loads[3].wait()

    def qkv_grad_tile(i, carry):
        some = lane_cols(i, 384)
        wqp[some, :] = tn(nrm[:, some], g[...]).astype(BF16)
        return carry

    lax.fori_loop(0, width // 384, qkv_grad_tile, 0)
    qkv_sum.begin()
    sums = jnp.zeros((1, gwid), F32)
    for i in range(row // 128):
        sums = sums + jnp.sum(g[i * 128 : (i + 1) * 128, :].astype(F32), axis=0, keepdims=True)
    kv_head = lane * KV_HEADS // LANES
    vec_ref[2:3, lane_cols(lane, hw)] = sums[:, :hw]
    vec_ref[3:4, lane_cols(kv_head, HD)] = sums[:, hw : hw + HD]
    vec_ref[4:5, lane_cols(kv_head, HD)] = sums[:, hw + HD :]

    def qkv_store(some, value):
        wqz_ref[lane, some, :] = value

    def zq_copy(target):
        return to_lane(
            wqz_ref.at[lane], wqz_ref.at[lane], zq_send.at[target], zq_recv.at[lane], target
        )

    own_out()
    qkv_sum.middle()
    for turn in ff_turns:
        ff_load(*turn)
        ff_add(*turn)
    qkv_sum.last(qkv_store)
    for step in range(1, LANES):
        zq_copy(lax.rem(lane + step, LANES)).start()
    for step in range(1, LANES):
        source = lax.rem(lane + step, LANES)
        to_lane(zin.at[source], zin.at[source], zr_send.at[0], zr_recv.at[source], source).wait_recv()
    total = zin[0].astype(F32)
    for j in range(1, LANES):
        total = total + zin[j].astype(F32)
    zsum[...] = total.astype(BF16)
    woz_ref[:, lane_cols(lane, quarter)] = zsum[...]

    def zg_copy(target):
        return to_lane(
            zsum, woz_ref.at[:, lane_cols(lane, quarter)], zg_send.at[target], zg_recv.at[lane], target
        )

    for step in range(1, LANES):
        zg_copy(lax.rem(lane + step, LANES)).start()

    for copy in loads[4:]:
        copy.wait()
    for step in range(1, LANES):
        source = lax.rem(lane + step, LANES)
        for begin, size, recv in ((0, hw, g_recv), (hw, 2 * HD, h_recv)):
            to_lane(
                g.at[here, pl.ds(begin, size)], gl.at[:, pl.ds(pl.multiple_of(source * gwid + begin, HD), size)],
                g_send.at[0], recv.at[source], source,
            ).wait_recv()
    group = LANES // KV_HEADS

    def kv_total(kv, offset):
        parts = [
            gl[:, (kv * group + j) * gwid + offset : (kv * group + j) * gwid + offset + HD].astype(F32)
            for j in range(group)
        ]
        return sum(parts[1:], parts[0]).astype(BF16)

    kv_grads = [kv_total(kv, hw + offset) for offset in (0, HD) for kv in range(KV_HEADS)]
    kv_grads = jnp.concatenate(kv_grads, axis=1)

    def normed_tile(i, carry):
        some = lane_cols(i, 512)
        total = nt(kv_grads, wfull[some, LANES * hw :])
        for j in range(LANES):
            total = total + nt(gl[:, j * gwid : j * gwid + hw], wfull[some, j * hw : (j + 1) * hw])
        gn[:, some] = total
        return carry

    lax.fori_loop(0, width // 512, normed_tile, 0)

    def input_rows(start):
        some = pl.ds(start, 32)
        values = x_ref[some, :].astype(F32)
        grad_in = gn[some, :]
        factor = lax.rsqrt(jnp.mean(values * values, axis=-1, keepdims=True) + EPS)
        scaled = grad_in * vecs_ref[0:1, :]
        inner = jnp.mean(scaled * values, axis=-1, keepdims=True)
        ig_ref[some, :] = gr_ref[some, :] + (
            factor * scaled - values * (factor * factor * factor) * inner
        )
        vec_ref[0:1, :] = vec_ref[0:1, :] + jnp.sum(grad_in * values * factor, axis=0, keepdims=True)

    chunked(tok, input_rows)

    def v_copy(target):
        return to_lane(vec_ref, vz.at[lane], v_send.at[target], v_recv.at[lane], target)

    for step in range(1, LANES):
        v_copy(lax.rem(lane + step, LANES)).start()

    for step in range(1, LANES):
        source = lax.rem(lane + step, LANES)
        to_lane(vz.at[source], vz.at[source], v_send.at[0], v_recv.at[source], source).wait_recv()
    for step in range(1, LANES):
        v_copy(lax.rem(lane + step, LANES)).wait_send()
    total = vec_ref[...]
    for step in range(1, LANES):
        total = total + vz[lax.rem(lane + step, LANES)]
    vd[chips] = total
    swap = to_dp(vd.at[chips], vd.at[chips + 1], vs_send.at[0], vs_recv.at[chips], sibling)
    swap.start()
    swap.wait()
    vd[chip] = vd[chips] + vd[chips + 1]

    def vs_copy(mask):
        return to_dp(
            vd.at[chip], vd.at[chip], vs_send.at[mask], vs_recv.at[chip], 2 * flipped(chip, mask) + core
        )

    for mask in range(1, chips):
        vs_copy(mask).start()
    for mask in range(1, chips):
        c = flipped(chip, mask)
        to_dp(vd.at[c], vd.at[c], vs_send.at[0], vs_recv.at[c], sibling).wait_recv()
    for mask in range(1, chips):
        vs_copy(mask).wait_send()
    total = vd[0]
    for c in range(1, chips):
        total = total + vd[c]
    vec_ref[...] = total

    for step in range(1, LANES):
        other = lax.rem(lane + step, LANES)
        to_lane(zsum, woz_ref.at[:, lane_cols(other, quarter)], zg_send.at[0], zg_recv.at[other], other).wait_recv()
        to_lane(wqz_ref.at[other], wqz_ref.at[other], zq_send.at[0], zq_recv.at[other], other).wait_recv()
        gq_copy(other).wait_send()
        gkv_copy(other).wait_send()
        zr_copy(other).wait_send()
        zg_copy(other).wait_send()
        zq_copy(other).wait_send()
    out_sum.end()
    qkv_sum.end()
    for k in range(len(mats)):
        for mask in range(chips):
            c = flipped(chip, mask)
            ff_pair(k, c).wait_send()
            if mask:
                to_dp(fland.at[k, c], fland.at[k, c], fs_send.at[k, 0], fs_recv.at[k, c], sibling).wait_recv()
                ff_send(k, mask).wait_send()


def back(
    chips, mats, grad_resid, mlp_vec, hidden_in, vecs, qkv, log_sum, cos_row, sin_row, seg_col,
    seg_row, grad_low, grad_att, attended, wq_full, wk_full, wv_full, normed_row, mlp_grads,
):
    tok, width = hidden_in.shape
    row = tok * LANES
    gwid = qkv.shape[1]
    hw = gwid - 2 * HD
    ff = mlp_grads.shape[2]
    own = width // (2 * chips)
    half = width // 2
    anywhere = pl.BlockSpec(memory_space=pl.ANY)
    vmem = pl.BlockSpec(memory_space=pltpu.VMEM)
    dma = pltpu.SemaphoreType.DMA
    shape = jax.ShapeDtypeStruct
    vmem_outs = [
        shape((tok, width), F32),
        shape((8, width), F32),
        shape((own, width), BF16),
        shape((LANES, own, gwid), BF16),
    ]
    hbm_outs = [shape((len(mats), chips, own, ff), BF16)] * 3
    return pl.pallas_call(
        functools.partial(back_kernel, chips, mats),
        out_shape=vmem_outs + hbm_outs,
        in_specs=[vmem] * 10 + [anywhere] * 8,
        out_specs=[vmem] * len(vmem_outs) + [anywhere] * len(hbm_outs),
        scratch_shapes=[
            pltpu.VMEM((tok, width), BF16),
            pltpu.VMEM((width, width + 2 * KV_HEADS * HD), BF16),
            pltpu.VMEM((row, width), BF16),
            pltpu.VMEM((tok, width), BF16),
            pltpu.VMEM((row, hw), BF16),
            pltpu.VMEM((row, HD), F32),
            pltpu.VMEM((row, HD), F32),
            pltpu.VMEM((row, gwid), BF16),
            pltpu.VMEM((tok, LANES * gwid), BF16),
            pltpu.VMEM((hw // HD, 8, row), F32),
            pltpu.VMEM((width, width), BF16),
            pltpu.VMEM((half, width), BF16),
            pltpu.VMEM((half, width), BF16),
            pltpu.VMEM((own, width), BF16),
            pltpu.VMEM((LANES, own, width // LANES), BF16),
            pltpu.VMEM((own, width // LANES), BF16),
            pltpu.VMEM((width, gwid), BF16),
            pltpu.VMEM((half, gwid), BF16),
            pltpu.VMEM((half, gwid), BF16),
            pltpu.VMEM((2, own, ff), BF16),
            pltpu.VMEM((LANES, 8, width), F32),
            pltpu.VMEM((chips + 2, 8, width), F32),
            pltpu.VMEM((tok, width), F32),
            dma((7,)),
            dma((LANES,)),
            dma((LANES,)),
            dma((LANES,)),
            dma((LANES,)),
            *[dma((chips,))] * 8,
            *[dma((LANES,))] * 6,
            *[dma((len(mats), chips))] * 4,
            dma((3,)),
            dma((LANES,)),
            dma((LANES,)),
            dma((chips,)),
            dma((chips + 1,)),
        ],
        compiler_params=pltpu.CompilerParams(
            collective_id=2, has_side_effects=True, vmem_limit_bytes=61 * 2**20
        ),
        cost_estimate=pl.CostEstimate(
            flops=20 * row * width * gwid, bytes_accessed=12 * width * ff, transcendentals=row * width
        ),
        name="back",
    )(
        grad_resid, mlp_vec, hidden_in, vecs, qkv, log_sum, cos_row, sin_row, seg_col, seg_row,
        grad_low, grad_att, attended, wq_full, wk_full, wv_full, normed_row, mlp_grads,
    )


def body(
    hidden_in,
    segment_ids,
    position_ids,
    out_grad,
    attn_norm,
    w_query,
    w_key,
    w_value,
    b_query,
    b_key,
    b_value,
    w_out,
    mlp_norm,
    w_gate,
    w_up,
    w_down,
):
    chips = lax.axis_size("dp") // 2
    dp, lane = lax.axis_index("dp"), lax.axis_index("seq")
    local_tok, width = hidden_in.shape
    kv_group = LANES // KV_HEADS
    query_width = HEADS // LANES * HD

    def side_by_side(vectors, step, size):
        return sum(
            lax.pad(v, jnp.zeros((), v.dtype), [(k * step, size - k * step - v.shape[0], 0)])
            for k, v in enumerate(vectors)
        )

    vec = side_by_side((attn_norm, mlp_norm, b_query, b_key, b_value), 2 * HD, 16 * HD).reshape(16, HD)
    ids = side_by_side((position_ids, segment_ids), local_tok, 8 * local_tok).reshape(8, local_tok)
    inv_freq = ROPE_BASE ** (-(np.arange(HD // 2, dtype=np.float32) * np.float32(2.0 / HD)))
    freqs = np.tile(np.concatenate([inv_freq, inv_freq]).astype(np.float32)[None, :], (8, 1))
    (
        resid, mlp_local, vecs, qkv, attended, log_sum, cos_row, sin_row, seg_col, seg_row,
        normed_row, grad_rows, _, _, wo_full, gate_full, up_full, down_full,
    ) = front(
        chips, hidden_in, ids, freqs, out_grad, vec, w_query, w_key, w_value, w_out.T, w_gate, w_up, w_down
    )
    total, grad_resid, mlp_vec, grad_low, grad_att, down_part, _, ff_grads, _, wq_full, wk_full, wv_full = feed_forward(
        chips, mlp_local, grad_rows, gate_full, up_full, down_full, w_query, w_key, w_value, resid, out_grad,
        wo_full, vecs,
    )
    block_out = total.astype(jnp.bfloat16)
    input_grad, vec_grads, out_grad_rows, qkv_grads, _, _, down_grads = back(
        chips, (0,), grad_resid, mlp_vec, hidden_in, vecs, qkv, log_sum, cos_row, sin_row, seg_col,
        seg_row, grad_low, grad_att, attended, wq_full, wk_full, wv_full, normed_row, down_part,
    )
    gate_grad, up_grad, down_grad = (
        jnp.sum(part.astype(jnp.float32), axis=0) for part in (ff_grads[0], ff_grads[1], down_grads[0])
    )
    own = width // (2 * chips)
    kv_own = KV_HEADS * HD // (2 * chips)
    query_grad = jnp.concatenate(
        [qkv_grads[k, :, :query_width] for k in range(LANES)], axis=1
    ).astype(jnp.float32)

    def kv_grad(offset):
        parts = qkv_grads[:, :, offset : offset + HD].astype(jnp.float32)
        return jnp.concatenate(
            [
                jnp.sum(parts[k * kv_group : (k + 1) * kv_group], axis=0)
                for k in range(KV_HEADS)
            ],
            axis=1,
        )

    def own_vec(k, size):
        return lax.dynamic_slice(vec_grads, (k, dp * size), (1, size))[0]

    return (
        block_out,
        input_grad,
        own_vec(0, own),
        query_grad,
        kv_grad(query_width),
        kv_grad(query_width + HD),
        own_vec(2, own),
        own_vec(3, kv_own),
        own_vec(4, kv_own),
        out_grad_rows.astype(jnp.float32).T,
        own_vec(1, own),
        gate_grad,
        up_grad,
        down_grad,
    )


def solution(mesh):
    return jax.shard_map(
        body,
        mesh=mesh,
        in_specs=(
            P(("dp", "seq"), None),
            P(("dp", "seq")),
            P(("dp", "seq")),
            P(("dp", "seq"), None),
            P("dp"),
            P("dp", None),
            P("dp", None),
            P("dp", None),
            P("dp"),
            P("dp"),
            P("dp"),
            P(None, "dp"),
            P("dp"),
            P("dp", "seq"),
            P("dp", "seq"),
            P("dp", "seq"),
        ),
        out_specs=(
            P(("dp", "seq"), None),
            P(("dp", "seq"), None),
            P("dp"),
            P("dp", None),
            P("dp", None),
            P("dp", None),
            P("dp"),
            P("dp"),
            P("dp"),
            P(None, "dp"),
            P("dp"),
            P("dp", "seq"),
            P("dp", "seq"),
            P("dp", "seq"),
        ),
        check_vma=False,
    )
```

time: 1170 us -> 442 us (0.38)
  waiting for transfers between devices: 675 us -> 0 us
  Pallas kernels: 157 us -> 420 us
  blocking collectives: 114 us -> 0 us
  matrix products: 66.9 us -> 0 us
  local copies, waits for them, and re-layouts: 64.6 us -> 6.49 us
  other arithmetic: 45.1 us -> 14.6 us
  starting transfers between devices: 25.9 us -> 0 us
  between operations: 17.7 us -> 0.72 us
    reduce_scatter x7 -> x0, waiting for transfers between devices: 362 us -> none  [the longest x3 153 us: body(): lax.psum_scatter(mlp_grads[k], 'dp', scatter_dimension=0, tiled=True)]
    pallas_call x1 -> x3, Pallas kernels: 157 us -> 420 us  [the longest x1 176 us: feed_forward(): pl.pallas_call(functools.partial(ff_kernel, chips), out_shape=(shape((tok...]
    all_gather x6 -> x0, waiting for transfers between devices: 115 us -> none  [the longest x1 50.6 us: body(): lax.all_gather(w_down, 'dp', axis=0, tiled=True)]
    psum x1 -> x0, waiting for transfers between devices: 110 us -> none  [body(): lax.psum((local_terms[0], local_terms[1], local_terms[2], local_terms[3],...]
    all_to_all x4 -> x0, waiting for transfers between devices: 83.4 us -> none  [the longest x1 51.3 us: body(): lax.all_to_all(outgoing, 'seq', split_axis=1, concat_axis=0, tiled=True)]
    dot_general x26 -> x0, matrix products: 66.9 us -> none  [the longest x4 13.5 us: contract_rows(): lax.dot_general(left, right, (((0,), (0,)), ((), ())), preferred_element_...]
    unnamed x2 -> x0, blocking collectives: 47.6 us -> none
    all_to_all x1 -> x0, blocking collectives: 31.9 us -> none  [body(): lax.all_to_all(returning.reshape(row_len, 1, query_width + 2 * HD), 'seq'...]
  transfers between devices with their start and end apart: 18 -> 0, of which waited for: 14 -> 0; matrix products, arithmetic and copies ran while one was open for 9% -> 0% of each run, Pallas kernels for 0% -> 0%
where the time goes in v2:
time: 442 us
  Pallas kernels  420 us (95%)
  other arithmetic  14.6 us (3%)
  local copies, waits for them, and re-layouts  6.49 us (1%)
    pallas_call x1, Pallas kernels, feed_forward(): pl.pallas_call(functools.partial(ff_kernel, chips), out_shape=(shape((tok...  176 us
    pallas_call x1, Pallas kernels, front(): pl.pallas_call(functools.partial(front_kernel, chips), out_shape=vmem_out...  132 us
    pallas_call x1, Pallas kernels, back(): pl.pallas_call(functools.partial(back_kernel, chips, mats), out_shape=vme...  112 us

profile of v2, /device:TPU:0, one launch (start us, length us, event | category | flops | bytes accessed | tf_op | source)
XLA Modules:
  0.0 441.6 jit_solution(8038437349879585151)
XLA Ops:
  0.6 0.7 pad_add_fusion
  1.3 0.6 reshape.37.ids_hbm
  2.0 1.3 add_bitcast_fusion.vec_hbm
  3.3 132.1 %front.1 = (f32[256,1536]{1,0:T(8,128)}, bf16[256,1536]{1,0:T(8,128)(2,1)}, f32[16,1536]{1,0:T(8,128)}, bf16[1024,640]{1,0:T(8,128)(2,1)}, bf16[256,1536]{1,0:T(...) custom-call(bf16[256,1536]{1,0:T(8,128)(2,1)} %x_ref.1, ...), custom_call_target="tpu_custom_call" | custom-call | flops 10066329600 | bytes 41287680 | tf_op jit(solution)/shard_map/front/pallas_call | solution.py:493
  135.4 176.2 %feed_forward.1 = (f32[256,1536]{1,0:T(8,128)}, f32[256,1536]{1,0:T(8,128)}, f32[8,1536]{1,0:T(8,128)}, bf16[256,1536]{1,0:T(8,128)(2,1)}, bf16[1024,384]{1,0:T(...) custom-call(bf16[256,1536]{1,0:T(8,128)(2,1)} %get-tuple-element.45., ...), custom_call_target="tpu_custom_call" | custom-call | flops 63417876480 | bytes 41287680 | tf_op jit(solution)/shard_map/feed_forward/pallas_call | solution.py:1055
  311.6 111.5 %back.1 = (f32[256,1536]{1,0:T(8,128)}, f32[8,1536]{1,0:T(8,128)}, bf16[192,1536]{1,0:T(8,128)(2,1)}, bf16[4,192,640]{2,1,0:T(8,128)(2,1)}, bf16[1,4,192,2240]{3...) custom-call(f32[256,1536]{1,0:T(8,128)} %get-tuple-element.54.gr_ref, ...), custom_call_target="tpu_custom_call" | custom-call | flops 20132659200 | bytes 41287680 | tf_op jit(solution)/shard_map/back/pallas_call | solution.py:1580
  423.1 0.0 copy-start.3
  423.2 1.2 slice_convert_fusion
  424.3 0.0 copy-start.4
  424.4 0.7 pad_maximum_fusion.1
  425.1 0.7 pad_maximum_fusion
  425.8 0.0 copy-done.3
  425.8 0.1 slice_bitcast_fusion.3
  425.8 0.0 copy-done.4
  425.8 0.0 copy-start
  425.9 1.7 convert_bitcast_fusion
  427.5 1.2 copy-done
  428.7 1.7 convert_reduce_fusion
  430.4 1.5 constant_dynamic-slice_fusion
  431.9 1.3 dynamic-slice_bitcast_fusion
  433.2 0.0 copy-start.1
  433.2 5.6 %convert_reduce_fusion.1 = (f32[192,2240]{1,0:T(8,128)}, f32[192,2240]{1,0:T(8,128)}) fusion(bf16[2,3,192,2240]{3,2,1,0:T(8,128)(2,1)} %get-tuple-element.74), kind=kLoop, calls=%fused_computation.1 | loop fusion | flops 4300800 | bytes 8601600 | tf_op jit(solution)/shard_map/reduce_sum | solution.py:1686
  438.8 0.0 copy-start.2
  438.8 0.0 copy-done.1
  438.8 1.0 convert_element_type.25
  439.8 0.7 copy-done.2
  440.5 1.1 copy.32
  (1 shorter events, 0.0 us)
Async XLA Ops:
  423.1 2.6 copy-start.3
  424.3 1.5 copy-start.4
  425.8 2.9 copy-start
  433.2 5.6 %copy-start.1 = (f32[256,1536]{1,0:T(8,128)S(1)}, f32[256,1536]{1,0:T(8,128)}, u32[]{:S(2)}) copy-start(f32[256,1536]{1,0:T(8,128)} %get-tuple-element.53) | copy-start | bytes 4718596
  438.8 1.7 copy-start.2

commit v3 on v2

--- a/solution.py
+++ b/solution.py
@@ -532,7 +532,7 @@
 def ff_kernel(
     chips,
     x_hbm, og_hbm, wg_hbm, wu_hbm, wd_hbm, wq_hbm, wk_hbm, wv_hbm, resid_hbm, own_og_hbm, wo_hbm, vecs_ref,
-    mo_ref, gm_ref, vec_ref, grl_hbm, ga_hbm, gw_hbm, fpair, fland, fmid, wqf, wkf, wvf,
+    mo_ref, gm_ref, vec_ref, grl_hbm, ga_hbm, gw_hbm, fpair, fland_gate, fland_up, fmid, wqf, wkf, wvf,
     xb, og, wg, wu, wd, hid, gg, gu, pb, rb, rf,
     load_sem, ag_send, ag_recv, rb_send, rb_recv, rf_send, rf_recv, out_sem,
     dp_send, dp_fwd, dp_recv, half_send, half_recv, own_sem, fp_send, fp_recv, fk_sem, fs_send, fs_recv, fl_sem,
@@ -546,6 +546,7 @@
     full_tiles = units // tile
     tail = units - full_tiles * tile
     wtile = 384
+    pieces = width // tile
     has_left, has_right = lane > 0, lane < LANES - 1
     is_end = jnp.logical_or(lane == 0, lane == LANES - 1)
     is_mid = jnp.logical_not(is_end)
@@ -617,35 +618,43 @@
             def _():
                 gather_copy(block, 1).start()
 
-    def sum_send(part, landing, send, recv, block):
+    def cols_of(piece):
+        return pl.ds(pl.multiple_of(piece * tile, tile), tile)
+
+    def sum_send(part, landing, send, recv, block, piece):
         goes_left = block < lane
         target = jnp.where(goes_left, left, right)
         slot = jnp.where(jnp.logical_and(goes_left, target == block), LANES, block)
         return pltpu.make_async_remote_copy(
-            part.at[rows_of(block, tok), pl.ds(0, width)], landing.at[rows_of(slot, tok)],
-            send.at[block], recv.at[slot],
+            part.at[rows_of(block, tok), cols_of(piece)], landing.at[rows_of(slot, tok), cols_of(piece)],
+            send.at[block, piece], recv.at[slot, piece],
             device_id={"seq": target}, device_id_type=MESH_ID,
         )
 
-    def sum_arrived(part, landing, send, recv, slot):
+    def sum_arrived(part, landing, send, recv, slot, piece):
+        there = landing.at[rows_of(slot, tok), cols_of(piece)]
         pltpu.make_async_remote_copy(
-            landing.at[rows_of(slot, tok)], landing.at[rows_of(slot, tok)],
-            send.at[0], recv.at[slot], device_id={"seq": left}, device_id_type=MESH_ID,
+            there, there, send.at[0, piece], recv.at[slot, piece], device_id={"seq": left}, device_id_type=MESH_ID
         ).wait_recv()
 
     def sum_pass(part, landing, send, recv, block):
         @pl.when(is_mid)
         def _():
-            sum_arrived(part, landing, send, recv, block)
-
-            def add(i, carry):
-                mine = pl.ds(pl.multiple_of(block * tok + i * 32, 32), 32)
-                total = part[mine, :width].astype(F32) + landing[mine, :].astype(F32)
-                part[mine, :width] = total.astype(BF16)
-                return carry
-
-            lax.fori_loop(0, tok // 32, add, 0)
-            sum_send(part, landing, send, recv, block).start()
+            def one(piece, c):
+                sum_arrived(part, landing, send, recv, block, piece)
+
+                def add(i, carry):
+                    mine = pl.ds(pl.multiple_of(block * tok + i * 64, 64), 64)
+                    cols = cols_of(piece)
+                    total = part[mine, cols].astype(F32) + landing[mine, cols].astype(F32)
+                    part[mine, cols] = total.astype(BF16)
+                    return carry
+
+                lax.fori_loop(0, tok // 64, add, 0)
+                sum_send(part, landing, send, recv, block, piece).start()
+                return c
+
+            lax.fori_loop(0, pieces, one, 0)
 
     def sum_last(part, landing, send, recv, out, onto=False):
         def begin(i, carry):
@@ -658,15 +667,20 @@
         lax.fori_loop(0, tok // 32, begin, 0)
 
         def take(slot):
-            sum_arrived(part, landing, send, recv, slot)
-
-            def add(i, carry):
-                here = pl.ds(pl.multiple_of(i * 32, 32), 32)
-                there = pl.ds(pl.multiple_of(slot * tok + i * 32, 32), 32)
-                out[here, :] = out[here, :] + landing[there, :].astype(F32)
-                return carry
-
-            lax.fori_loop(0, tok // 32, add, 0)
+            def one(piece, c):
+                sum_arrived(part, landing, send, recv, slot, piece)
+
+                def add(i, carry):
+                    here = pl.ds(pl.multiple_of(i * 64, 64), 64)
+                    there = pl.ds(pl.multiple_of(slot * tok + i * 64, 64), 64)
+                    cols = cols_of(piece)
+                    out[here, cols] = out[here, cols] + landing[there, cols].astype(F32)
+                    return carry
+
+                lax.fori_loop(0, tok // 64, add, 0)
+                return c
+
+            lax.fori_loop(0, pieces, one, 0)
 
         @pl.when(has_left)
         def _():
@@ -687,6 +701,16 @@
         for copy in loads + attn_own:
             copy.wait()
 
+    def down_part(block):
+        mine = rows_of(block, tok)
+
+        def down_tile(t, c):
+            cols = cols_of(t)
+            og[mine, cols] = nt(hid[mine, :], wd[cols, :]).astype(BF16)
+            return c
+
+        lax.fori_loop(0, pieces, down_tile, 0)
+
     def block_step(step, carry):
         block = order_of(step, lane)
         mine = rows_of(block, tok)
@@ -710,7 +734,7 @@
             if tail:
                 act(pl.ds(full_tiles * tile, tail))
 
-        @pl.when(step < LANES - 1)
+        @pl.when(step < LANES - 2)
         def _():
             with jax.named_scope("row_arrival"):
                 arrivals(step + 1)
@@ -730,42 +754,36 @@
         def back_tile(t, c):
             cols = pl.ds(pl.multiple_of(t * tile, tile), tile)
             pb[mine, cols] = (nt(gg[mine, :], wg[cols, :]) + nt(gu[mine, :], wu[cols, :])).astype(BF16)
+
+            @pl.when(jnp.logical_and(is_end, step > 0))
+            def _():
+                sum_send(*back, block, t).start()
+
             return c
 
         with jax.named_scope("input_grad_part"):
             lax.fori_loop(0, width // tile, back_tile, 0)
 
-        @pl.when(jnp.logical_and(is_end, step > 0))
+        @pl.when(step < LANES - 1)
         def _():
-            sum_send(*back, block).start()
+            down_part(block)
+
+        @pl.when(step == LANES - 2)
+        def _():
+            with jax.named_scope("row_arrival"):
+                arrivals(LANES - 1)
+
 
         return carry
 
     lax.fori_loop(0, LANES, block_step, 0)
-
-    def down_step(step, carry):
-        block = order_of(LANES - 1 - step, lane)
-        mine = rows_of(block, tok)
-
-        def down_tile(t, c):
-            cols = pl.ds(pl.multiple_of(t * tile, tile), tile)
-            og[mine, cols] = nt(hid[mine, :], wd[cols, :]).astype(BF16)
-            return c
-
-        with jax.named_scope("down_part"):
-            lax.fori_loop(0, width // tile, down_tile, 0)
-
-        @pl.when(jnp.logical_and(is_end, step < LANES - 1))
-        def _():
-            sum_send(*ahead, block).start()
-
-        return carry
 
     wtiles = width // wtile
     part_rows = width // (2 * chips)
     tile_chips = wtile // (2 * part_rows)
 
     square = chips == 4
+    fland = (fland_gate, fland_up)
     half = part_rows // 2
 
     def tile_at(step):
@@ -793,12 +811,12 @@
 
     def chip_keep(which):
         return pltpu.make_async_copy(
-            wg.at[held(which, chip)], fland.at[which, 0], fl_sem.at[which]
+            wg.at[held(which, chip)], fland[which].at[0], fl_sem.at[which]
         )
 
     def chip_send(which, mask):
         return to_chip(
-            wg.at[held(which, flipped(chip, mask))], fland.at[which, mask], fs_send.at[which, mask],
+            wg.at[held(which, flipped(chip, mask))], fland[which].at[mask], fs_send.at[which, mask],
             fs_recv.at[which, mask], mask,
         )
 
@@ -809,14 +827,14 @@
         if mask == 3:
             landing = fmid.at[which, upper]
         else:
-            landing = fland.at[which, 1, pl.ds(upper * half, half)]
+            landing = fland[which].at[1, pl.ds(upper * half, half)]
         k = 2 * (mask == 3) + upper
         return to_chip(part_of(which, mask, upper), landing, p1_send.at[which, k], p1_recv.at[which, k], 1 + upper)
 
     def second_hop(which, upper):
         mask = 2 - upper
         return to_chip(
-            part_of(which, mask, upper), fland.at[which, 2, pl.ds(upper * half, half)],
+            part_of(which, mask, upper), fland[which].at[2, pl.ds(upper * half, half)],
             p2_send.at[which, upper], p2_recv.at[which, upper], mask,
         )
 
@@ -848,18 +866,24 @@
             add_in(which, (which * chips + c) * part_rows + upper * half, half)
             second_hop(which, upper).start()
 
+    def pair_load(which, c):
+        return pltpu.make_async_copy(fpair.at[which, c], load_slot(which), load_sem.at[which])
+
+    def load_pairs(step, r=0):
+        for which in range(2):
+            c = tile_at(step) * tile_chips + r
+            pair_send(which, c, r).wait_recv()
+            pair_load(which, c).start()
+
     def add_pairs(step):
         k = tile_at(step)
         for r in range(tile_chips):
             c = k * tile_chips + r
-            arrived = []
+            if r:
+                load_pairs(step, r)
             for which in range(2):
                 pair_keep(which, c, r).wait()
-                pair_send(which, c, r).wait_recv()
-                arrived.append(pltpu.make_async_copy(fpair.at[which, c], load_slot(which), load_sem.at[which]))
-                arrived[which].start()
-            for which in range(2):
-                arrived[which].wait()
+                pair_load(which, c).wait()
                 add_in(which, (which * chips + c) * part_rows, part_rows)
                 if not square:
                     continue
@@ -918,21 +942,30 @@
         return carry
 
     mid_near, mid_far, mid_back = 3 - lane, 6 - 3 * lane, 3 * lane - 3
+    down_part(order_of(LANES - 1, lane))
+
+    @pl.when(is_end)
+    def _():
+        for step in range(LANES - 1, 0, -1):
+            for piece in range(pieces):
+                sum_send(*ahead, order_of(step, lane), piece).start()
+
     sum_pass(*back, mid_near)
-    grad_tile(0)
-    lax.fori_loop(0, 1, down_step, 0)
-    add_pairs(0)
-    lax.fori_loop(1, LANES, down_step, 0)
     wo = wd.at[:, pl.ds(0, width)]
     wo_load = pltpu.make_async_copy(wo_hbm, wo, late_sem.at[1])
     wo_load.start()
+    grad_tile(0)
+    load_pairs(0)
+    add_pairs(0)
+    grad_tile(1)
+    load_pairs(1)
     sum_pass(*back, mid_far)
-    grad_tile(1)
     add_pairs(1)
+    grad_tile(2)
+    load_pairs(2)
+    sum_pass(*back, mid_back)
     sum_pass(*ahead, mid_far)
-    grad_tile(2)
     add_pairs(2)
-    sum_pass(*back, mid_back)
     grad_tile(3)
     for block in range(LANES):
         @pl.when(jnp.logical_and(has_right, block <= lane))
@@ -945,22 +978,13 @@
 
     again = pltpu.make_async_copy(og_hbm, xb, load_sem.at[3])
     again.start()
-    add_pairs(3)
-    sum_pass(*ahead, mid_near)
-    sum_pass(*ahead, mid_back)
-    if square:
-        pass_halves(0)
-        pass_halves(1)
-    else:
-        for which in range(2):
-            chip_keep(which).start()
-            for mask in range(1, chips):
-                chip_send(which, mask).start()
+    load_pairs(3)
     sum_last(*back, gm_ref)
     for block in range(LANES):
         @pl.when(block != lane)
         def _(block=block):
-            sum_send(*back, block).wait_send()
+            for piece in range(pieces):
+                sum_send(*back, block, piece).wait_send()
 
     own_og, grl, gao = (pb.at[pl.ds(k * tok, tok)] for k in range(3))
     og_load = pltpu.make_async_copy(own_og_hbm, own_og, late_sem.at[2])
@@ -1003,6 +1027,17 @@
             a_copy(target).start()
     ga_own = pltpu.make_async_copy(gao.at[:, head_cols(lane)], ga_hbm.at[rows_of(lane, tok)], late_sem.at[1])
     ga_own.start()
+    add_pairs(3)
+    sum_pass(*ahead, mid_near)
+    sum_pass(*ahead, mid_back)
+    if square:
+        pass_halves(0)
+        pass_halves(1)
+    else:
+        for which in range(2):
+            chip_keep(which).start()
+            for mask in range(1, chips):
+                chip_send(which, mask).start()
     again.wait()
     lax.fori_loop(0, wtiles, down_grad_tile, 0)
     sum_last(*ahead, mo_ref, True)
@@ -1038,7 +1073,8 @@
     for block in range(LANES):
         @pl.when(block != lane)
         def _(block=block):
-            sum_send(*ahead, block).wait_send()
+            for piece in range(pieces):
+                sum_send(*ahead, block, piece).wait_send()
 
 
 def feed_forward(
@@ -1062,14 +1098,15 @@
             shape((row, width // LANES), BF16),
             shape((1, width, units), BF16),
             shape((2, chips, own, units), BF16),
-            shape((2, 3 if chips == 4 else chips, own, units), BF16),
+            shape((3 if chips == 4 else chips, own, units), BF16),
+            shape((3 if chips == 4 else chips, own, units), BF16),
             shape((2, 2, own // 2, units), BF16),
             shape((width, w_query.shape[1]), BF16),
             shape((width, w_key.shape[1]), BF16),
             shape((width, w_value.shape[1]), BF16),
         ),
         in_specs=[anywhere] * 11 + [vmem],
-        out_specs=(vmem, vmem, vmem) + (anywhere,) * 9,
+        out_specs=(vmem, vmem, vmem) + (anywhere,) * 10,
         scratch_shapes=[
             pltpu.VMEM((row, width), BF16),
             pltpu.VMEM((row, width), BF16),
@@ -1085,10 +1122,10 @@
             dma((5,)),
             dma((2, LANES)),
             dma((LANES,)),
-            dma((LANES,)),
-            dma((LANES + 1,)),
-            dma((LANES,)),
-            dma((LANES + 1,)),
+            dma((LANES, width // 512)),
+            dma((LANES + 1, width // 512)),
+            dma((LANES, width // 512)),
+            dma((LANES + 1, width // 512)),
             dma((2,)),
             dma((3, chips)),
             dma((3, chips)),
@@ -1130,10 +1167,10 @@
     chips, mats,
     gr_ref, mlp_vec_ref, x_ref, vecs_ref, qkv_ref, lse_ref, cos_ref, sin_ref, segc_ref, segr_ref,
     grl_hbm, ga_hbm, att_hbm, wq_hbm, wk_hbm, wv_hbm, nrm_hbm, gw_hbm,
-    ig_ref, vec_ref, woz_ref, wqz_ref, fpair, fsum, fland,
+    ig_ref, vec_ref, woz_ref, wqz_ref, fland,
     att, wfull, nrm, grl, ga, gk, gv, g, gl, lt,
     wop, wopair, woland, wores, zin, zsum,
-    wqp, wqpair, wqland, slots, vz, vd, gn,
+    wqp, wqpair, wqland, theirs, mine, pairs, vz, vd, gn,
     load_sem, g_send, g_recv, h_send, h_recv,
     po_send, po_recv, so_send, so_recv, pq_send, pq_recv, sq_send, sq_recv,
     zr_send, zr_recv, zg_send, zg_recv, zq_send, zq_recv,
@@ -1182,52 +1219,46 @@
             src, dst, send, recv, device_id={"seq": target}, device_id_type=MESH_ID
         )
 
+    def ff_load(k, c, other):
+        kept, sem = (theirs, slot_sem.at[0, k, c]) if other else (mine, slot_sem.at[1, k, c])
+        rows = rows_of(2 * c + (1 - core if other else core), part_rows)
+        return pltpu.make_async_copy(gw_hbm.at[mats[k], rows], kept.at[k, c], sem)
+
     def ff_pair(k, c):
-        return to_dp(
-            gw_hbm.at[mats[k], rows_of(2 * c + 1 - core, part_rows)], fpair.at[k, c],
-            fp_send.at[k, c], fp_recv.at[k, c], sibling,
-        )
+        return to_dp(theirs.at[k, c], pairs.at[k, c], fp_send.at[k, c], fp_recv.at[k, c], sibling)
 
     def ff_send(k, mask):
         c = flipped(chip, mask)
         return to_dp(
-            fsum.at[k, c], fland.at[k, chip], fs_send.at[k, c], fs_recv.at[k, chip], 2 * c + core
-        )
-
-    for k in range(len(mats)):
-        for mask in range(chips):
-            ff_pair(k, flipped(chip, mask)).start()
-
-    def ff_loads(k, mask):
+            mine.at[k, c], fland.at[k, chip], fs_send.at[k, c], fs_recv.at[k, chip], 2 * c + core
+        )
+
+    def ff_own(k):
+        return pltpu.make_async_copy(mine.at[k, chip], fland.at[k, chip], slot_sem.at[0, k, chip])
+
+    ff_turns = [(k, mask) for k in range(len(mats)) for mask in list(range(chips - 1, 0, -1)) + [0]]
+    for k, mask in ff_turns:
+        ff_load(k, flipped(chip, mask), True).start()
+        ff_load(k, flipped(chip, mask), False).start()
+    for k, mask in ff_turns:
         c = flipped(chip, mask)
-        return [
-            pltpu.make_async_copy(
-                gw_hbm.at[mats[k], rows_of(2 * c + core, part_rows)], slots.at[0], slot_sem.at[0]
-            ),
-            pltpu.make_async_copy(fpair.at[k, c], slots.at[1], slot_sem.at[1]),
-        ]
-
-    def ff_load(k, mask):
-        ff_pair(k, flipped(chip, mask)).wait_recv()
-        for copy in ff_loads(k, mask):
-            copy.start()
+        ff_load(k, c, True).wait()
+        ff_pair(k, c).start()
 
     def ff_add(k, mask):
-        for copy in ff_loads(k, mask):
-            copy.wait()
+        c = flipped(chip, mask)
+        ff_load(k, c, False).wait()
+        ff_pair(k, c).wait_recv()
 
         def add(start):
             some = pl.ds(start, 16)
-            slots[0, some, :] = (slots[0, some, :].astype(F32) + slots[1, some, :].astype(F32)).astype(BF16)
+            mine[k, c, some, :] = (mine[k, c, some, :].astype(F32) + pairs[k, c, some, :].astype(F32)).astype(BF16)
 
         chunked(part_rows, add, 16)
-        out = pltpu.make_async_copy(
-            slots.at[0], fsum.at[k, flipped(chip, mask)] if mask else fland.at[k, chip], slot_sem.at[2]
-        )
-        out.start()
-        out.wait()
         if mask:
             ff_send(k, mask).start()
+        else:
+            ff_own(k).start()
 
     loads[0].wait()
     loads[1].wait()
@@ -1320,7 +1351,6 @@
     gk[...] = jnp.zeros_like(gk)
     gv[...] = jnp.zeros_like(gv)
     out_sum.middle()
-    ff_turns = [(k, mask) for k in range(len(mats)) for mask in list(range(chips - 1, 0, -1)) + [0]]
     loads[2].wait()
 
     def out_store(some, value):
@@ -1431,7 +1461,6 @@
     own_out()
     qkv_sum.middle()
     for turn in ff_turns:
-        ff_load(*turn)
         ff_add(*turn)
     qkv_sum.last(qkv_store)
     for step in range(1, LANES):
@@ -1547,6 +1576,7 @@
     out_sum.end()
     qkv_sum.end()
     for k in range(len(mats)):
+        ff_own(k).wait()
         for mask in range(chips):
             c = flipped(chip, mask)
             ff_pair(k, c).wait_send()
@@ -1576,7 +1606,7 @@
         shape((own, width), BF16),
         shape((LANES, own, gwid), BF16),
     ]
-    hbm_outs = [shape((len(mats), chips, own, ff), BF16)] * 3
+    hbm_outs = [shape((len(mats), chips, own, ff), BF16)]
     return pl.pallas_call(
         functools.partial(back_kernel, chips, mats),
         out_shape=vmem_outs + hbm_outs,
@@ -1602,7 +1632,7 @@
             pltpu.VMEM((width, gwid), BF16),
             pltpu.VMEM((half, gwid), BF16),
             pltpu.VMEM((half, gwid), BF16),
-            pltpu.VMEM((2, own, ff), BF16),
+            *[pltpu.VMEM((len(mats), chips, own, ff), BF16)] * 3,
             pltpu.VMEM((LANES, 8, width), F32),
             pltpu.VMEM((chips + 2, 8, width), F32),
             pltpu.VMEM((tok, width), F32),
@@ -1614,7 +1644,7 @@
             *[dma((chips,))] * 8,
             *[dma((LANES,))] * 6,
             *[dma((len(mats), chips))] * 4,
-            dma((3,)),
+            dma((2, len(mats), chips)),
             dma((LANES,)),
             dma((LANES,)),
             dma((chips,)),
@@ -1673,18 +1703,25 @@
     ) = front(
         chips, hidden_in, ids, freqs, out_grad, vec, w_query, w_key, w_value, w_out.T, w_gate, w_up, w_down
     )
-    total, grad_resid, mlp_vec, grad_low, grad_att, down_part, _, ff_grads, _, wq_full, wk_full, wv_full = feed_forward(
+    (
+        total, grad_resid, mlp_vec, grad_low, grad_att, down_part, _, gate_grads, up_grads, _,
+        wq_full, wk_full, wv_full,
+    ) = feed_forward(
         chips, mlp_local, grad_rows, gate_full, up_full, down_full, w_query, w_key, w_value, resid, out_grad,
         wo_full, vecs,
     )
     block_out = total.astype(jnp.bfloat16)
-    input_grad, vec_grads, out_grad_rows, qkv_grads, _, _, down_grads = back(
+    input_grad, vec_grads, out_grad_rows, qkv_grads, down_grads = back(
         chips, (0,), grad_resid, mlp_vec, hidden_in, vecs, qkv, log_sum, cos_row, sin_row, seg_col,
         seg_row, grad_low, grad_att, attended, wq_full, wk_full, wv_full, normed_row, down_part,
     )
-    gate_grad, up_grad, down_grad = (
-        jnp.sum(part.astype(jnp.float32), axis=0) for part in (ff_grads[0], ff_grads[1], down_grads[0])
-    )
+    def chip_sum(parts):
+        return jnp.sum(parts.astype(jnp.float32), axis=0)
+
+    gate_grads, vec_grads = lax.optimization_barrier((gate_grads, vec_grads))
+    gate_grad = chip_sum(gate_grads)
+    gate_grad, up_grads = lax.optimization_barrier((gate_grad, up_grads))
+    up_grad, down_grad = chip_sum(up_grads), chip_sum(down_grads[0])
     own = width // (2 * chips)
     kv_own = KV_HEADS * HD // (2 * chips)
     query_grad = jnp.concatenate(

time: 442 us -> 433 us (0.980)
  Pallas kernels: 420 us -> 414 us
    pallas_call x1, Pallas kernels: 176 us -> 163 us  [feed_forward(): pl.pallas_call(functools.partial(ff_kernel, chips), out_shape=(shape((tok...]
    pallas_call x1, Pallas kernels: 112 us -> 119 us  [back(): pl.pallas_call(functools.partial(back_kernel, chips, mats), out_shape=vme...]
where the time goes in v3:
time: 433 us; the launch traced here: 432 us
  Pallas kernels  414 us (96%)
  other arithmetic  11.1 us (3%)
  local copies, waits for them, and re-layouts  6.61 us (2%)
    pallas_call x1, Pallas kernels, feed_forward(): pl.pallas_call(functools.partial(ff_kernel, chips), out_shape=(shape((tok...  163 us
    pallas_call x1, Pallas kernels, front(): pl.pallas_call(functools.partial(front_kernel, chips), out_shape=vmem_out...  132 us
    pallas_call x1, Pallas kernels, back(): pl.pallas_call(functools.partial(back_kernel, chips, mats), out_shape=vme...  119 us

profile of v3, /device:TPU:0, one launch (start us, length us, event | category | flops | bytes accessed | tf_op | source)
XLA Modules:
  0.0 432.1 jit_solution(5205108045742726708)
XLA Ops:
  0.6 0.7 pad_add_fusion
  1.3 0.6 reshape.35.ids_hbm
  2.0 1.3 add_bitcast_fusion.vec_hbm
  3.3 132.1 %front.1 = (f32[256,1536]{1,0:T(8,128)}, bf16[256,1536]{1,0:T(8,128)(2,1)}, f32[16,1536]{1,0:T(8,128)}, bf16[1024,640]{1,0:T(8,128)(2,1)}, bf16[256,1536]{1,0:T(...) custom-call(bf16[256,1536]{1,0:T(8,128)(2,1)} %x_ref.1, ...), custom_call_target="tpu_custom_call" | custom-call | flops 10066329600 | bytes 41287680 | tf_op jit(solution)/shard_map/front/pallas_call | solution.py:493
  135.4 163.0 %feed_forward.1 = (f32[256,1536]{1,0:T(8,128)}, f32[256,1536]{1,0:T(8,128)}, f32[8,1536]{1,0:T(8,128)}, bf16[256,1536]{1,0:T(8,128)(2,1)}, bf16[1024,384]{1,0:T(...) custom-call(bf16[256,1536]{1,0:T(8,128)(2,1)} %get-tuple-element.50., ...), custom_call_target="tpu_custom_call" | custom-call | flops 63417876480 | bytes 41287680 | tf_op jit(solution)/shard_map/feed_forward/pallas_call | solution.py:1091
  298.4 0.0 copy-start.2
  298.4 118.6 %back.1 = (f32[256,1536]{1,0:T(8,128)}, f32[8,1536]{1,0:T(8,128)}, bf16[192,1536]{1,0:T(8,128)(2,1)}, bf16[4,192,640]{2,1,0:T(8,128)(2,1)}, bf16[1,4,192,2240]{3,2,1,0:T(8,128)(2,1)}) custom-call(f32[256,1536]{1,0:T(8,128)} %get-tuple-element.59.gr_ref, f32[8,1536]{1,0:T(8,128)} %get-tuple-element.60.mlp_vec_ref, bf16[256,1536]{1,0:T(8,128)(2,1)} %x_ref.1, ...), custom_call_target="tpu_custom_call" | custom-call | flops 20132659200 | bytes 41287680 | tf_op jit(solution)/shard_map/back/pallas_call | solution.py:1610
  417.0 0.0 copy-done.2
  417.0 0.0 copy-start.1
  417.0 1.6 convert_reduce_fusion.2
  418.6 0.8 copy-done.1
  419.4 0.0 copy-start.5
  419.4 1.6 convert_reduce_fusion.1
  421.0 0.0 copy-done.5
  421.0 0.1 slice_convert_fusion
  421.0 0.0 copy-start.6
  421.1 0.7 pad_maximum_fusion.1
  421.8 0.7 pad_maximum_fusion
  422.5 0.1 slice_bitcast_fusion.3
  422.5 0.0 copy-done.6
  422.6 0.0 copy-start
  422.6 1.7 convert_bitcast_fusion
  424.3 1.1 copy-done
  425.4 0.0 copy-start.3
  425.4 1.7 convert_reduce_fusion
  427.1 0.0 copy-start.4
  427.1 1.4 dynamic-slice_bitcast_fusion
  428.5 1.5 constant_dynamic-slice_fusion
  430.0 0.0 copy-done.3
  430.0 1.0 convert_element_type.23
  430.9 0.0 copy-done.4
  430.9 1.1 copy.32
  (1 shorter events, 0.0 us)
Async XLA Ops:
  298.4 118.6 %copy-start.2 = (bf16[3,192,2240]{2,1,0:T(8,128)(2,1)S(1)}, bf16[3,192,2240]{2,1,0:T(8,128)(2,1)}, u32[]{:S(2)}) copy-start(bf16[3,192,2240]{2,1,0:T(8,128)(2,1)} %get-tuple-element.81) | copy-start | bytes 7741444
  417.0 2.4 copy-start.1
  419.4 1.6 copy-start.5
  421.0 1.5 copy-start.6
  422.6 2.9 copy-start
  425.4 4.6 %copy-start.3 = (f32[256,1536]{1,0:T(8,128)S(1)}, f32[256,1536]{1,0:T(8,128)}, u32[]{:S(2)}) copy-start(f32[256,1536]{1,0:T(8,128)} %get-tuple-element.58) | copy-start | bytes 4718596
  427.1 3.8 copy-start.4

commit v4 on v3

--- a/solution.py
+++ b/solution.py
@@ -267,14 +267,14 @@
                 for line in lines:
                     line_copy(*line, block, 1).wait_send()
 
+    first_loads[0].wait()
+    first_loads[1].wait()
+    line_begin(i_line, x_line)
     with jax.named_scope("first_sends"):
         gathers[0].begin()
         for copy in qkv_loads:
             copy.wait()
         gathers[1].begin()
-    first_loads[0].wait()
-    first_loads[1].wait()
-    line_begin(i_line, x_line)
     for load in own_loads:
         load.wait()
     for copy in own_copies:
@@ -646,8 +646,7 @@
                 def add(i, carry):
                     mine = pl.ds(pl.multiple_of(block * tok + i * 64, 64), 64)
                     cols = cols_of(piece)
-                    total = part[mine, cols].astype(F32) + landing[mine, cols].astype(F32)
-                    part[mine, cols] = total.astype(BF16)
+                    part[mine, cols] = part[mine, cols] + landing[mine, cols]
                     return carry
 
                 lax.fori_loop(0, tok // 64, add, 0)
@@ -845,7 +844,7 @@
         def add(i, carry):
             mine = pl.ds(pl.multiple_of(first + i * 16, 16), 16)
             other = pl.ds(pl.multiple_of(3 * wtile + which * part_rows + i * 16, 16), 16)
-            wg[mine, :] = (wg[mine, :].astype(F32) + wu[other, :].astype(F32)).astype(BF16)
+            wg[mine, :] = wg[mine, :] + wu[other, :]
             return carry
 
         lax.fori_loop(0, rows // 16, add, 0)
@@ -1252,7 +1251,7 @@
 
         def add(start):
             some = pl.ds(start, 16)
-            mine[k, c, some, :] = (mine[k, c, some, :].astype(F32) + pairs[k, c, some, :].astype(F32)).astype(BF16)
+            mine[k, c, some, :] = mine[k, c, some, :] + pairs[k, c, some, :]
 
         chunked(part_rows, add, 16)
         if mask:
@@ -1302,9 +1301,7 @@
                 def add(start, c=c):
                     mine = pl.ds(pl.multiple_of((2 * c + core) * part_rows + start, 16), 16)
                     other = pl.ds(pl.multiple_of(c * part_rows + start, 16), 16)
-                    self.partial[mine, :] = (
-                        self.partial[mine, :].astype(F32) + self.pair[other, :].astype(F32)
-                    ).astype(BF16)
+                    self.partial[mine, :] = self.partial[mine, :] + self.pair[other, :]
 
                 chunked(part_rows, add, 16)
                 if mask:
@@ -1458,8 +1455,8 @@
             wqz_ref.at[lane], wqz_ref.at[lane], zq_send.at[target], zq_recv.at[lane], target
         )
 
+    qkv_sum.middle()
     own_out()
-    qkv_sum.middle()
     for turn in ff_turns:
         ff_add(*turn)
     qkv_sum.last(qkv_store)

time: 433 us -> 432 us (level)
  no operation moved by 1% of the time
where the time goes in v4:
time: 432 us
  Pallas kernels  413 us (96%)
  other arithmetic  11.1 us (3%)
  local copies, waits for them, and re-layouts  6.61 us (2%)
    pallas_call x1, Pallas kernels, feed_forward(): pl.pallas_call(functools.partial(ff_kernel, chips), out_shape=(shape((tok...  163 us
    pallas_call x1, Pallas kernels, front(): pl.pallas_call(functools.partial(front_kernel, chips), out_shape=vmem_out...  132 us
    pallas_call x1, Pallas kernels, back(): pl.pallas_call(functools.partial(back_kernel, chips, mats), out_shape=vme...  119 us

profile of v4, /device:TPU:0, one launch (start us, length us, event | category | flops | bytes accessed | tf_op | source)
XLA Modules:
  0.0 431.8 jit_solution(14411391696821031777)
XLA Ops:
  0.6 0.7 pad_add_fusion
  1.3 0.6 reshape.35.ids_hbm
  2.0 1.3 add_bitcast_fusion.vec_hbm
  3.3 132.1 %front.1 = (f32[256,1536]{1,0:T(8,128)}, bf16[256,1536]{1,0:T(8,128)(2,1)}, f32[16,1536]{1,0:T(8,128)}, bf16[1024,640]{1,0:T(8,128)(2,1)}, bf16[256,1536]{1,0:T(...) custom-call(bf16[256,1536]{1,0:T(8,128)(2,1)} %x_ref.1, ...), custom_call_target="tpu_custom_call" | custom-call | flops 10066329600 | bytes 41287680 | tf_op jit(solution)/shard_map/front/pallas_call | solution.py:493
  135.4 162.7 %feed_forward.1 = (f32[256,1536]{1,0:T(8,128)}, f32[256,1536]{1,0:T(8,128)}, f32[8,1536]{1,0:T(8,128)}, bf16[256,1536]{1,0:T(8,128)(2,1)}, bf16[1024,384]{1,0:T(...) custom-call(bf16[256,1536]{1,0:T(8,128)(2,1)} %get-tuple-element.50., ...), custom_call_target="tpu_custom_call" | custom-call | flops 63417876480 | bytes 41287680 | tf_op jit(solution)/shard_map/feed_forward/pallas_call | solution.py:1090
  298.2 0.0 copy-start.2
  298.2 118.5 %back.1 = (f32[256,1536]{1,0:T(8,128)}, f32[8,1536]{1,0:T(8,128)}, bf16[192,1536]{1,0:T(8,128)(2,1)}, bf16[4,192,640]{2,1,0:T(8,128)(2,1)}, bf16[1,4,192,2240]{3,2,1,0:T(8,128)(2,1)}) custom-call(f32[256,1536]{1,0:T(8,128)} %get-tuple-element.59.gr_ref, f32[8,1536]{1,0:T(8,128)} %get-tuple-element.60.mlp_vec_ref, bf16[256,1536]{1,0:T(8,128)(2,1)} %x_ref.1, ...), custom_call_target="tpu_custom_call" | custom-call | flops 20132659200 | bytes 41287680 | tf_op jit(solution)/shard_map/back/pallas_call | solution.py:1607
  416.7 0.0 copy-done.2
  416.7 0.0 copy-start.1
  416.7 1.6 convert_reduce_fusion.2
  418.3 0.8 copy-done.1
  419.1 0.0 copy-start.5
  419.1 1.6 convert_reduce_fusion.1
  420.7 0.0 copy-done.5
  420.7 0.1 slice_convert_fusion
  420.8 0.0 copy-start.6
  420.8 0.7 pad_maximum_fusion.1
  421.5 0.7 pad_maximum_fusion
  422.2 0.1 slice_bitcast_fusion.3
  422.3 0.0 copy-done.6
  422.3 0.0 copy-start
  422.3 1.7 convert_bitcast_fusion
  424.0 1.1 copy-done
  425.1 0.0 copy-start.3
  425.1 1.7 convert_reduce_fusion
  426.9 0.0 copy-start.4
  426.9 1.4 dynamic-slice_bitcast_fusion
  428.2 1.5 constant_dynamic-slice_fusion
  429.7 0.0 copy-done.3
  429.7 1.0 convert_element_type.23
  430.7 0.0 copy-done.4
  430.7 1.1 copy.32
  (1 shorter events, 0.0 us)
Async XLA Ops:
  298.2 118.5 %copy-start.2 = (bf16[3,192,2240]{2,1,0:T(8,128)(2,1)S(1)}, bf16[3,192,2240]{2,1,0:T(8,128)(2,1)}, u32[]{:S(2)}) copy-start(bf16[3,192,2240]{2,1,0:T(8,128)(2,1)} %get-tuple-element.81) | copy-start | bytes 7741444
  416.7 2.4 copy-start.1
  419.1 1.6 copy-start.5
  420.8 1.5 copy-start.6
  422.3 2.9 copy-start
  425.1 4.6 %copy-start.3 = (f32[256,1536]{1,0:T(8,128)S(1)}, f32[256,1536]{1,0:T(8,128)}, u32[]{:S(2)}) copy-start(f32[256,1536]{1,0:T(8,128)} %get-tuple-element.58) | copy-start | bytes 4718596
  426.9 3.8 copy-start.4
